TPU v7x, 32 devices: a whole 2x2x4 slice. The times are simulated.
32 devices in a mesh: replica: 4 (over x, core), inner: 8 (over z, y).
Axes of the slice: x: 2, y: 2, z: 4, core: 2. Of those that a mesh axis runs over, the one named last changes fastest.
Arguments:
- square_weights: float32 [2, 1024, 1024], P(None, 'inner'), may hold values from -6 to 6
- square_copies: float32 [4, 2, 1024, 1024], P('replica', None, 'inner'), may hold values from -6 to 6
- square_moment: float32 [2, 1024, 1024], P(None, 'inner'), may hold values from -6 to 6
- broad_weights: float32 [2, 1024, 2048], P(None, 'inner'), may hold values from -6 to 6
- broad_copies: float32 [4, 2, 1024, 2048], P('replica', None, 'inner'), may hold values from -6 to 6
- broad_moment: float32 [2, 1024, 2048], P(None, 'inner'), may hold values from -6 to 6
- embed_weights: float32 [16384, 1024], P('inner'), may hold values from -6 to 6
- embed_copies: float32 [4, 16384, 1024], P('replica', 'inner'), may hold values from -90 to 90, as said below
- embed_moment: float32 [16384, 1024], P('inner'), may hold values from -6 to 6
- embed_error: float32 [4, 16384, 1024], P('replica', 'inner'), may hold values from -3 to 3
- warm_start: float32 [64, 1024], replicated, may hold values from -6 to 6
Outputs:
- square_updated: float32 [2, 1024, 1024], P(None, 'inner')
- square_velocity: float32 [2, 1024, 1024], P(None, 'inner')
- broad_updated: float32 [2, 1024, 2048], P(None, 'inner')
- broad_velocity: float32 [2, 1024, 2048], P(None, 'inner')
- embed_updated: float32 [16384, 1024], P('inner')
- embed_velocity: float32 [16384, 1024], P('inner')
- embed_carried: float32 [4, 16384, 1024], P('replica', 'inner')
Inputs may be any that keep to these rules, and one draw needn't show every extreme that they name: `embed_copies`: each replica's embedding after its inner steps.
All inputs are finite; a program needn't handle non-finite values.
Results may differ from a plain program's by a relative error of at most 0.0001.
Values sent between devices are 32-bit elements; how exact they have to be, the bound alone decides.
No kernel may reach another device: no remote copies, remote signals or barrier semaphores. Data moves between devices by JAX's collectives and lax.ppermute only.
A program may use at most 128 MiB of HBM per device.

v0:
```python
import jax
import jax.numpy as jnp
from jax import lax
from jax.sharding import PartitionSpec as P

outer_rate = 0.7
momentum_decay = 0.9


def nesterov(weights, gradient, moment):
    velocity = momentum_decay * moment + gradient
    return (weights - outer_rate * (gradient + momentum_decay * velocity), velocity)


def local(
    square_weights,
    square_copies,
    square_moment,
    broad_weights,
    broad_copies,
    broad_moment,
    embed_weights,
    embed_copies,
    embed_moment,
    embed_error,
    warm_start,
):
    replicas = lax.axis_size("replica")
    highest = lax.Precision.HIGHEST
    contract_last = (((1,), (1,)), ((), ()))
    square_term = square_weights - square_copies[0]
    broad_term = broad_weights - broad_copies[0]
    corrected = embed_weights - embed_copies[0] + embed_error[0]
    square_sum, broad_sum = lax.psum((square_term, broad_term), "replica")
    left_local = lax.dot_general(warm_start, corrected, contract_last, precision=highest)
    left_factor = lax.psum(left_local, "replica") / replicas
    gram_local = lax.dot_general(left_factor, left_factor, contract_last, precision=highest)
    gram_matrix = lax.psum(gram_local, "inner")
    lower_factor = jnp.linalg.cholesky(gram_matrix)
    basis_rows = lax.linalg.triangular_solve(lower_factor, left_factor, left_side=True, lower=True)
    right_term = jnp.dot(basis_rows, corrected, precision=highest)
    right_total = lax.psum(right_term, ("replica", "inner"))
    right_factor = right_total / replicas
    embed_step = lax.dot_general(
        basis_rows, right_factor, (((0,), (0,)), ((), ())), precision=highest
    )
    embed_updated, embed_velocity = nesterov(embed_weights, embed_step, embed_moment)
    square_updated, square_velocity = nesterov(square_weights, square_sum / replicas, square_moment)
    broad_updated, broad_velocity = nesterov(broad_weights, broad_sum / replicas, broad_moment)
    embed_carried = (corrected - embed_step)[None]
    return (
        square_updated,
        square_velocity,
        broad_updated,
        broad_velocity,
        embed_updated,
        embed_velocity,
        embed_carried,
    )


def solution(mesh):
    in_specs = (
        P(None, "inner", None),
        P("replica", None, "inner", None),
        P(None, "inner", None),
        P(None, "inner", None),
        P("replica", None, "inner", None),
        P(None, "inner", None),
        P("inner", None),
        P("replica", "inner", None),
        P("inner", None),
        P("replica", "inner", None),
        P(),
    )
    out_specs = (
        P(None, "inner", None),
        P(None, "inner", None),
        P(None, "inner", None),
        P(None, "inner", None),
        P("inner", None),
        P("inner", None),
        P("replica", "inner", None),
    )
    return jax.shard_map(local, mesh=mesh, in_specs=in_specs, out_specs=out_specs, check_vma=False)
```

profile of v0, /device:TPU:1, one launch (start us, length us, event | category | flops | bytes accessed | tf_op | source)
XLA Modules:
  0.0 323.0 jit_solution(3803335754698956015)
XLA Ops:
  7.2 0.0 copy-start
  7.2 0.0 all-reduce.6.cloned.1.call-start
  7.2 0.0 copy-start.3
  7.2 2.8 bitcast_subtract_fusion.2
  10.1 4.5 %bitcast_subtract_fusion.1 = f32[2,128,2048]{2,1,0:T(8,128)} fusion(f32[2,128,2048]{2,1,0:T(8,128)} %param.14, f32[1,2,128,2048]{3,2,1,0:T(8,128)} %param.15), kind=kLoop, calls=%fused_computation.6 | loop fusion | flops 524288 | bytes 6291456 | tf_op jit(solution)/shard_map/sub | solution.py:32
  14.5 0.0 copy-done.3
  14.5 7.4 %bitcast_add_fusion = f32[2048,1024]{1,0:T(8,128)S(1)} fusion(f32[1,2048,1024]{2,1,0:T(8,128)} %param.20, f32[2048,1024]{1,0:T(8,128)S(1)} %copy-done.3, f32[1,2048,1024]{2,1,0:T(8,128)} %param.18), kind=kLoop, calls=%fused_computation | loop fusion | flops 4194304 | bytes 33554432 | tf_op jit(solution)/shard_map/add | solution.py:33
  21.9 0.0 copy-start.2
  21.9 3.4 %copy-done.2 = f32[2048,1024]{1,0:T(8,128)} copy-done((f32[2048,1024]{1,0:T(8,128)}, f32[2048,1024]{1,0:T(8,128)S(1)}, u32[]{:S(2)}) %copy-start.2) | copy-done | bytes 8388632
  25.3 0.0 copy-done
  25.3 9.0 %convolution_bitcast_fusion = f32[64,2048]{1,0:T(8,128)} fusion(f32[2048,1024]{1,0:T(8,128)S(1)} %bitcast_add_fusion, f32[64,1024]{1,0:T(8,128)S(1)} %copy-done), kind=kOutput, calls=%fused_computation.5 | convolution fusion | flops 1610612736 | bytes 9175040 | tf_op jit(solution)/shard_map/dot_general | solution.py:35
  34.3 0.0 copy-start.4
  34.3 0.0 all-reduce.6.cloned.1.call-update
  34.4 0.0 all-reduce.4.cloned.1.call-start
  34.4 79.4 %all-reduce.6.cloned.1.call-done = (f32[2,128,1024]{2,1,0:T(8,128)}, f32[2,128,2048]{2,1,0:T(8,128)}, f32[64,2048]{1,0:T(8,128)}) async-done(((f32[2,128,1024]{2,1,0:T(8,128)}, f32[2,128,2048]{2,1,0:T(8,128)}, f32[64,2048]{1,0:T(8,128)}), (f32[2,128,1024]{2,1,0:T(8,128)}, f32[2,128,2048]{2,1,0:T(8,128)}, f32[64,2048]{1,0:T(8,128)})) %all-reduce.6.cloned.1.call-update) | async-done | bytes 3670032 | tf_op jit(solution)/shard_map/psum | solution.py:34
  113.8 1.8 fusion.2
  115.6 30.1 %psum.38 = f32[64,64]{0,1:T(8,128)S(1)} all-reduce(f32[64,64]{0,1:T(8,128)S(1)} %fusion.2), channel_id=1, replica_groups=mesh['replica'=4,'inner'=8] {'inner'}, use_global_device_ids=true, to_apply=%region_3.0 | all-reduce | flops 4096 | bytes 32768 | tf_op jit(solution)/shard_map/psum | solution.py:38
  145.8 0.1 copy.19
  145.9 5.8 %cholesky.16 = f32[64,64]{1,0:T(8,128)S(1)} custom-call(f32[64,64]{1,0:T(8,128)S(1)} %fusion.11), custom_call_target="Cholesky" | custom-call | tf_op jit(solution)/shard_map/jit(cholesky)/cholesky | solution.py:39
  151.7 0.6 compare_reduce_fusion
  152.4 0.7 fusion.9
  153.0 4.9 %custom-call.6 = f32[1,64,64]{1,2,0:T(8,128)S(1)} custom-call(f32[1,64,64]{2,1,0:T(8,128)S(1)} %fusion.9), custom_call_target="InvertDiagBlocksLowerTriangular" | custom-call | tf_op jit(solution)/shard_map/triangular_solve | solution.py:40
  157.9 1.7 fusion
  159.6 8.2 %fusion.17 = f32[64,1024]{1,0:T(8,128)} fusion(f32[64,2048]{1,0:T(8,128)S(1)} %fusion, f32[2048,1024]{1,0:T(8,128)} %copy-done.2), kind=kOutput, calls=%fused_computation.33 | convolution fusion | flops 1610612736 | bytes 9175040 | tf_op jit(solution)/shard_map/dot_general | solution.py:41
  167.8 0.0 all-reduce.4.cloned.1.call-update
  167.9 0.0 copy-start.5
  167.9 0.0 copy-start.6
  167.9 0.0 copy-start.7
  167.9 0.0 copy-done.4
  167.9 5.3 %multiply_subtract_fusion.1 = (f32[2,128,2048]{2,1,0:T(8,128)}, f32[2,128,2048]{2,1,0:T(8,128)}) fusion(f32[2,128,2048]{2,1,0:T(8,128)S(1)} %copy-done.4, f32[2,128,2048]{2,1,0:T(8,128)} %get-tuple-element.8, f32[2,128,2048]{2,1,0:T(8,128)} %param.16), kind=kLoop, calls=%fused_computation.7 | loop fusion | flops 3670016 | bytes 10485760 | tf_op jit(solution)/shard_map/sub | solution.py:12
  173.2 0.0 copy-done.5
  173.2 0.0 copy-done.6
  173.2 0.0 copy-done.7
  173.2 1.7 multiply_subtract_fusion.2
  174.9 120.9 %all-reduce.4.cloned.1.call-done = f32[64,1024]{1,0:T(8,128)} async-done(((f32[64,1024]{1,0:T(8,128)}), f32[64,1024]{1,0:T(8,128)}) %all-reduce.4.cloned.1.call-update) | async-done | bytes 262160 | tf_op jit(solution)/shard_map/psum | solution.py:42
  295.8 0.0 copy-start.1
  295.8 20.4 %multiply_subtract_fusion = (f32[2048,1024]{1,0:T(8,128)}, f32[2048,1024]{1,0:T(8,128)}, f32[1,2048,1024]{2,1,0:T(8,128)}) fusion(f32[2048,1024]{1,0:T(8,128)} %param.17, f32[2048,1024]{1,0:T(8,128)} %param.19, f32[2048,1024]{1,0:T(8,128)} %copy-done.2, f32[64,2048]{1,0:T(8,128)S(1)} %fusion, f32[64,1024]{1,0:T(8,128)} %all-reduce.4.cloned.1.call-done), kind=kOutput, calls=%fused_computation.3 | convolution fusion | flops 1625358336 | bytes 51118080 | tf_op jit(solution)/shard_map/dot_general | solution.py:44
  316.2 0.0 copy-done.1
  (2 shorter events, 0.0 us)
Async XLA Ops:
  7.2 18.1 %copy-start = (f32[64,1024]{1,0:T(8,128)S(1)}, f32[64,1024]{1,0:T(8,128)}, u32[]{:S(2)}) copy-start(f32[64,1024]{1,0:T(8,128)} %param.21) | copy-start | bytes 786436
  7.2 106.6 %all-reduce.6.cloned.1.call-start = ((), (), s32[]{:S(2)}) async-start(), calls=%async_computation.1 | async-start | bytes 7340032 | tf_op jit(solution)/shard_map/psum | solution.py:34
  7.2 7.3 %copy-start.3 = (f32[2048,1024]{1,0:T(8,128)S(1)}, f32[2048,1024]{1,0:T(8,128)}, u32[]{:S(2)}) copy-start(f32[2048,1024]{1,0:T(8,128)} %param.17) | copy-start | bytes 25165828
  21.9 3.4 %copy-start.2 = (f32[2048,1024]{1,0:T(8,128)}, f32[2048,1024]{1,0:T(8,128)S(1)}, u32[]{:S(2)}) copy-start(f32[2048,1024]{1,0:T(8,128)S(1)} %bitcast_add_fusion) | copy-start | bytes 25165828
  34.3 133.5 %copy-start.4 = (f32[2,128,2048]{2,1,0:T(8,128)S(1)}, f32[2,128,2048]{2,1,0:T(8,128)}, u32[]{:S(2)}) copy-start(f32[2,128,2048]{2,1,0:T(8,128)} %param.14) | copy-start | bytes 6291460
  34.4 261.4 %all-reduce.4.cloned.1.call-start = ((), (), s32[]{:S(2)}) async-start(), calls=%async_computation | async-start | bytes 524288 | tf_op jit(solution)/shard_map/psum | solution.py:42
  167.9 5.3 %copy-start.5 = (f32[2,128,1024]{2,1,0:T(8,128)S(1)}, f32[2,128,1024]{2,1,0:T(8,128)}, u32[]{:S(2)}) copy-start(f32[2,128,1024]{2,1,0:T(8,128)} %param.11) | copy-start | bytes 3145732
  167.9 5.3 %copy-start.6 = (f32[2,128,1024]{2,1,0:T(8,128)S(1)}, f32[2,128,1024]{2,1,0:T(8,128)}, u32[]{:S(2)}) copy-start(f32[2,128,1024]{2,1,0:T(8,128)} %param.13) | copy-start | bytes 3145732
  167.9 5.3 %copy-start.7 = (f32[2,128,1024]{2,1,0:T(8,128)S(1)}, f32[2,128,1024]{2,1,0:T(8,128)}, u32[]{:S(2)}) copy-start(f32[2,128,1024]{2,1,0:T(8,128)} %get-tuple-element.7) | copy-start | bytes 3145732
  295.8 20.4 %copy-start.1 = (f32[64,1024]{1,0:T(8,128)S(1)}, f32[64,1024]{1,0:T(8,128)}, u32[]{:S(2)}) copy-start(f32[64,1024]{1,0:T(8,128)} %param.21) | copy-start | bytes 786436
Sparse Core Ops, SparseCore 0:
  34.5 79.2 all-reduce.5
  168.0 127.7 all-reduce.3
where the time goes:
time: 325 us; the launch traced here: 323 us
  waiting for transfers between devices  200 us (62%)
  matrix products  41.1 us (13%)
  other arithmetic  33.7 us (10%)
  blocking collectives  30.1 us (9%)
  between operations  14.2 us (4%)
  local copies, waits for them, and re-layouts  3.51 us (1%)
    psum x1, waiting for transfers between devices, local(): right_total = lax.psum(right_term, ('replica', 'inner'))  121 us
    psum x1, waiting for transfers between devices, local(): square_sum, broad_sum = lax.psum((square_term, broad_term), 'replica')  79.4 us
    psum x1, blocking collectives, local(): gram_matrix = lax.psum(gram_local, 'inner')  30.1 us
    dot_general x1, matrix products, local(): lax.dot_general(basis_rows, right_factor, (((0,), (0,)), ((), ())), preci...  20.4 us
    dot_general x1, matrix products, local(): lax.dot_general(warm_start, corrected, contract_last, precision=highest)  9.04 us
    dot_general x1, matrix products, local(): right_term = jnp.dot(basis_rows, corrected, precision=highest)  8.2 us
    add x1, other arithmetic, local(): corrected = embed_weights - embed_copies[0] + embed_error[0]  7.35 us
    sub x2, other arithmetic, nesterov(): weights - outer_rate * (gradient + momentum_decay * velocity)  6.98 us
  transfers between devices with their start and end apart: 2, of which 2 were waited for; matrix products, arithmetic and copies ran while one was open for 2% of the time, Pallas kernels for 0%

commit v1 on v0

--- a/solution.py
+++ b/solution.py
@@ -10,6 +10,31 @@
 def nesterov(weights, gradient, moment):
     velocity = momentum_decay * moment + gradient
     return (weights - outer_rate * (gradient + momentum_decay * velocity), velocity)
+
+
+def swap(value, axis, bit):
+    return lax.ppermute(value, axis, [(i, i ^ bit) for i in range(lax.axis_size(axis))])
+
+
+def doubled(value, axis, first=1):
+    bit = first
+    while bit < lax.axis_size(axis):
+        value = value + swap(value, axis, bit)
+        bit *= 2
+    return value
+
+
+def halved(value):
+    core = lax.axis_index("replica") % 2
+    away = lax.dynamic_index_in_dim(value, 1 - core, 0, keepdims=True)
+    kept = lax.dynamic_index_in_dim(value, core, 0, keepdims=True)
+    return kept + swap(away, "replica", 1)
+
+
+def rejoined(half):
+    other = swap(half, "replica", 1)
+    first = lax.axis_index("replica") % 2 == 0
+    return jnp.concatenate([jnp.where(first, half, other), jnp.where(first, other, half)], axis=0)
 
 
 def local(
@@ -28,19 +53,24 @@
     replicas = lax.axis_size("replica")
     highest = lax.Precision.HIGHEST
     contract_last = (((1,), (1,)), ((), ()))
-    square_term = square_weights - square_copies[0]
-    broad_term = broad_weights - broad_copies[0]
+    rank, width = warm_start.shape
     corrected = embed_weights - embed_copies[0] + embed_error[0]
-    square_sum, broad_sum = lax.psum((square_term, broad_term), "replica")
     left_local = lax.dot_general(warm_start, corrected, contract_last, precision=highest)
-    left_factor = lax.psum(left_local, "replica") / replicas
+    left_half = doubled(halved(left_local.reshape(2, rank // 2, -1)), "replica", 2)
+    left_factor = rejoined(left_half).reshape(rank, -1) / replicas
+
+    square_sum = rejoined(doubled(halved(square_weights - square_copies[0]), "replica", 2))
+    broad_sum = rejoined(doubled(halved(broad_weights - broad_copies[0]), "replica", 2))
+
     gram_local = lax.dot_general(left_factor, left_factor, contract_last, precision=highest)
-    gram_matrix = lax.psum(gram_local, "inner")
+    right_local = jnp.dot(left_factor, corrected, precision=highest)
+    gram_matrix = doubled(gram_local, "inner")
+    right_half = halved(right_local.reshape(2, rank // 2, width))
+    right_half = doubled(doubled(right_half, "inner"), "replica", 2)
     lower_factor = jnp.linalg.cholesky(gram_matrix)
     basis_rows = lax.linalg.triangular_solve(lower_factor, left_factor, left_side=True, lower=True)
-    right_term = jnp.dot(basis_rows, corrected, precision=highest)
-    right_total = lax.psum(right_term, ("replica", "inner"))
-    right_factor = right_total / replicas
+    right_total = rejoined(right_half).reshape(rank, width) / replicas
+    right_factor = lax.linalg.triangular_solve(lower_factor, right_total, left_side=True, lower=True)
     embed_step = lax.dot_general(
         basis_rows, right_factor, (((0,), (0,)), ((), ())), precision=highest
     )

time: 325 us -> 133 us (0.41)
  waiting for transfers between devices: 200 us -> 24 us
  blocking collectives: 30.1 us -> 0 us
  starting transfers between devices: 0.08 us -> 21.2 us
  between operations: 14.2 us -> 0.94 us
  other arithmetic: 33.7 us -> 43.5 us
  matrix products: 41.1 us -> 35.6 us
  local copies, waits for them, and re-layouts: 3.51 us -> 7.58 us
    psum x2 -> x0, waiting for transfers between devices: 200 us -> none  [the longest x1 121 us: local(): right_total = lax.psum(right_term, ('replica', 'inner'))]
    psum x1 -> x0, blocking collectives: 30.1 us -> none  [local(): gram_matrix = lax.psum(gram_local, 'inner')]
    ppermute x0 -> x18, waiting for transfers between devices: none -> 24 us  [swap(): lax.ppermute(value, axis, [(i, i ^ bit) for i in range(lax.axis_size(axis...]
    ppermute x0 -> x18, starting transfers between devices: none -> 21.2 us  [swap(): lax.ppermute(value, axis, [(i, i ^ bit) for i in range(lax.axis_size(axis...]
    add x0 -> x14, other arithmetic: none -> 9.63 us  [the longest x4 5.78 us: halved(): return kept + swap(away, 'replica', 1)]
    sub x2, other arithmetic: 7.3 us -> 3.21 us  [the longest x1 1.85 us: local(): broad_weights - broad_copies[0]]
  transfers between devices with their start and end apart: 2 -> 18, of which waited for: 2 -> 6; matrix products, arithmetic and copies ran while one was open for 2% -> 43% of each run, Pallas kernels for 0% -> 0%
where the time goes in v1:
time: 133 us
  other arithmetic  43.5 us (33%)
  matrix products  35.6 us (27%)
  waiting for transfers between devices  24 us (18%)
  starting transfers between devices  21.2 us (16%)
  local copies, waits for them, and re-layouts  7.58 us (6%)
    ppermute x18, waiting for transfers between devices, swap(): lax.ppermute(value, axis, [(i, i ^ bit) for i in range(lax.axis_size(axis...  24 us
    ppermute x18, starting transfers between devices, swap(): lax.ppermute(value, axis, [(i, i ^ bit) for i in range(lax.axis_size(axis...  21.2 us
    dot_general x1, matrix products, local(): lax.dot_general(basis_rows, right_factor, (((0,), (0,)), ((), ())), preci...  18 us
    add x1, other arithmetic, local(): corrected = embed_weights - embed_copies[0] + embed_error[0]  9.77 us
    dot_general x1, matrix products, local(): lax.dot_general(warm_start, corrected, contract_last, precision=highest)  8.25 us
    dot_general x1, matrix products, local(): right_local = jnp.dot(left_factor, corrected, precision=highest)  7.73 us
    another operation x3, other arithmetic, local(): lower_factor = jnp.linalg.cholesky(gram_matrix)  6.51 us
    sub x2, other arithmetic, nesterov(): weights - outer_rate * (gradient + momentum_decay * velocity)  5.8 us
  transfers between devices with their start and end apart: 18, of which 6 were waited for; matrix products, arithmetic and copies ran while one was open for 43% of the time, Pallas kernels for 0%

profile of v1, /device:TPU:1, one launch (start us, length us, event | category | flops | bytes accessed | tf_op | source)
XLA Modules:
  0.0 132.8 jit_solution(16941047801465233329)
XLA Ops:
  0.6 0.0 copy-start
  0.7 9.8 %bitcast_add_fusion = f32[2048,1024]{1,0:T(8,128)S(1)} fusion(f32[1,2048,1024]{2,1,0:T(8,128)} %param.20, f32[2048,1024]{1,0:T(8,128)} %param.17, f32[1,2048,1024]{2,1,0:T(8,128)} %param.18), kind=kLoop, calls=%fused_computation.2 | loop fusion | flops 4194304 | bytes 33554432 | tf_op jit(solution)/shard_map/add | solution.py:57
  10.4 0.0 copy-start.2
  10.5 3.4 %copy-done.2 = f32[2048,1024]{1,0:T(8,128)} copy-done((f32[2048,1024]{1,0:T(8,128)}, f32[2048,1024]{1,0:T(8,128)S(1)}, u32[]{:S(2)}) %copy-start.2) | copy-done | bytes 8388632
  13.9 8.3 %fusion.8 = f32[2048,64]{0,1:T(8,128)S(1)} fusion(f32[2048,1024]{1,0:T(8,128)S(1)} %bitcast_add_fusion, f32[64,1024]{1,0:T(8,128)S(1)} %copy-done), kind=kOutput, calls=%fused_computation.45 | convolution fusion | flops 1610612736 | bytes 9175040 | tf_op jit(solution)/shard_map/dot_general | solution.py:58
  22.1 0.8 copy-done.9
  22.9 0.1 collective-permute-start.6
  23.1 1.6 %collective-permute-done.6 = f32[1,32,2048]{2,1,0:T(8,128)} collective-permute-done((f32[1,32,2048]{2,1,0:T(8,128)S(1)}, f32[1,32,2048]{2,1,0:T(8,128)}, u32[]{:S(2)}, u32[]{:S(2)}) %collective-permute-start.6) | collective-permute-done | bytes 262176 | tf_op jit(solution)/shard_map/ppermute | solution.py:16
  24.7 1.1 dynamic-slice_add_fusion.2
  25.7 2.4 %collective-permute-start.7 = (f32[1,32,2048]{2,1,0:T(8,128)S(1)}, f32[1,32,2048]{2,1,0:T(8,128)S(1)}, u32[]{:S(2)}, u32[]{:S(2)}) collective-permute-start(f32[1,32,2048]{2,1,0:T(8,128)S(1)} %dynamic-slice_add_fusion.2), channel_id=1, source_target_pairs={{0,16},{8,24},{16,0},{24,8},{1,17},{9,25},{17,1},{25,9},{2,18},{10... | collective-permute-start | bytes 786440 | tf_op jit(solution)/shard_map/ppermute | solution.py:16
  28.1 1.4 %bitcast_subtract_fusion.2 = f32[2,128,1024]{2,1,0:T(8,128)S(1)} fusion(f32[2,128,1024]{2,1,0:T(8,128)S(1)} %copy-done.5, f32[1,2,128,1024]{3,2,1,0:T(8,128)} %param.12), kind=kLoop, calls=%fused_computation.12 | loop fusion | flops 262144 | bytes 3145728 | tf_op jit(solution)/shard_map/sub | solution.py:62
  29.5 0.0 copy-start.7
  29.5 0.9 constant_dynamic-slice_fusion.3
  30.4 0.7 collective-permute-start
  31.1 3.4 %collective-permute-done.7 = f32[1,32,2048]{2,1,0:T(8,128)S(1)} collective-permute-done((f32[1,32,2048]{2,1,0:T(8,128)S(1)}, f32[1,32,2048]{2,1,0:T(8,128)S(1)}, u32[]{:S(2)}, u32[]{:S(2)}) %collective-permute-start.7) | collective-permute-done | bytes 262176 | tf_op jit(solution)/shard_map/ppermute | solution.py:16
  34.6 0.9 collective-permute-start.8
  35.5 1.8 %bitcast_subtract_fusion.1 = f32[2,128,2048]{2,1,0:T(8,128)S(1)} fusion(f32[2,128,2048]{2,1,0:T(8,128)S(1)} %copy-done.3, f32[1,2,128,2048]{3,2,1,0:T(8,128)} %param.15), kind=kLoop, calls=%fused_computation.8 | loop fusion | flops 524288 | bytes 6291456 | tf_op jit(solution)/shard_map/sub | solution.py:63
  37.4 0.0 copy-start.4
  37.4 1.3 copy-done.4
  38.7 1.0 constant_dynamic-slice_fusion.2
  39.7 0.0 collective-permute-start.3
  39.8 0.6 fusion.9
  40.4 1.6 %collective-permute-start.9 = (f32[64,64]{0,1:T(8,128)S(1)}, f32[64,64]{0,1:T(8,128)S(1)}, u32[]{:S(2)}, u32[]{:S(2)}) collective-permute-start(f32[64,64]{0,1:T(8,128)S(1)} %fusion.9), channel_id=1, source_target_pairs={{0,1},{1,0},{2,3},{3,2},{4,5},{5,4},{6,7},{7,6},{8,9},{9,8},{10,11... | collective-permute-start | bytes 49160 | tf_op jit(solution)/shard_map/ppermute | solution.py:16
  42.0 7.7 %fusion = f32[2,32,1024]{2,1,0:T(8,128)S(1)} fusion(f32[2048,1024]{1,0:T(8,128)} %copy-done.2, f32[1,32,2048]{2,1,0:T(8,128)S(1)} %get-tuple-element.19, f32[1,32,2048]{2,1,0:T(8,128)S(1)} %get-tuple-element.18), kind=kOutput, calls=%fused_computation | convolution fusion | flops 1610874880 | bytes 9175040 | tf_op jit(solution)/shard_map/dot_general | solution.py:66
  49.7 0.0 collective-permute-done.9
  49.7 1.4 %collective-permute-start.10 = (f32[64,64]{0,1:T(8,128)S(1)}, f32[64,64]{0,1:T(8,128)S(1)}, u32[]{:S(2)}, u32[]{:S(2)}) collective-permute-start(f32[64,64]{0,1:T(8,128)S(1)} %add.118), channel_id=1, source_target_pairs={{0,2},{1,3},{2,0},{3,1},{4,6},{5,7},{6,4},{7,5},{8,10},{9,11},{10,... | collective-permute-start | bytes 49160 | tf_op jit(solution)/shard_map/ppermute | solution.py:16
  51.1 1.1 collective-permute-start.12
  52.2 0.3 collective-permute-done.10
  52.6 2.3 %collective-permute-start.11 = (f32[64,64]{0,1:T(8,128)S(1)}, f32[64,64]{0,1:T(8,128)S(1)}, u32[]{:S(2)}, u32[]{:S(2)}) collective-permute-start(f32[64,64]{0,1:T(8,128)S(1)} %add.119), channel_id=1, source_target_pairs={{0,4},{1,5},{2,6},{3,7},{4,0},{5,1},{6,2},{7,3},{8,12},{9,13},{10,... | collective-permute-start | bytes 49160 | tf_op jit(solution)/shard_map/ppermute | solution.py:16
  54.9 2.1 %dynamic-slice_add_fusion.1 = f32[1,128,1024]{2,1,0:T(8,128)} fusion(f32[1,128,1024]{2,1,0:T(8,128)} %collective-permute-done, f32[2,128,1024]{2,1,0:T(8,128)} %copy-done.7, s32[]{:T(128)S(6)} %select_n.91), kind=kLoop, calls=%fused_computation.17 | loop fusion | flops 131072 | bytes 1572868 | tf_op jit(solution)/shard_map/add | solution.py:31
  56.9 1.2 collective-permute-start.1
  58.2 0.0 collective-permute-done.11
  58.2 0.1 copy.20
  58.2 0.0 collective-permute-done.12
  58.3 0.3 collective-permute-start.13
  58.6 5.8 %cholesky.16 = f32[64,64]{1,0:T(8,128)S(1)} custom-call(f32[64,64]{1,0:T(8,128)S(1)} %fusion.7), custom_call_target="Cholesky" | custom-call | tf_op jit(solution)/shard_map/jit(cholesky)/cholesky | solution.py:70
  64.4 0.0 collective-permute-done.13
  64.5 1.4 %collective-permute-start.14 = (f32[1,32,1024]{2,1,0:T(8,128)S(1)}, f32[1,32,1024]{2,1,0:T(8,128)S(1)}, u32[]{:S(2)}, u32[]{:S(2)}) collective-permute-start(f32[1,32,1024]{2,1,0:T(8,128)S(1)} %add.123), channel_id=1, source_target_pairs={{0,2},{1,3},{2,0},{3,1},{4,6},{5,7},{6,4},{7,5},{8,10},{9,11},{10,... | collective-permute-start | bytes 393224 | tf_op jit(solution)/shard_map/ppermute | solution.py:16
  65.9 0.6 compare_reduce_fusion
  66.5 2.3 %collective-permute-done.14 = f32[1,32,1024]{2,1,0:T(8,128)S(1)} collective-permute-done((f32[1,32,1024]{2,1,0:T(8,128)S(1)}, f32[1,32,1024]{2,1,0:T(8,128)S(1)}, u32[]{:S(2)}, u32[]{:S(2)}) %collective-permute-start.14) | collective-permute-done | bytes 131104 | tf_op jit(solution)/shard_map/ppermute | solution.py:16
  68.8 0.5 collective-permute-start.15
  69.3 0.0 collective-permute-done.3
  69.3 2.6 %dynamic-slice_add_fusion = f32[1,128,2048]{2,1,0:T(8,128)} fusion(f32[1,128,2048]{2,1,0:T(8,128)} %collective-permute-done.3, f32[2,128,2048]{2,1,0:T(8,128)} %copy-done.4, s32[]{:T(128)S(6)} %select_n.91), kind=kLoop, calls=%fused_computation.13 | loop fusion | flops 262144 | bytes 3145732 | tf_op jit(solution)/shard_map/add | solution.py:31
  71.9 1.2 collective-permute-start.4
  73.2 1.8 %collective-permute-done.15 = f32[1,32,1024]{2,1,0:T(8,128)S(1)} collective-permute-done((f32[1,32,1024]{2,1,0:T(8,128)S(1)}, f32[1,32,1024]{2,1,0:T(8,128)S(1)}, u32[]{:S(2)}, u32[]{:S(2)}) %collective-permute-start.15) | collective-permute-done | bytes 131104 | tf_op jit(solution)/shard_map/ppermute | solution.py:16
  75.0 0.3 collective-permute-start.16
  75.3 0.7 fusion.2
  76.0 4.9 %custom-call.8 = f32[1,64,64]{1,2,0:T(8,128)S(1)} custom-call(f32[1,64,64]{2,1,0:T(8,128)S(1)} %fusion.2), custom_call_target="InvertDiagBlocksLowerTriangular" | custom-call | tf_op jit(solution)/shard_map/triangular_solve | solution.py:71
  80.9 14.5 %collective-permute-done.16 = f32[1,32,1024]{2,1,0:T(8,128)S(1)} collective-permute-done((f32[1,32,1024]{2,1,0:T(8,128)S(1)}, f32[1,32,1024]{2,1,0:T(8,128)S(1)}, u32[]{:S(2)}, u32[]{:S(2)}) %collective-permute-start.16) | collective-permute-done | bytes 131104 | tf_op jit(solution)/shard_map/ppermute | solution.py:16
  95.4 5.2 %collective-permute-start.17 = (f32[1,32,1024]{2,1,0:T(8,128)S(1)}, f32[1,32,1024]{2,1,0:T(8,128)S(1)}, u32[]{:S(2)}, u32[]{:S(2)}) collective-permute-start(f32[1,32,1024]{2,1,0:T(8,128)S(1)} %add.126), channel_id=1, source_target_pairs={{0,8},{8,0},{16,24},{24,16},{1,9},{9,1},{17,25},{25,17},{2,10},{10... | collective-permute-start | bytes 393224 | tf_op jit(solution)/shard_map/ppermute | solution.py:16
  100.6 0.6 fusion.5
  101.3 0.0 collective-permute-done.1
  101.3 2.1 %add.108 = f32[1,128,1024]{2,1,0:T(8,128)} add(f32[1,128,1024]{2,1,0:T(8,128)} %dynamic-slice_add_fusion.1, f32[1,128,1024]{2,1,0:T(8,128)} %collective-permute-done.1) | non-fusion elementwise | flops 131072 | bytes 1572864 | tf_op jit(solution)/shard_map/add | solution.py:22
  103.3 0.0 collective-permute-start.2
  103.4 0.4 fusion.3
  103.8 1.7 %add.112 = f32[1,128,2048]{2,1,0:T(8,128)S(1)} add(f32[1,128,2048]{2,1,0:T(8,128)} %dynamic-slice_add_fusion, f32[1,128,2048]{2,1,0:T(8,128)} %collective-permute-done.4) | non-fusion elementwise | flops 262144 | bytes 3145728 | tf_op jit(solution)/shard_map/add | solution.py:22
  105.5 0.0 copy-start.6
  105.5 0.6 collective-permute-start.5
  106.1 18.0 %multiply_subtract_fusion = (f32[2048,1024]{1,0:T(8,128)}, f32[2048,1024]{1,0:T(8,128)}, f32[1,2048,1024]{2,1,0:T(8,128)}) fusion(f32[2048,1024]{1,0:T(8,128)} %param.17, f32[2048,1024]{1,0:T(8,128)} %param.19, f32[2048,1024]{1,0:T(8,128)} %copy-done.2, f32[64,2048]{1,0:T(8,128)S(1)} %fusion.5, f32[64,1024]{1,0:T(8,128)S(1)} %fusion.3), kind=kOutput, calls=%fused_computation.5 | convolution fusion | flops 1625292800 | bytes 51118080 | tf_op jit(solution)/shard_map/dot_general | solution.py:74
  124.1 1.4 %broadcast_select_fusion.3 = (f32[1,128,1024]{2,1,0:T(8,128)S(1)}, f32[1,128,1024]{2,1,0:T(8,128)S(1)}) fusion(f32[1,128,1024]{2,1,0:T(8,128)} %add.108, f32[1,128,1024]{2,1,0:T(8,128)} %collective-permute-done.2, pred[]{:T(512)S(6)} %eq.15), kind=kLoop, calls=%fused_computation.23 | loop fusion | flops 262144 | bytes 2097153 | tf_op jit(solution)/shard_map/jit(_where)/select_n | solution.py:37
  125.6 0.0 copy-start.1
  125.6 2.9 %multiply_subtract_fusion.2 = (f32[2,128,1024]{2,1,0:T(8,128)}, f32[2,128,1024]{2,1,0:T(8,128)}) fusion(f32[2,128,1024]{2,1,0:T(8,128)S(1)} %copy-done.6, f32[1,128,1024]{2,1,0:T(8,128)S(1)} %get-tuple-element.17, f32[1,128,1024]{2,1,0:T(8,128)S(1)} %get-tuple-element.16, f32[2,128,1024]{2,1,0:T(8,128)} %param.13), kind=kLoop, calls=%fused_computation.14 | loop fusion | flops 2097152 | bytes 5242880 | tf_op jit(solution)/shard_map/sub | solution.py:12
  128.5 1.4 %broadcast_select_fusion.1 = (f32[1,128,2048]{2,1,0:T(8,128)S(1)}, f32[1,128,2048]{2,1,0:T(8,128)S(1)}) fusion(f32[1,128,2048]{2,1,0:T(8,128)S(1)} %add.112, f32[1,128,2048]{2,1,0:T(8,128)} %collective-permute-done.5, pred[]{:T(512)S(6)} %eq.15), kind=kLoop, calls=%fused_computation.19 | loop fusion | flops 524288 | bytes 4194305 | tf_op jit(solution)/shard_map/jit(_where)/select_n | solution.py:37
  130.0 2.9 %multiply_subtract_fusion.1 = (f32[2,128,2048]{2,1,0:T(8,128)}, f32[2,128,2048]{2,1,0:T(8,128)}) fusion(f32[2,128,2048]{2,1,0:T(8,128)S(1)} %copy-done.3, f32[1,128,2048]{2,1,0:T(8,128)S(1)} %get-tuple-element.15, f32[1,128,2048]{2,1,0:T(8,128)S(1)} %get-tuple-element.14, f32[2,128,2048]{2,1,0:T(8,128)S(1)} %copy-done.8), kind=kLoop, calls=%fused_computation.9 | loop fusion | flops 4194304 | bytes 10485760 | tf_op jit(solution)/shard_map/sub | solution.py:12
  (34 shorter events, 0.4 us)
Async XLA Ops:
  0.6 13.2 %copy-start = (f32[64,1024]{1,0:T(8,128)S(1)}, f32[64,1024]{1,0:T(8,128)}, u32[]{:S(2)}) copy-start(f32[64,1024]{1,0:T(8,128)} %param.21) | copy-start | bytes 786436
  10.4 3.4 %copy-start.2 = (f32[2048,1024]{1,0:T(8,128)}, f32[2048,1024]{1,0:T(8,128)S(1)}, u32[]{:S(2)}) copy-start(f32[2048,1024]{1,0:T(8,128)S(1)} %bitcast_add_fusion) | copy-start | bytes 25165828
  13.9 14.3 %copy-start.5 = (f32[2,128,1024]{2,1,0:T(8,128)S(1)}, f32[2,128,1024]{2,1,0:T(8,128)}, u32[]{:S(2)}) copy-start(f32[2,128,1024]{2,1,0:T(8,128)} %param.11) | copy-start | bytes 3145732
  13.9 21.6 %copy-start.3 = (f32[2,128,2048]{2,1,0:T(8,128)S(1)}, f32[2,128,2048]{2,1,0:T(8,128)}, u32[]{:S(2)}) copy-start(f32[2,128,2048]{2,1,0:T(8,128)} %param.14) | copy-start | bytes 6291460
  22.1 0.8 copy-start.9
  22.9 1.7 %collective-permute-start.6 = (f32[1,32,2048]{2,1,0:T(8,128)S(1)}, f32[1,32,2048]{2,1,0:T(8,128)}, u32[]{:S(2)}, u32[]{:S(2)}) collective-permute-start(f32[1,32,2048]{2,1,0:T(8,128)S(1)} %constant_dynamic-slice_fusion.1), channel_id=1, source_target_pairs={{0,8},{8,0},{16,24},{24,16},{1,9},{9,1},{17,25},{25,17},{2,10},{10... | collective-permute-start | bytes 786440 | tf_op jit(solution)/shard_map/ppermute | solution.py:16
  25.7 8.8 %collective-permute-start.7 = (f32[1,32,2048]{2,1,0:T(8,128)S(1)}, f32[1,32,2048]{2,1,0:T(8,128)S(1)}, u32[]{:S(2)}, u32[]{:S(2)}) collective-permute-start(f32[1,32,2048]{2,1,0:T(8,128)S(1)} %dynamic-slice_add_fusion.2), channel_id=1, source_target_pairs={{0,16},{8,24},{16,0},{24,8},{1,17},{9,25},{17,1},{25,9},{2,18},{10... | collective-permute-start | bytes 786440 | tf_op jit(solution)/shard_map/ppermute | solution.py:16
  29.5 5.0 %copy-start.7 = (f32[2,128,1024]{2,1,0:T(8,128)}, f32[2,128,1024]{2,1,0:T(8,128)S(1)}, u32[]{:S(2)}) copy-start(f32[2,128,1024]{2,1,0:T(8,128)S(1)} %bitcast_subtract_fusion.2) | copy-start | bytes 3145732
  30.4 24.5 %collective-permute-start = (f32[1,128,1024]{2,1,0:T(8,128)}, f32[1,128,1024]{2,1,0:T(8,128)}, u32[]{:S(2)}, u32[]{:S(2)}) collective-permute-start(f32[1,128,1024]{2,1,0:T(8,128)} %constant_dynamic-slice_fusion.3), channel_id=1, source_target_pairs={{0,8},{8,0},{16,24},{24,16},{1,9},{9,1},{17,25},{25,17},{2,10},{10... | collective-permute-start | bytes 1572872 | tf_op jit(solution)/shard_map/ppermute | solution.py:16
  34.6 5.2 %collective-permute-start.8 = (f32[1,32,2048]{2,1,0:T(8,128)S(1)}, f32[1,32,2048]{2,1,0:T(8,128)S(1)}, u32[]{:S(2)}, u32[]{:S(2)}) collective-permute-start(f32[1,32,2048]{2,1,0:T(8,128)S(1)} %add.117), channel_id=1, source_target_pairs={{0,8},{8,0},{16,24},{24,16},{1,9},{9,1},{17,25},{25,17},{2,10},{10... | collective-permute-start | bytes 786440 | tf_op jit(solution)/shard_map/ppermute | solution.py:16
  37.4 1.3 copy-start.4
  39.7 29.6 %collective-permute-start.3 = (f32[1,128,2048]{2,1,0:T(8,128)}, f32[1,128,2048]{2,1,0:T(8,128)}, u32[]{:S(2)}, u32[]{:S(2)}) collective-permute-start(f32[1,128,2048]{2,1,0:T(8,128)} %constant_dynamic-slice_fusion.2), channel_id=1, source_target_pairs={{0,8},{8,0},{16,24},{24,16},{1,9},{9,1},{17,25},{25,17},{2,10},{10... | collective-permute-start | bytes 3145736 | tf_op jit(solution)/shard_map/ppermute | solution.py:16
  40.4 9.3 %collective-permute-start.9 = (f32[64,64]{0,1:T(8,128)S(1)}, f32[64,64]{0,1:T(8,128)S(1)}, u32[]{:S(2)}, u32[]{:S(2)}) collective-permute-start(f32[64,64]{0,1:T(8,128)S(1)} %fusion.9), channel_id=1, source_target_pairs={{0,1},{1,0},{2,3},{3,2},{4,5},{5,4},{6,7},{7,6},{8,9},{9,8},{10,11... | collective-permute-start | bytes 49160 | tf_op jit(solution)/shard_map/ppermute | solution.py:16
  49.7 2.8 %collective-permute-start.10 = (f32[64,64]{0,1:T(8,128)S(1)}, f32[64,64]{0,1:T(8,128)S(1)}, u32[]{:S(2)}, u32[]{:S(2)}) collective-permute-start(f32[64,64]{0,1:T(8,128)S(1)} %add.118), channel_id=1, source_target_pairs={{0,2},{1,3},{2,0},{3,1},{4,6},{5,7},{6,4},{7,5},{8,10},{9,11},{10,... | collective-permute-start | bytes 49160 | tf_op jit(solution)/shard_map/ppermute | solution.py:16
  51.1 7.1 %collective-permute-start.12 = (f32[1,32,1024]{2,1,0:T(8,128)S(1)}, f32[1,32,1024]{2,1,0:T(8,128)S(1)}, u32[]{:S(2)}, u32[]{:S(2)}) collective-permute-start(f32[1,32,1024]{2,1,0:T(8,128)S(1)} %constant_dynamic-slice_fusion), channel_id=1, source_target_pairs={{0,8},{8,0},{16,24},{24,16},{1,9},{9,1},{17,25},{25,17},{2,10},{10... | collective-permute-start | bytes 393224 | tf_op jit(solution)/shard_map/ppermute | solution.py:16
  52.6 5.6 %collective-permute-start.11 = (f32[64,64]{0,1:T(8,128)S(1)}, f32[64,64]{0,1:T(8,128)S(1)}, u32[]{:S(2)}, u32[]{:S(2)}) collective-permute-start(f32[64,64]{0,1:T(8,128)S(1)} %add.119), channel_id=1, source_target_pairs={{0,4},{1,5},{2,6},{3,7},{4,0},{5,1},{6,2},{7,3},{8,12},{9,13},{10,... | collective-permute-start | bytes 49160 | tf_op jit(solution)/shard_map/ppermute | solution.py:16
  56.9 44.3 %collective-permute-start.1 = (f32[1,128,1024]{2,1,0:T(8,128)}, f32[1,128,1024]{2,1,0:T(8,128)}, u32[]{:S(2)}, u32[]{:S(2)}) collective-permute-start(f32[1,128,1024]{2,1,0:T(8,128)} %dynamic-slice_add_fusion.1), channel_id=1, source_target_pairs={{0,16},{8,24},{16,0},{24,8},{1,17},{9,25},{17,1},{25,9},{2,18},{10... | collective-permute-start | bytes 1572872 | tf_op jit(solution)/shard_map/ppermute | solution.py:16
  58.3 6.2 %collective-permute-start.13 = (f32[1,32,1024]{2,1,0:T(8,128)S(1)}, f32[1,32,1024]{2,1,0:T(8,128)S(1)}, u32[]{:S(2)}, u32[]{:S(2)}) collective-permute-start(f32[1,32,1024]{2,1,0:T(8,128)S(1)} %dynamic-slice_add_fusion.3), channel_id=1, source_target_pairs={{0,1},{1,0},{2,3},{3,2},{4,5},{5,4},{6,7},{7,6},{8,9},{9,8},{10,11... | collective-permute-start | bytes 393224 | tf_op jit(solution)/shard_map/ppermute | solution.py:16
  64.5 4.3 %collective-permute-start.14 = (f32[1,32,1024]{2,1,0:T(8,128)S(1)}, f32[1,32,1024]{2,1,0:T(8,128)S(1)}, u32[]{:S(2)}, u32[]{:S(2)}) collective-permute-start(f32[1,32,1024]{2,1,0:T(8,128)S(1)} %add.123), channel_id=1, source_target_pairs={{0,2},{1,3},{2,0},{3,1},{4,6},{5,7},{6,4},{7,5},{8,10},{9,11},{10,... | collective-permute-start | bytes 393224 | tf_op jit(solution)/shard_map/ppermute | solution.py:16
  68.8 6.2 %collective-permute-start.15 = (f32[1,32,1024]{2,1,0:T(8,128)S(1)}, f32[1,32,1024]{2,1,0:T(8,128)S(1)}, u32[]{:S(2)}, u32[]{:S(2)}) collective-permute-start(f32[1,32,1024]{2,1,0:T(8,128)S(1)} %add.124), channel_id=1, source_target_pairs={{0,4},{1,5},{2,6},{3,7},{4,0},{5,1},{6,2},{7,3},{8,12},{9,13},{10,... | collective-permute-start | bytes 393224 | tf_op jit(solution)/shard_map/ppermute | solution.py:16
  71.9 31.9 %collective-permute-start.4 = (f32[1,128,2048]{2,1,0:T(8,128)}, f32[1,128,2048]{2,1,0:T(8,128)}, u32[]{:S(2)}, u32[]{:S(2)}) collective-permute-start(f32[1,128,2048]{2,1,0:T(8,128)} %dynamic-slice_add_fusion), channel_id=1, source_target_pairs={{0,16},{8,24},{16,0},{24,8},{1,17},{9,25},{17,1},{25,9},{2,18},{10... | collective-permute-start | bytes 3145736 | tf_op jit(solution)/shard_map/ppermute | solution.py:16
  75.0 20.4 %collective-permute-start.16 = (f32[1,32,1024]{2,1,0:T(8,128)S(1)}, f32[1,32,1024]{2,1,0:T(8,128)S(1)}, u32[]{:S(2)}, u32[]{:S(2)}) collective-permute-start(f32[1,32,1024]{2,1,0:T(8,128)S(1)} %add.125), channel_id=1, source_target_pairs={{0,16},{8,24},{16,0},{24,8},{1,17},{9,25},{17,1},{25,9},{2,18},{10... | collective-permute-start | bytes 393224 | tf_op jit(solution)/shard_map/ppermute | solution.py:16
  95.4 7.9 %collective-permute-start.17 = (f32[1,32,1024]{2,1,0:T(8,128)S(1)}, f32[1,32,1024]{2,1,0:T(8,128)S(1)}, u32[]{:S(2)}, u32[]{:S(2)}) collective-permute-start(f32[1,32,1024]{2,1,0:T(8,128)S(1)} %add.126), channel_id=1, source_target_pairs={{0,8},{8,0},{16,24},{24,16},{1,9},{9,1},{17,25},{25,17},{2,10},{10... | collective-permute-start | bytes 393224 | tf_op jit(solution)/shard_map/ppermute | solution.py:16
  103.3 20.8 %collective-permute-start.2 = (f32[1,128,1024]{2,1,0:T(8,128)}, f32[1,128,1024]{2,1,0:T(8,128)}, u32[]{:S(2)}, u32[]{:S(2)}) collective-permute-start(f32[1,128,1024]{2,1,0:T(8,128)} %add.108), channel_id=1, source_target_pairs={{0,8},{8,0},{16,24},{24,16},{1,9},{9,1},{17,25},{25,17},{2,10},{10... | collective-permute-start | bytes 1572872 | tf_op jit(solution)/shard_map/ppermute | solution.py:16
  105.5 20.0 %copy-start.6 = (f32[2,128,1024]{2,1,0:T(8,128)S(1)}, f32[2,128,1024]{2,1,0:T(8,128)}, u32[]{:S(2)}) copy-start(f32[2,128,1024]{2,1,0:T(8,128)} %param.11) | copy-start | bytes 3145732
  105.5 23.0 %collective-permute-start.5 = (f32[1,128,2048]{2,1,0:T(8,128)S(1)}, f32[1,128,2048]{2,1,0:T(8,128)}, u32[]{:S(2)}, u32[]{:S(2)}) collective-permute-start(f32[1,128,2048]{2,1,0:T(8,128)S(1)} %add.112), channel_id=1, source_target_pairs={{0,8},{8,0},{16,24},{24,16},{1,9},{9,1},{17,25},{25,17},{2,10},{10... | collective-permute-start | bytes 3145736 | tf_op jit(solution)/shard_map/ppermute | solution.py:16
  124.1 5.8 %copy-start.8 = (f32[2,128,2048]{2,1,0:T(8,128)S(1)}, f32[2,128,2048]{2,1,0:T(8,128)}, u32[]{:S(2)}) copy-start(f32[2,128,2048]{2,1,0:T(8,128)} %param.16) | copy-start | bytes 6291460
  125.6 7.2 %copy-start.1 = (f32[64,1024]{1,0:T(8,128)S(1)}, f32[64,1024]{1,0:T(8,128)}, u32[]{:S(2)}) copy-start(f32[64,1024]{1,0:T(8,128)} %param.21) | copy-start | bytes 786436

commit v2 on v0

v2 whole, which is shorter than its diff:
```python
import functools
import math

import jax
import jax.numpy as jnp
from jax import lax
from jax.experimental import pallas as pl
from jax.experimental.pallas import tpu as pltpu
from jax.sharding import PartitionSpec as P

outer_rate = 0.7
momentum_decay = 0.9
MIB = 1 << 20


def nesterov(weights, gradient, moment):
    velocity = momentum_decay * moment + gradient
    return (weights - outer_rate * (gradient + momentum_decay * velocity), velocity)


def split3(value):
    high = value.astype(jnp.bfloat16)
    rest = value - high.astype(jnp.float32)
    middle = rest.astype(jnp.bfloat16)
    low = (rest - middle.astype(jnp.float32)).astype(jnp.bfloat16)
    return high, middle, low


def stacked_product(parts, right, dims):
    rows = parts.shape[0] // 3
    high, middle, low = split3(right)
    dot = functools.partial(lax.dot_general, dimension_numbers=(dims, ((), ())), preferred_element_type=jnp.float32)
    one = dot(parts, high)
    two = dot(parts[: 2 * rows], middle)
    three = dot(parts[:rows], low)
    small = one[2 * rows :] + two[rows:] + three
    return one[:rows] + (one[rows : 2 * rows] + two[:rows] + small)


def swap(value, axis, bit):
    return lax.ppermute(value, axis, [(i, i ^ bit) for i in range(lax.axis_size(axis))])


def doubled(value, axis, first=1):
    bit = first
    while bit < lax.axis_size(axis):
        value = value + swap(value, axis, bit)
        bit *= 2
    return value


def sum_over_chips(value, after):
    bit = 2
    while bit < lax.axis_size("replica"):
        value = sum_call(value, swap(value, "replica", bit), after)
        bit *= 2
    return value


def in_hbm(value):
    return pltpu.with_memory_space_constraint(value, pltpu.HBM)


def in_vmem(value):
    return pltpu.with_memory_space_constraint(value, pltpu.VMEM)


VMEM = pl.BlockSpec(memory_space=pltpu.VMEM)
SMEM = pl.BlockSpec(memory_space=pltpu.SMEM)
ANY = pl.BlockSpec(memory_space=pl.ANY)


def ordered(first, mine, other):
    return jnp.concatenate([jnp.where(first, mine, other), jnp.where(first, other, mine)], axis=0)


def left_kernel(chunk_after, core, weights, copies, error, warm, *refs):
    corrected, held, away, kept, parts = refs[chunk_after:]
    step = pl.program_id(0)
    rows = weights.shape[0]
    half = away.shape[0]

    @pl.when(step == 0)
    def _():
        first = core[0] == 0
        top, bottom = warm[:half], warm[half:]
        both = jnp.concatenate([jnp.where(first, bottom, top), jnp.where(first, top, bottom)], axis=0)
        parts[...] = jnp.concatenate(split3(both), axis=0)

    value = weights[...] - copies[0] + error[0]
    here = pl.ds(pl.multiple_of(step * rows, rows), rows)
    corrected[here, :] = value
    held[here, :] = weights[...]
    left = stacked_product(parts[...], value, ((1,), (1,)))
    away[...] = left[:half]
    kept[...] = left[half:]


def left_call(core, weights, copies, error, warm, after, start, rows, block):
    rank, width = warm.shape
    first = start // block
    row = lambda i: (first + i, 0)
    lead = lambda i: (0, first + i, 0)
    return pl.pallas_call(
        functools.partial(left_kernel, len(after)),
        grid=(rows // block,),
        in_specs=[
            SMEM,
            pl.BlockSpec((block, width), row),
            pl.BlockSpec((1, block, width), lead),
            pl.BlockSpec((1, block, width), lead),
            VMEM,
        ]
        + [ANY] * len(after),
        out_specs=[
            VMEM,
            VMEM,
            pl.BlockSpec((rank // 2, block), lambda i: (0, i)),
            pl.BlockSpec((rank // 2, block), lambda i: (0, i)),
        ],
        out_shape=[
            pltpu.VMEM((rows, width), jnp.float32),
            pltpu.VMEM((rows, width), jnp.float32),
            jax.ShapeDtypeStruct((rank // 2, rows), jnp.float32),
            jax.ShapeDtypeStruct((rank // 2, rows), jnp.float32),
        ],
        scratch_shapes=[pltpu.VMEM((3 * rank, width), jnp.bfloat16)],
        compiler_params=pltpu.CompilerParams(vmem_limit_bytes=26 * MIB),
        name="left",
    )(core, in_hbm(weights), in_hbm(copies), in_hbm(error), warm, *after)


def right_kernel(scale, block, core, mine, other, corrected, *refs):
    away, kept, left = refs[-3:]
    half, rows = mine.shape
    width = corrected.shape[1]
    first = core[0] == 0
    whole = ordered(first, mine[...] * scale, other[...] * scale)
    left[...] = whole
    parts = jnp.concatenate(split3(whole), axis=0)
    total = None
    for i in range(rows // block):
        cut = slice(i * block, (i + 1) * block)
        term = stacked_product(parts[:, cut], corrected[cut, :], ((1,), (0,)))
        total = term if total is None else total + term
    square = stacked_product(parts, whole, ((1,), (1,)))
    top, bottom = total[:half], total[half:]
    away_value, kept_value = jnp.where(first, bottom, top), jnp.where(first, top, bottom)
    gram = jnp.concatenate([square[:half], square[half:]], axis=1)
    if len(refs) > 3:
        away_before, kept_before = refs[:2]
        away_value = away_value + away_before[:, :width]
        kept_value = kept_value + kept_before[:, :width]
        gram = gram + kept_before[:, width:]
    away[:, :width] = away_value
    away[:, width:] = jnp.zeros_like(gram)
    kept[:, :width] = kept_value
    kept[:, width:] = gram


def right_call(core, mine, other, corrected, before, scale, block):
    half, rows = mine.shape
    width = corrected.shape[1]
    message = jax.ShapeDtypeStruct((half, width + 4 * half), jnp.float32)
    return pl.pallas_call(
        functools.partial(right_kernel, scale, block),
        in_specs=[SMEM] + [VMEM] * (3 + len(before)),
        out_specs=[VMEM] * 3,
        out_shape=[message, message, jax.ShapeDtypeStruct((2 * half, rows), jnp.float32)],
        compiler_params=pltpu.CompilerParams(vmem_limit_bytes=12 * MIB),
        name="right",
    )(core, mine, other, in_vmem(corrected), *before)


def factor_kernel(width, message, *refs):
    chunks = (len(refs) - 1) // 2
    left, inverse, basis = refs[:chunks], refs[chunks], refs[chunks + 1 :]
    half = message.shape[0]
    rank = 2 * half
    pair = message[:, width:]
    gram = jnp.concatenate([pair[:, :rank], pair[:, rank:]], axis=0)
    eye = jnp.where(
        lax.broadcasted_iota(jnp.int32, (rank, rank), 0) == lax.broadcasted_iota(jnp.int32, (rank, rank), 1), 1.0, 0.0
    )
    both = jnp.concatenate([gram, eye], axis=1)
    bands = [both[i : i + 8, :] for i in range(0, rank, 8)]
    for j in range(rank):
        band, line = divmod(j, 8)
        row = bands[band][line : line + 1, :]
        root = lax.rsqrt(row[:, j : j + 1])
        row = row * root
        inverse[j : j + 1, :] = row[:, rank:]
        for i in range(band, rank // 8):
            bands[i] = bands[i] - (bands[i][:, j : j + 1] * root) * row
    for chunk in range(chunks):
        rows = lax.dot_general(
            inverse[...],
            left[chunk][...],
            (((1,), (0,)), ((), ())),
            precision=lax.Precision.HIGHEST,
            preferred_element_type=jnp.float32,
        )
        high, middle, low = split3(rows.T)
        basis[chunk][...] = jnp.concatenate([high, high, middle, high, low, middle], axis=1)


def factor_call(message, left, width):
    half = message.shape[0]
    rank = 2 * half
    return pl.pallas_call(
        functools.partial(factor_kernel, width),
        in_specs=[VMEM] * (1 + len(left)),
        out_specs=[VMEM] * (1 + len(left)),
        out_shape=[jax.ShapeDtypeStruct((rank, rank), jnp.float32)]
        + [jax.ShapeDtypeStruct((piece.shape[1], 6 * rank), jnp.bfloat16) for piece in left],
        compiler_params=pltpu.CompilerParams(vmem_limit_bytes=12 * MIB),
        name="factor",
    )(message, *left)


def final_kernel(scale, chunks, core, mine, other, inverse, moment, *refs):
    weights, corrected, basis = refs[:chunks], refs[chunks : 2 * chunks], refs[2 * chunks : 3 * chunks]
    updated, velocity, carried, parts = refs[3 * chunks :]
    step = pl.program_id(0)
    rows, width = updated.shape
    here = pl.ds(pl.multiple_of(step * rows, rows), rows)

    @pl.when(step == 0)
    def _():
        whole = ordered(core[0] == 0, mine[:, :width] * scale, other[:, :width] * scale)
        right = lax.dot_general(
            inverse[...], whole, (((1,), (0,)), ((), ())), precision=lax.Precision.HIGHEST, preferred_element_type=jnp.float32
        )
        high, middle, low = split3(right)
        parts[...] = jnp.concatenate([high, middle, high, low, high, middle], axis=0)

    def work(chunk, at):
        there = pl.ds(pl.multiple_of(at, rows), rows)
        change = jnp.dot(basis[chunk][there, :], parts[...], preferred_element_type=jnp.float32)
        carried[0] = corrected[chunk][there, :] - change
        new, speed = nesterov(weights[chunk][there, :], change, moment[here, :])
        updated[...] = new
        velocity[...] = speed

    per = corrected[0].shape[0] // rows
    for chunk in range(chunks):
        pl.when(step // per == chunk)(functools.partial(work, chunk, (step - chunk * per) * rows))


def final_call(core, mine, other, inverse, moment, weights, corrected, basis, scale, block):
    rows, width = moment.shape
    rank = inverse.shape[0]
    chunks = len(corrected)
    out = pl.BlockSpec((block, width), lambda i: (i, 0))
    large = [in_vmem(value) for value in (moment, *weights, *corrected, *basis)]
    return pl.pallas_call(
        functools.partial(final_kernel, scale, chunks),
        grid=(rows // block,),
        in_specs=[SMEM] + [VMEM] * (3 + len(large)),
        out_specs=[out, out, pl.BlockSpec((1, block, width), lambda i: (0, i, 0))],
        out_shape=[
            jax.ShapeDtypeStruct((rows, width), jnp.float32),
            jax.ShapeDtypeStruct((rows, width), jnp.float32),
            jax.ShapeDtypeStruct((1, rows, width), jnp.float32),
        ],
        scratch_shapes=[pltpu.VMEM((6 * rank, width), jnp.bfloat16)],
        compiler_params=pltpu.CompilerParams(vmem_limit_bytes=16 * MIB),
        name="final",
    )(core, mine, other, inverse, *large)


def sum_kernel(one, two, *refs):
    refs[-1][...] = one[...] + two[...]


def sum_call(one, two, after):
    return pl.pallas_call(
        sum_kernel,
        in_specs=[VMEM] * 2 + [ANY] * len(after),
        out_specs=VMEM,
        out_shape=jax.ShapeDtypeStruct(one.shape, one.dtype),
        compiler_params=pltpu.CompilerParams(vmem_limit_bytes=8 * MIB),
        name="sum",
    )(one, two, *after)


def term_kernel(core, weights, copies, received, *refs):
    at = core[0]
    refs[-1][0] = (weights[at] - copies[0, at]) + (weights[at] - received[0, at])


def term_call(core, weights, copies, received, after):
    return pl.pallas_call(
        term_kernel,
        in_specs=[SMEM] + [VMEM] * 3 + [ANY] * len(after),
        out_specs=VMEM,
        out_shape=jax.ShapeDtypeStruct((1, *weights.shape[1:]), jnp.float32),
        compiler_params=pltpu.CompilerParams(vmem_limit_bytes=12 * MIB),
        name="term",
    )(core, weights, copies, received, *after)


def layer_kernel(scale, core, mine, other, weights, moment, *refs):
    updated, velocity = refs[-2:]
    for value, at in ((mine, core[0]), (other, 1 - core[0])):
        updated[at], velocity[at] = nesterov(weights[at], value[0] * scale, moment[at])


def layer_call(core, mine, other, weights, moment, after, scale):
    return pl.pallas_call(
        functools.partial(layer_kernel, scale),
        in_specs=[SMEM] + [VMEM] * 4 + [ANY] * len(after),
        out_specs=[VMEM] * 2,
        out_shape=[jax.ShapeDtypeStruct(weights.shape, jnp.float32)] * 2,
        compiler_params=pltpu.CompilerParams(vmem_limit_bytes=16 * MIB),
        name="layer",
    )(core, mine, other, weights, moment, *after)


def local(
    square_weights,
    square_copies,
    square_moment,
    broad_weights,
    broad_copies,
    broad_moment,
    embed_weights,
    embed_copies,
    embed_moment,
    embed_error,
    warm_start,
):
    replicas = lax.axis_size("replica")
    scale = 1 / replicas
    rank, width = warm_start.shape
    rows = embed_weights.shape[0]
    chunks = 2 if rows % 512 == 0 else 1
    size = rows // chunks
    block = math.gcd(size, 256)
    wide = math.gcd(size, 512)
    core = jnp.reshape(lax.axis_index("replica") % 2, (1,)).astype(jnp.int32)

    square_received = swap(square_copies, "replica", 1)
    broad_received = swap(broad_copies, "replica", 1)
    corrected, held, halves, after = [], [], [], ()
    for chunk in range(chunks):
        value, weights, away, kept = left_call(
            core, embed_weights, embed_copies, embed_error, warm_start, after, chunk * size, size, wide
        )
        corrected.append(value)
        held.append(weights)
        halves.append(sum_call(kept, swap(away, "replica", 1), ()))
        if chunk == 0:
            square_half = term_call(core, square_weights, square_copies, square_received, (away,))
            after = (square_half, halves[0])
    left, before = [], ()
    for chunk in range(chunks):
        half = doubled(halves[chunk], "replica", 2)
        other = swap(half, "replica", 1)
        *before, piece = right_call(core, half, other, corrected[chunk], before, scale, block)
        left.append(piece)
    away, kept = before
    broad_half = term_call(core, broad_weights, broad_copies, broad_received, (half,))

    message = sum_call(kept, swap(away, "replica", 1), ())
    inner = lax.axis_size("inner")
    bit = 1
    while bit < inner:
        received = swap(message, "inner", bit)
        after = ()
        if 2 * bit >= inner:
            square_half = sum_over_chips(square_half, (message,))
            square_other = swap(square_half, "replica", 1)
            square_updated, square_velocity = layer_call(
                core, square_half, square_other, square_weights, square_moment, (), scale
            )
            after = (square_velocity,)
        message = sum_call(message, received, after)
        bit *= 2
    inverse, *basis = factor_call(message, left, width)
    right_half = sum_over_chips(message, (inverse,))
    broad_half = sum_over_chips(broad_half, (inverse,))
    broad_other = swap(broad_half, "replica", 1)
    broad_updated, broad_velocity = layer_call(
        core, broad_half, broad_other, broad_weights, broad_moment, (right_half,), scale
    )
    right_other = swap(right_half, "replica", 1)
    embed_updated, embed_velocity, embed_carried = final_call(
        core, right_half, right_other, inverse, embed_moment, held, corrected, basis, scale, block
    )
    return (
        square_updated,
        square_velocity,
        broad_updated,
        broad_velocity,
        embed_updated,
        embed_velocity,
        embed_carried,
    )


def solution(mesh):
    in_specs = (
        P(None, "inner", None),
        P("replica", None, "inner", None),
        P(None, "inner", None),
        P(None, "inner", None),
        P("replica", None, "inner", None),
        P(None, "inner", None),
        P("inner", None),
        P("replica", "inner", None),
        P("inner", None),
        P("replica", "inner", None),
        P(),
    )
    out_specs = (
        P(None, "inner", None),
        P(None, "inner", None),
        P(None, "inner", None),
        P(None, "inner", None),
        P("inner", None),
        P("inner", None),
        P("replica", "inner", None),
    )
    return jax.shard_map(local, mesh=mesh, in_specs=in_specs, out_specs=out_specs, check_vma=False)
```

time: 325 us -> 84.2 us (0.26)
  waiting for transfers between devices: 200 us -> 23.7 us
  matrix products: 41.1 us -> 0 us
  Pallas kernels: 0 us -> 37.5 us
  other arithmetic: 33.7 us -> 0.03 us
  blocking collectives: 30.1 us -> 0 us
  starting transfers between devices: 0.08 us -> 19.5 us
  between operations: 14.2 us -> 0.84 us
    psum x2 -> x0, waiting for transfers between devices: 200 us -> none  [the longest x1 121 us: local(): right_total = lax.psum(right_term, ('replica', 'inner'))]
    dot_general x4 -> x0, matrix products: 39.4 us -> none  [the longest x1 20.4 us: local(): lax.dot_general(basis_rows, right_factor, (((0,), (0,)), ((), ())), preci...]
    pallas_call x0 -> x19, Pallas kernels: none -> 37.5 us  [the longest x2 12.7 us: left_call(): pl.pallas_call(functools.partial(left_kernel, len(after)), grid=(rows //...]
    psum x1 -> x0, blocking collectives: 30.1 us -> none  [local(): gram_matrix = lax.psum(gram_local, 'inner')]
    ppermute x0 -> x18, waiting for transfers between devices: none -> 23.7 us  [swap(): lax.ppermute(value, axis, [(i, i ^ bit) for i in range(lax.axis_size(axis...]
    ppermute x0 -> x18, starting transfers between devices: none -> 19.5 us  [swap(): lax.ppermute(value, axis, [(i, i ^ bit) for i in range(lax.axis_size(axis...]
    sub x4 -> x0, other arithmetic: 14.3 us -> none  [the longest x2 6.98 us: nesterov(): weights - outer_rate * (gradient + momentum_decay * velocity)]
    another operation x5 -> x0, other arithmetic: 12.1 us -> none  [the longest x3 6.52 us: local(): lower_factor = jnp.linalg.cholesky(gram_matrix)]
  transfers between devices with their start and end apart: 2 -> 18, of which waited for: 2 -> 9; matrix products, arithmetic and copies ran while one was open for 2% -> 0% of each run, Pallas kernels for 0% -> 42%
where the time goes in v2:
time: 84.2 us; the launch traced here: 83.7 us
  Pallas kernels  37.5 us (45%)
  waiting for transfers between devices  23.7 us (28%)
  starting transfers between devices  19.5 us (23%)
  local copies, waits for them, and re-layouts  2.22 us (3%)
    ppermute x18, waiting for transfers between devices, swap(): lax.ppermute(value, axis, [(i, i ^ bit) for i in range(lax.axis_size(axis...  23.7 us
    ppermute x18, starting transfers between devices, swap(): lax.ppermute(value, axis, [(i, i ^ bit) for i in range(lax.axis_size(axis...  19.5 us
    pallas_call x2, Pallas kernels, left_call(): pl.pallas_call(functools.partial(left_kernel, len(after)), grid=(rows //...  12.7 us
    pallas_call x1, Pallas kernels, final_call(): pl.pallas_call(functools.partial(final_kernel, scale, chunks), grid=(rows...  10.2 us
    pallas_call x1, Pallas kernels, factor_call(): pl.pallas_call(functools.partial(factor_kernel, width), in_specs=[VMEM] *...  6.45 us
    pallas_call x2, Pallas kernels, layer_call(): pl.pallas_call(functools.partial(layer_kernel, scale), in_specs=[SMEM] +...  4.27 us
    pallas_call x2, Pallas kernels, right_call(): pl.pallas_call(functools.partial(right_kernel, scale, block), in_specs=[S...  3.43 us
    unnamed x20, local copies, waits for them, and re-layouts  2.22 us
  transfers between devices with their start and end apart: 18, of which 9 were waited for; matrix products, arithmetic and copies ran while one was open for 0% of the time, Pallas kernels for 42%

profile of v2, /device:TPU:1, one launch (start us, length us, event | category | flops | bytes accessed | tf_op | source)
XLA Modules:
  0.0 83.7 jit_solution(5513305030615704402)
XLA Ops:
  0.6 0.1 collective-permute-start.12
  0.8 0.5 collective-permute-start
  1.2 0.0 copy-start.4
  1.2 0.9 %copy-done.4 = f32[64,1024]{1,0:T(8,128)S(1)} copy-done((f32[64,1024]{1,0:T(8,128)S(1)}, f32[64,1024]{1,0:T(8,128)}, u32[]{:S(2)}) %copy-start.4) | copy-done | bytes 262168
  2.2 0.0 copy-start.1
  2.2 6.3 %left.2 = (f32[1024,1024]{1,0:T(8,128)S(1)}, f32[1024,1024]{1,0:T(8,128)S(1)}, f32[32,1024]{1,0:T(8,128)S(1)}, f32[32,1024]{1,0:T(8,128)S(1)}) custom-call(s32[1]{0:T(128)} %bitcast.core, f32[2048,1024]{1,0:T(8,128)} %weights.8, f32[1,2048,1024]{2,1,0:T(8,128)} %copies.6, f32[1,2048,1024]{2,1,0:T(8,128)} %error.3, f32[64,1024]{1,0:T(8,128)S(1)} %copy-done.4), custom_call_target="tpu_custom_call" | custom-call | tf_op jit(solution)/shard_map/left/pallas_call | solution.py:104
  8.5 0.1 collective-permute-start.2
  8.6 1.3 %collective-permute-done.2.two = f32[32,1024]{1,0:T(8,128)S(1)} collective-permute-done((f32[32,1024]{1,0:T(8,128)S(1)}, f32[32,1024]{1,0:T(8,128)S(1)}, u32[]{:S(2)}, u32[]{:S(2)}) %collective-permute-start.2) | collective-permute-done | bytes 131104 | tf_op jit(solution)/shard_map/ppermute | solution.py:41
  9.9 0.0 collective-permute-done.received
  9.9 0.0 copy-done.1
  9.9 0.0 copy-done.7
  10.0 0.1 term.2.refs_0_.one
  10.0 0.0 copy-start
  10.1 0.0 copy-start.3
  10.1 6.4 %left.3 = (f32[1024,1024]{1,0:T(8,128)S(1)}, f32[1024,1024]{1,0:T(8,128)S(1)}, f32[32,1024]{1,0:T(8,128)S(1)}, f32[32,1024]{1,0:T(8,128)S(1)}) custom-call(s32[1]{0:T(128)} %bitcast.core, f32[2048,1024]{1,0:T(8,128)} %weights.8, f32[1,2048,1024]{2,1,0:T(8,128)} %copies.6, f32[1,2048,1024]{2,1,0:T(8,128)} %error.3, f32[64,1024]{1,0:T(8,128)S(1)} %copy-done.4, ...), custom_call_target="tpu_custom_call" | custom-call | tf_op jit(solution)/shard_map/left/pallas_call | solution.py:104
  16.4 0.2 collective-permute-start.3
  16.6 2.6 %collective-permute-start.6 = (f32[32,1024]{1,0:T(8,128)S(1)}, f32[32,1024]{1,0:T(8,128)S(1)}, u32[]{:S(2)}, u32[]{:S(2)}) collective-permute-start(f32[32,1024]{1,0:T(8,128)S(1)} %sum.9.refs_1_), channel_id=1, source_target_pairs={{0,16},{8,24},{16,0},{24,8},{1,17},{9,25},{17,1},{25,9},{2,18},{10... | collective-permute-start | bytes 393224 | tf_op jit(solution)/shard_map/ppermute | solution.py:41
  19.2 0.0 collective-permute-done.3.two
  19.2 1.0 %collective-permute-start.4 = (f32[32,1024]{1,0:T(8,128)S(1)}, f32[32,1024]{1,0:T(8,128)S(1)}, u32[]{:S(2)}, u32[]{:S(2)}) collective-permute-start(f32[32,1024]{1,0:T(8,128)S(1)} %sum.10), channel_id=1, source_target_pairs={{0,16},{8,24},{16,0},{24,8},{1,17},{9,25},{17,1},{25,9},{2,18},{10... | collective-permute-start | bytes 393224 | tf_op jit(solution)/shard_map/ppermute | solution.py:41
  20.3 2.7 %collective-permute-done.6 = f32[32,1024]{1,0:T(8,128)S(1)} collective-permute-done((f32[32,1024]{1,0:T(8,128)S(1)}, f32[32,1024]{1,0:T(8,128)S(1)}, u32[]{:S(2)}, u32[]{:S(2)}) %collective-permute-start.6) | collective-permute-done | bytes 131104 | tf_op jit(solution)/shard_map/ppermute | solution.py:41
  23.0 1.1 %collective-permute-start.7 = (f32[32,1024]{1,0:T(8,128)S(1)}, f32[32,1024]{1,0:T(8,128)S(1)}, u32[]{:S(2)}, u32[]{:S(2)}) collective-permute-start(f32[32,1024]{1,0:T(8,128)S(1)} %add.12.mine), channel_id=1, source_target_pairs={{0,8},{8,0},{16,24},{24,16},{1,9},{9,1},{17,25},{25,17},{2,10},{10... | collective-permute-start | bytes 393224 | tf_op jit(solution)/shard_map/ppermute | solution.py:41
  24.1 1.7 %collective-permute-done.4 = f32[32,1024]{1,0:T(8,128)S(1)} collective-permute-done((f32[32,1024]{1,0:T(8,128)S(1)}, f32[32,1024]{1,0:T(8,128)S(1)}, u32[]{:S(2)}, u32[]{:S(2)}) %collective-permute-start.4) | collective-permute-done | bytes 131104 | tf_op jit(solution)/shard_map/ppermute | solution.py:41
  25.8 0.8 collective-permute-start.5
  26.5 1.5 %collective-permute-start.1 = (f32[1,128,1024]{2,1,0:T(8,128)S(1)}, f32[1,128,1024]{2,1,0:T(8,128)S(1)}, u32[]{:S(2)}, u32[]{:S(2)}) collective-permute-start(f32[1,128,1024]{2,1,0:T(8,128)S(1)} %term.2.refs_0_.one), channel_id=1, source_target_pairs={{0,16},{8,24},{16,0},{24,8},{1,17},{9,25},{17,1},{25,9},{2,18},{10... | collective-permute-start | bytes 1572872 | tf_op jit(solution)/shard_map/ppermute | solution.py:41
  28.0 0.0 collective-permute-done.12.received
  28.0 0.0 copy-done
  28.0 0.0 copy-done.3
  28.0 0.2 term.3.one
  28.2 0.1 collective-permute-start.13
  28.3 0.0 collective-permute-done.7.other
  28.3 1.7 %right.2 = (f32[32,1152]{1,0:T(8,128)S(1)}, f32[32,1152]{1,0:T(8,128)S(1)}, f32[64,1024]{1,0:T(8,128)S(1)}) custom-call(s32[1]{0:T(128)} %bitcast.core, f32[32,1024]{1,0:T(8,128)S(1)} %add.12.mine, f32[32,1024]{1,0:T(8,128)S(1)} %collective-permute-done.7.other, f32[1024,1024]{1,0:T(8,128)S(1)} %get-tuple-element.36.corrected.refs_2_), custom_call_target="tpu_custom_call" | custom-call | tf_op jit(solution)/shard_map/right/pallas_call | solution.py:165
  30.0 0.0 collective-permute-done.5.other
  30.0 0.0 slice-start
  30.0 1.7 %right.3 = (f32[32,1152]{1,0:T(8,128)S(1)}, f32[32,1152]{1,0:T(8,128)S(1)}, f32[64,1024]{1,0:T(8,128)S(1)}) custom-call(s32[1]{0:T(128)} %bitcast.core, f32[32,1024]{1,0:T(8,128)S(1)} %add.11.mine.refs_0_, f32[32,1024]{1,0:T(8,128)S(1)} %collective-permute-done.5.other, f32[1024,1024]{1,0:T(8,128)S(1)} %get-tuple-element.35.corrected.refs_3_, ...), custom_call_target="tpu_custom_call" | custom-call | tf_op jit(solution)/shard_map/right/pallas_call | solution.py:165
  31.7 0.6 collective-permute-start.8
  32.4 1.0 %collective-permute-done.8.two = f32[32,1152]{1,0:T(8,128)S(1)} collective-permute-done((f32[32,1152]{1,0:T(8,128)S(1)}, f32[32,1152]{1,0:T(8,128)S(1)}, u32[]{:S(2)}, u32[]{:S(2)}) %collective-permute-start.8) | collective-permute-done | bytes 147488 | tf_op jit(solution)/shard_map/ppermute | solution.py:41
  33.4 1.6 %collective-permute-start.9 = (f32[32,1152]{1,0:T(8,128)S(1)}, f32[32,1152]{1,0:T(8,128)S(1)}, u32[]{:S(2)}, u32[]{:S(2)}) collective-permute-start(f32[32,1152]{1,0:T(8,128)S(1)} %sum.11.one), channel_id=1, source_target_pairs={{0,1},{1,0},{2,3},{3,2},{4,5},{5,4},{6,7},{7,6},{8,9},{9,8},{10,11... | collective-permute-start | bytes 442376 | tf_op jit(solution)/shard_map/ppermute | solution.py:41
  34.9 3.6 %collective-permute-done.9.two = f32[32,1152]{1,0:T(8,128)S(1)} collective-permute-done((f32[32,1152]{1,0:T(8,128)S(1)}, f32[32,1152]{1,0:T(8,128)S(1)}, u32[]{:S(2)}, u32[]{:S(2)}) %collective-permute-start.9) | collective-permute-done | bytes 147488 | tf_op jit(solution)/shard_map/ppermute | solution.py:41
  38.6 1.5 %collective-permute-start.10 = (f32[32,1152]{1,0:T(8,128)S(1)}, f32[32,1152]{1,0:T(8,128)S(1)}, u32[]{:S(2)}, u32[]{:S(2)}) collective-permute-start(f32[32,1152]{1,0:T(8,128)S(1)} %sum.12.one), channel_id=1, source_target_pairs={{0,2},{1,3},{2,0},{3,1},{4,6},{5,7},{6,4},{7,5},{8,10},{9,11},{10,... | collective-permute-start | bytes 442376 | tf_op jit(solution)/shard_map/ppermute | solution.py:41
  40.2 2.8 %collective-permute-done.10.two = f32[32,1152]{1,0:T(8,128)S(1)} collective-permute-done((f32[32,1152]{1,0:T(8,128)S(1)}, f32[32,1152]{1,0:T(8,128)S(1)}, u32[]{:S(2)}, u32[]{:S(2)}) %collective-permute-start.10) | collective-permute-done | bytes 147488 | tf_op jit(solution)/shard_map/ppermute | solution.py:41
  43.0 0.0 collective-permute-done.1.two
  43.0 0.1 sum.14.mine
  43.1 0.0 slice-start.1
  43.1 2.1 %collective-permute-start.11 = (f32[1,128,1024]{2,1,0:T(8,128)S(1)}, f32[1,128,1024]{2,1,0:T(8,128)S(1)}, u32[]{:S(2)}, u32[]{:S(2)}) collective-permute-start(f32[1,128,1024]{2,1,0:T(8,128)S(1)} %sum.14.mine), channel_id=1, source_target_pairs={{0,8},{8,0},{16,24},{24,16},{1,9},{9,1},{17,25},{25,17},{2,10},{10... | collective-permute-start | bytes 1572872 | tf_op jit(solution)/shard_map/ppermute | solution.py:41
  45.1 2.5 %collective-permute-start.14 = (f32[32,1152]{1,0:T(8,128)S(1)}, f32[32,1152]{1,0:T(8,128)S(1)}, u32[]{:S(2)}, u32[]{:S(2)}) collective-permute-start(f32[32,1152]{1,0:T(8,128)S(1)} %sum.13.refs_0_.one), channel_id=1, source_target_pairs={{0,4},{1,5},{2,6},{3,7},{4,0},{5,1},{6,2},{7,3},{8,12},{9,13},{10,... | collective-permute-start | bytes 442376 | tf_op jit(solution)/shard_map/ppermute | solution.py:41
  47.7 0.0 collective-permute-done.11.other
  47.7 0.0 copy-done.5
  47.7 1.6 %layer.2 = (f32[2,128,1024]{2,1,0:T(8,128)}, f32[2,128,1024]{2,1,0:T(8,128)}) custom-call(s32[1]{0:T(128)} %bitcast.core, f32[1,128,1024]{2,1,0:T(8,128)S(1)} %sum.14.mine, f32[1,128,1024]{2,1,0:T(8,128)S(1)} %collective-permute-done.11.other, f32[2,128,1024]{2,1,0:T(8,128)S(1)} %copy-done.1, f32[2,128,1024]{2,1,0:T(8,128)S(1)} %copy-done.5), custom_call_target="tpu_custom_call" | custom-call | tf_op jit(solution)/shard_map/layer/pallas_call | solution.py:310
  49.3 5.6 %collective-permute-done.14.two = f32[32,1152]{1,0:T(8,128)S(1)} collective-permute-done((f32[32,1152]{1,0:T(8,128)S(1)}, f32[32,1152]{1,0:T(8,128)S(1)}, u32[]{:S(2)}, u32[]{:S(2)}) %collective-permute-start.14) | collective-permute-done | bytes 147488 | tf_op jit(solution)/shard_map/ppermute | solution.py:41
  55.0 1.2 %copy-done.6 = f32[2,128,1024]{2,1,0:T(8,128)S(1)} copy-done((f32[2,128,1024]{2,1,0:T(8,128)S(1)}, f32[2,128,1024]{2,1,0:T(8,128)}, u32[]{:S(2)}) %copy-start.6) | copy-done | bytes 1048600
  56.2 6.4 %factor.1 = (f32[64,64]{1,0:T(8,128)S(1)}, bf16[1024,384]{1,0:T(8,128)(2,1)S(1)}, bf16[1024,384]{1,0:T(8,128)(2,1)S(1)}) custom-call(f32[32,1152]{1,0:T(8,128)S(1)} %sum.15.message.one, f32[64,1024]{1,0:T(8,128)S(1)} %get-tuple-element.43.refs_0_, f32[64,1024]{1,0:T(8,128)S(1)} %get-tuple-element.44.refs_1_), custom_call_target="tpu_custom_call" | custom-call | tf_op jit(solution)/shard_map/factor/pallas_call | solution.py:210
  62.7 0.0 collective-permute-done.13.two
  62.7 0.1 sum.16.mine
  62.8 0.8 collective-permute-start.15
  63.5 1.5 %collective-permute-start.16 = (f32[32,1152]{1,0:T(8,128)S(1)}, f32[32,1152]{1,0:T(8,128)S(1)}, u32[]{:S(2)}, u32[]{:S(2)}) collective-permute-start(f32[32,1152]{1,0:T(8,128)S(1)} %sum.15.message.one), channel_id=1, source_target_pairs={{0,16},{8,24},{16,0},{24,8},{1,17},{9,25},{17,1},{25,9},{2,18},{10... | collective-permute-start | bytes 442376 | tf_op jit(solution)/shard_map/ppermute | solution.py:41
  65.0 3.9 %collective-permute-done.16.two = f32[32,1152]{1,0:T(8,128)S(1)} collective-permute-done((f32[32,1152]{1,0:T(8,128)S(1)}, f32[32,1152]{1,0:T(8,128)S(1)}, u32[]{:S(2)}, u32[]{:S(2)}) %collective-permute-start.16) | collective-permute-done | bytes 147488 | tf_op jit(solution)/shard_map/ppermute | solution.py:41
  69.0 0.9 %collective-permute-start.17 = (f32[32,1152]{1,0:T(8,128)S(1)}, f32[32,1152]{1,0:T(8,128)S(1)}, u32[]{:S(2)}, u32[]{:S(2)}) collective-permute-start(f32[32,1152]{1,0:T(8,128)S(1)} %sum.17.refs_0_.mine), channel_id=1, source_target_pairs={{0,8},{8,0},{16,24},{24,16},{1,9},{9,1},{17,25},{25,17},{2,10},{10... | collective-permute-start | bytes 442376 | tf_op jit(solution)/shard_map/ppermute | solution.py:41
  69.9 1.0 %collective-permute-done.17.other = f32[32,1152]{1,0:T(8,128)S(1)} collective-permute-done((f32[32,1152]{1,0:T(8,128)S(1)}, f32[32,1152]{1,0:T(8,128)S(1)}, u32[]{:S(2)}, u32[]{:S(2)}) %collective-permute-start.17) | collective-permute-done | bytes 147488 | tf_op jit(solution)/shard_map/ppermute | solution.py:41
  70.9 0.0 slice-done
  70.9 0.0 slice-done.1
  70.9 10.2 %final.1 = (f32[2048,1024]{1,0:T(8,128)}, f32[2048,1024]{1,0:T(8,128)}, f32[1,2048,1024]{2,1,0:T(8,128)}) custom-call(s32[1]{0:T(128)} %bitcast.core, f32[32,1152]{1,0:T(8,128)S(1)} %sum.17.refs_0_.mine, f32[32,1152]{1,0:T(8,128)S(1)} %collective-permute-done.17.other, f32[64,64]{1,0:T(8,128)S(1)} %get-tuple-element.45.refs_0_.inverse, ...), custom_call_target="tpu_custom_call" | custom-call | tf_op jit(solution)/shard_map/final/pallas_call | solution.py:256
  81.1 0.0 collective-permute-done.15.other
  81.1 0.0 copy-done.2
  81.1 2.6 %layer.3 = (f32[2,128,2048]{2,1,0:T(8,128)}, f32[2,128,2048]{2,1,0:T(8,128)}) custom-call(s32[1]{0:T(128)} %bitcast.core, f32[1,128,2048]{2,1,0:T(8,128)S(1)} %sum.16.mine, f32[1,128,2048]{2,1,0:T(8,128)S(1)} %collective-permute-done.15.other, f32[2,128,2048]{2,1,0:T(8,128)S(1)} %copy-done, f32[2,128,2048]{2,1,0:T(8,128)S(1)} %copy-done.2, ...), custom_call_target="tpu_custom_call" | custom-call | tf_op jit(solution)/shard_map/layer/pallas_call | solution.py:310
  (14 shorter events, 0.2 us)
Async XLA Ops:
  0.6 27.4 %collective-permute-start.12 = (f32[1,2,128,2048]{3,2,1,0:T(8,128)}, f32[1,2,128,2048]{3,2,1,0:T(8,128)S(1)}, u32[]{:S(2)}, u32[]{:S(2)}) collective-permute-start(f32[1,2,128,2048]{3,2,1,0:T(8,128)} %copies.7), channel_id=1, source_target_pairs={{0,8},{8,0},{16,24},{24,16},{1,9},{9,1},{17,25},{25,17},{2,10},{10... | collective-permute-start | bytes 6291464 | tf_op jit(solution)/shard_map/ppermute | solution.py:41
  0.8 9.2 %collective-permute-start = (f32[1,2,128,1024]{3,2,1,0:T(8,128)}, f32[1,2,128,1024]{3,2,1,0:T(8,128)S(1)}, u32[]{:S(2)}, u32[]{:S(2)}) collective-permute-start(f32[1,2,128,1024]{3,2,1,0:T(8,128)} %copies.5), channel_id=1, source_target_pairs={{0,8},{8,0},{16,24},{24,16},{1,9},{9,1},{17,25},{25,17},{2,10},{10... | collective-permute-start | bytes 3145736 | tf_op jit(solution)/shard_map/ppermute | solution.py:41
  1.2 0.9 %copy-start.4 = (f32[64,1024]{1,0:T(8,128)S(1)}, f32[64,1024]{1,0:T(8,128)}, u32[]{:S(2)}) copy-start(f32[64,1024]{1,0:T(8,128)} %warm.3) | copy-start | bytes 786436
  2.2 7.8 %copy-start.1 = (f32[2,128,1024]{2,1,0:T(8,128)S(1)}, f32[2,128,1024]{2,1,0:T(8,128)}, u32[]{:S(2)}) copy-start(f32[2,128,1024]{2,1,0:T(8,128)} %weights.9) | copy-start | bytes 3145732
  2.2 7.8 %copy-start.7 = (f32[1,2,128,1024]{3,2,1,0:T(8,128)S(1)}, f32[1,2,128,1024]{3,2,1,0:T(8,128)}, u32[]{:S(2)}) copy-start(f32[1,2,128,1024]{3,2,1,0:T(8,128)} %copies.5) | copy-start | bytes 3145732
  8.5 1.4 %collective-permute-start.2 = (f32[32,1024]{1,0:T(8,128)S(1)}, f32[32,1024]{1,0:T(8,128)S(1)}, u32[]{:S(2)}, u32[]{:S(2)}) collective-permute-start(f32[32,1024]{1,0:T(8,128)S(1)} %get-tuple-element.31.refs_0_), channel_id=1, source_target_pairs={{0,8},{8,0},{16,24},{24,16},{1,9},{9,1},{17,25},{25,17},{2,10},{10... | collective-permute-start | bytes 393224 | tf_op jit(solution)/shard_map/ppermute | solution.py:41
  10.0 18.0 %copy-start = (f32[2,128,2048]{2,1,0:T(8,128)S(1)}, f32[2,128,2048]{2,1,0:T(8,128)}, u32[]{:S(2)}) copy-start(f32[2,128,2048]{2,1,0:T(8,128)} %weights.11) | copy-start | bytes 6291460
  10.1 18.0 %copy-start.3 = (f32[1,2,128,2048]{3,2,1,0:T(8,128)S(1)}, f32[1,2,128,2048]{3,2,1,0:T(8,128)}, u32[]{:S(2)}) copy-start(f32[1,2,128,2048]{3,2,1,0:T(8,128)} %copies.7) | copy-start | bytes 6291460
  16.4 2.8 %collective-permute-start.3 = (f32[32,1024]{1,0:T(8,128)S(1)}, f32[32,1024]{1,0:T(8,128)S(1)}, u32[]{:S(2)}, u32[]{:S(2)}) collective-permute-start(f32[32,1024]{1,0:T(8,128)S(1)} %get-tuple-element.34), channel_id=1, source_target_pairs={{0,8},{8,0},{16,24},{24,16},{1,9},{9,1},{17,25},{25,17},{2,10},{10... | collective-permute-start | bytes 393224 | tf_op jit(solution)/shard_map/ppermute | solution.py:41
  16.6 6.3 %collective-permute-start.6 = (f32[32,1024]{1,0:T(8,128)S(1)}, f32[32,1024]{1,0:T(8,128)S(1)}, u32[]{:S(2)}, u32[]{:S(2)}) collective-permute-start(f32[32,1024]{1,0:T(8,128)S(1)} %sum.9.refs_1_), channel_id=1, source_target_pairs={{0,16},{8,24},{16,0},{24,8},{1,17},{9,25},{17,1},{25,9},{2,18},{10... | collective-permute-start | bytes 393224 | tf_op jit(solution)/shard_map/ppermute | solution.py:41
  19.2 6.5 %collective-permute-start.4 = (f32[32,1024]{1,0:T(8,128)S(1)}, f32[32,1024]{1,0:T(8,128)S(1)}, u32[]{:S(2)}, u32[]{:S(2)}) collective-permute-start(f32[32,1024]{1,0:T(8,128)S(1)} %sum.10), channel_id=1, source_target_pairs={{0,16},{8,24},{16,0},{24,8},{1,17},{9,25},{17,1},{25,9},{2,18},{10... | collective-permute-start | bytes 393224 | tf_op jit(solution)/shard_map/ppermute | solution.py:41
  23.0 5.3 %collective-permute-start.7 = (f32[32,1024]{1,0:T(8,128)S(1)}, f32[32,1024]{1,0:T(8,128)S(1)}, u32[]{:S(2)}, u32[]{:S(2)}) collective-permute-start(f32[32,1024]{1,0:T(8,128)S(1)} %add.12.mine), channel_id=1, source_target_pairs={{0,8},{8,0},{16,24},{24,16},{1,9},{9,1},{17,25},{25,17},{2,10},{10... | collective-permute-start | bytes 393224 | tf_op jit(solution)/shard_map/ppermute | solution.py:41
  25.8 4.2 %collective-permute-start.5 = (f32[32,1024]{1,0:T(8,128)S(1)}, f32[32,1024]{1,0:T(8,128)S(1)}, u32[]{:S(2)}, u32[]{:S(2)}) collective-permute-start(f32[32,1024]{1,0:T(8,128)S(1)} %add.11.mine.refs_0_), channel_id=1, source_target_pairs={{0,8},{8,0},{16,24},{24,16},{1,9},{9,1},{17,25},{25,17},{2,10},{10... | collective-permute-start | bytes 393224 | tf_op jit(solution)/shard_map/ppermute | solution.py:41
  26.5 16.5 %collective-permute-start.1 = (f32[1,128,1024]{2,1,0:T(8,128)S(1)}, f32[1,128,1024]{2,1,0:T(8,128)S(1)}, u32[]{:S(2)}, u32[]{:S(2)}) collective-permute-start(f32[1,128,1024]{2,1,0:T(8,128)S(1)} %term.2.refs_0_.one), channel_id=1, source_target_pairs={{0,16},{8,24},{16,0},{24,8},{1,17},{9,25},{17,1},{25,9},{2,18},{10... | collective-permute-start | bytes 1572872 | tf_op jit(solution)/shard_map/ppermute | solution.py:41
  28.2 34.5 %collective-permute-start.13 = (f32[1,128,2048]{2,1,0:T(8,128)S(1)}, f32[1,128,2048]{2,1,0:T(8,128)S(1)}, u32[]{:S(2)}, u32[]{:S(2)}) collective-permute-start(f32[1,128,2048]{2,1,0:T(8,128)S(1)} %term.3.one), channel_id=1, source_target_pairs={{0,16},{8,24},{16,0},{24,8},{1,17},{9,25},{17,1},{25,9},{2,18},{10... | collective-permute-start | bytes 3145736 | tf_op jit(solution)/shard_map/ppermute | solution.py:41
  30.0 17.7 %copy-start.5 = (f32[2,128,1024]{2,1,0:T(8,128)S(1)}, f32[2,128,1024]{2,1,0:T(8,128)}, u32[]{:S(2)}) copy-start(f32[2,128,1024]{2,1,0:T(8,128)} %moment.3) | copy-start | bytes 3145732
  30.0 40.9 %slice-start = ((s8[8388608]{0:T(1024)(128)(4,1)}), s8[4194304]{0:T(1024)(128)(4,1)S(1)}, s32[]{:S(2)}) async-start(s8[8388608]{0:T(1024)(128)(4,1)} %bitcast.1), calls=%async_computation | async-start | bytes 8388608
  31.7 1.6 %collective-permute-start.8 = (f32[32,1152]{1,0:T(8,128)S(1)}, f32[32,1152]{1,0:T(8,128)S(1)}, u32[]{:S(2)}, u32[]{:S(2)}) collective-permute-start(f32[32,1152]{1,0:T(8,128)S(1)} %get-tuple-element.40), channel_id=1, source_target_pairs={{0,8},{8,0},{16,24},{24,16},{1,9},{9,1},{17,25},{25,17},{2,10},{10... | collective-permute-start | bytes 442376 | tf_op jit(solution)/shard_map/ppermute | solution.py:41
  33.4 5.2 %collective-permute-start.9 = (f32[32,1152]{1,0:T(8,128)S(1)}, f32[32,1152]{1,0:T(8,128)S(1)}, u32[]{:S(2)}, u32[]{:S(2)}) collective-permute-start(f32[32,1152]{1,0:T(8,128)S(1)} %sum.11.one), channel_id=1, source_target_pairs={{0,1},{1,0},{2,3},{3,2},{4,5},{5,4},{6,7},{7,6},{8,9},{9,8},{10,11... | collective-permute-start | bytes 442376 | tf_op jit(solution)/shard_map/ppermute | solution.py:41
  38.6 4.4 %collective-permute-start.10 = (f32[32,1152]{1,0:T(8,128)S(1)}, f32[32,1152]{1,0:T(8,128)S(1)}, u32[]{:S(2)}, u32[]{:S(2)}) collective-permute-start(f32[32,1152]{1,0:T(8,128)S(1)} %sum.12.one), channel_id=1, source_target_pairs={{0,2},{1,3},{2,0},{3,1},{4,6},{5,7},{6,4},{7,5},{8,10},{9,11},{10,... | collective-permute-start | bytes 442376 | tf_op jit(solution)/shard_map/ppermute | solution.py:41
  43.1 27.9 %slice-start.1 = ((s8[8388608]{0:T(1024)(128)(4,1)}), s8[4194304]{0:T(1024)(128)(4,1)S(1)}, s32[]{:S(2)}) async-start(s8[8388608]{0:T(1024)(128)(4,1)} %bitcast.1), calls=%async_computation.1 | async-start | bytes 8388608
  43.1 4.6 %collective-permute-start.11 = (f32[1,128,1024]{2,1,0:T(8,128)S(1)}, f32[1,128,1024]{2,1,0:T(8,128)S(1)}, u32[]{:S(2)}, u32[]{:S(2)}) collective-permute-start(f32[1,128,1024]{2,1,0:T(8,128)S(1)} %sum.14.mine), channel_id=1, source_target_pairs={{0,8},{8,0},{16,24},{24,16},{1,9},{9,1},{17,25},{25,17},{2,10},{10... | collective-permute-start | bytes 1572872 | tf_op jit(solution)/shard_map/ppermute | solution.py:41
  45.1 9.8 %collective-permute-start.14 = (f32[32,1152]{1,0:T(8,128)S(1)}, f32[32,1152]{1,0:T(8,128)S(1)}, u32[]{:S(2)}, u32[]{:S(2)}) collective-permute-start(f32[32,1152]{1,0:T(8,128)S(1)} %sum.13.refs_0_.one), channel_id=1, source_target_pairs={{0,4},{1,5},{2,6},{3,7},{4,0},{5,1},{6,2},{7,3},{8,12},{9,13},{10,... | collective-permute-start | bytes 442376 | tf_op jit(solution)/shard_map/ppermute | solution.py:41
  55.0 1.2 %copy-start.6 = (f32[2,128,1024]{2,1,0:T(8,128)S(1)}, f32[2,128,1024]{2,1,0:T(8,128)}, u32[]{:S(2)}) copy-start(f32[2,128,1024]{2,1,0:T(8,128)} %get-tuple-element.25.refs_0_) | copy-start | bytes 3145732
  62.8 18.3 %collective-permute-start.15 = (f32[1,128,2048]{2,1,0:T(8,128)S(1)}, f32[1,128,2048]{2,1,0:T(8,128)S(1)}, u32[]{:S(2)}, u32[]{:S(2)}) collective-permute-start(f32[1,128,2048]{2,1,0:T(8,128)S(1)} %sum.16.mine), channel_id=1, source_target_pairs={{0,8},{8,0},{16,24},{24,16},{1,9},{9,1},{17,25},{25,17},{2,10},{10... | collective-permute-start | bytes 3145736 | tf_op jit(solution)/shard_map/ppermute | solution.py:41
  63.5 5.4 %collective-permute-start.16 = (f32[32,1152]{1,0:T(8,128)S(1)}, f32[32,1152]{1,0:T(8,128)S(1)}, u32[]{:S(2)}, u32[]{:S(2)}) collective-permute-start(f32[32,1152]{1,0:T(8,128)S(1)} %sum.15.message.one), channel_id=1, source_target_pairs={{0,16},{8,24},{16,0},{24,8},{1,17},{9,25},{17,1},{25,9},{2,18},{10... | collective-permute-start | bytes 442376 | tf_op jit(solution)/shard_map/ppermute | solution.py:41
  69.0 1.9 %collective-permute-start.17 = (f32[32,1152]{1,0:T(8,128)S(1)}, f32[32,1152]{1,0:T(8,128)S(1)}, u32[]{:S(2)}, u32[]{:S(2)}) collective-permute-start(f32[32,1152]{1,0:T(8,128)S(1)} %sum.17.refs_0_.mine), channel_id=1, source_target_pairs={{0,8},{8,0},{16,24},{24,16},{1,9},{9,1},{17,25},{25,17},{2,10},{10... | collective-permute-start | bytes 442376 | tf_op jit(solution)/shard_map/ppermute | solution.py:41
  70.9 10.2 %copy-start.2 = (f32[2,128,2048]{2,1,0:T(8,128)S(1)}, f32[2,128,2048]{2,1,0:T(8,128)}, u32[]{:S(2)}) copy-start(f32[2,128,2048]{2,1,0:T(8,128)} %moment.4) | copy-start | bytes 6291460

commit v3 on v2

--- a/solution.py
+++ b/solution.py
@@ -109,7 +109,7 @@
             pl.BlockSpec((block, width), row),
             pl.BlockSpec((1, block, width), lead),
             pl.BlockSpec((1, block, width), lead),
-            VMEM,
+            pl.BlockSpec((rank, width), lambda i: (0, 0)),
         ]
         + [ANY] * len(after),
         out_specs=[
@@ -127,7 +127,7 @@
         scratch_shapes=[pltpu.VMEM((3 * rank, width), jnp.bfloat16)],
         compiler_params=pltpu.CompilerParams(vmem_limit_bytes=26 * MIB),
         name="left",
-    )(core, in_hbm(weights), in_hbm(copies), in_hbm(error), warm, *after)
+    )(core, in_hbm(weights), in_hbm(copies), in_hbm(error), in_hbm(warm), *after)
 
 
 def right_kernel(scale, block, core, mine, other, corrected, *refs):
@@ -184,14 +184,35 @@
     )
     both = jnp.concatenate([gram, eye], axis=1)
     bands = [both[i : i + 8, :] for i in range(0, rank, 8)]
-    for j in range(rank):
+    group = 4
+    for j in range(0, rank, group):
         band, line = divmod(j, 8)
-        row = bands[band][line : line + 1, :]
-        root = lax.rsqrt(row[:, j : j + 1])
-        row = row * root
-        inverse[j : j + 1, :] = row[:, rank:]
+        columns = [
+            [jnp.broadcast_to(rest[:, j + k : j + k + 1], rest.shape) for k in range(group)] for rest in bands[band:]
+        ]
+        rows = [bands[band][line + k : line + k + 1, :] for k in range(group)]
+        corner = [[columns[0][m][line + k : line + k + 1, :] for m in range(group)] for k in range(group)]
+        roots, factors = [], []
+        for k in range(group):
+            root = lax.rsqrt(corner[k][k])
+            rows[k] = rows[k] * root
+            inverse[j + k : j + k + 1, :] = rows[k][:, rank:]
+            factor = {m: corner[m][k] * root for m in range(k + 1, group)}
+            for m in range(k + 1, group):
+                rows[m] = rows[m] - factor[m] * rows[k]
+                for n in range(k + 1, m + 1):
+                    corner[m][n] = corner[m][n] - factor[m] * factor[n]
+            roots.append(root)
+            factors.append(factor)
+        for k in reversed(range(group)):
+            for m in range(k + 1, group):
+                rows[k] = rows[k] - factors[k][m] * rows[m]
+            rows[k] = rows[k] * roots[k]
         for i in range(band, rank // 8):
-            bands[i] = bands[i] - (bands[i][:, j : j + 1] * root) * row
+            column = columns[i - band]
+            bands[i] = bands[i] - (
+                (column[0] * rows[0] + column[1] * rows[1]) + (column[2] * rows[2] + column[3] * rows[3])
+            )
     for chunk in range(chunks):
         rows = lax.dot_general(
             inverse[...],
@@ -220,7 +241,7 @@
 
 def final_kernel(scale, chunks, core, mine, other, inverse, moment, *refs):
     weights, corrected, basis = refs[:chunks], refs[chunks : 2 * chunks], refs[2 * chunks : 3 * chunks]
-    updated, velocity, carried, parts = refs[3 * chunks :]
+    updated, velocity, carried, parts = refs[-4:]
     step = pl.program_id(0)
     rows, width = updated.shape
     here = pl.ds(pl.multiple_of(step * rows, rows), rows)
@@ -242,12 +263,15 @@
         updated[...] = new
         velocity[...] = speed
 
-    per = corrected[0].shape[0] // rows
+    first = 0
     for chunk in range(chunks):
-        pl.when(step // per == chunk)(functools.partial(work, chunk, (step - chunk * per) * rows))
-
-
-def final_call(core, mine, other, inverse, moment, weights, corrected, basis, scale, block):
+        count = corrected[chunk].shape[0] // rows
+        here_now = jnp.logical_and(step >= first, step < first + count)
+        pl.when(here_now)(functools.partial(work, chunk, (step - first) * rows))
+        first += count
+
+
+def final_call(core, mine, other, inverse, moment, weights, corrected, basis, after, scale, block):
     rows, width = moment.shape
     rank = inverse.shape[0]
     chunks = len(corrected)
@@ -256,7 +280,7 @@
     return pl.pallas_call(
         functools.partial(final_kernel, scale, chunks),
         grid=(rows // block,),
-        in_specs=[SMEM] + [VMEM] * (3 + len(large)),
+        in_specs=[SMEM] + [VMEM] * (3 + len(large)) + [ANY] * len(after),
         out_specs=[out, out, pl.BlockSpec((1, block, width), lambda i: (0, i, 0))],
         out_shape=[
             jax.ShapeDtypeStruct((rows, width), jnp.float32),
@@ -266,7 +290,7 @@
         scratch_shapes=[pltpu.VMEM((6 * rank, width), jnp.bfloat16)],
         compiler_params=pltpu.CompilerParams(vmem_limit_bytes=16 * MIB),
         name="final",
-    )(core, mine, other, inverse, *large)
+    )(core, mine, other, inverse, *large, *after)
 
 
 def sum_kernel(one, two, *refs):
@@ -284,34 +308,45 @@
     )(one, two, *after)
 
 
+def away_kernel(core, weights, copies, *refs):
+    at = 1 - core[0]
+    refs[-1][...] = weights[at] - copies[0, at]
+
+
 def term_kernel(core, weights, copies, received, *refs):
     at = core[0]
-    refs[-1][0] = (weights[at] - copies[0, at]) + (weights[at] - received[0, at])
-
-
-def term_call(core, weights, copies, received, after):
-    return pl.pallas_call(
-        term_kernel,
-        in_specs=[SMEM] + [VMEM] * 3 + [ANY] * len(after),
+    refs[-1][...] = (weights[at] - copies[0, at]) + received[...]
+
+
+def both_kernel(core, weights, copies, received, *refs):
+    at = core[0]
+    refs[-1][...] = (weights[at] - copies[0, at]) + (weights[at] - received[0, at])
+
+
+def difference_call(kernel, core, operands, after):
+    return pl.pallas_call(
+        kernel,
+        in_specs=[SMEM] + [VMEM] * len(operands) + [ANY] * len(after),
         out_specs=VMEM,
-        out_shape=jax.ShapeDtypeStruct((1, *weights.shape[1:]), jnp.float32),
+        out_shape=jax.ShapeDtypeStruct(operands[0].shape[1:], jnp.float32),
         compiler_params=pltpu.CompilerParams(vmem_limit_bytes=12 * MIB),
-        name="term",
-    )(core, weights, copies, received, *after)
+        name=kernel.__name__[:-7],
+    )(core, *operands, *after)
 
 
 def layer_kernel(scale, core, mine, other, weights, moment, *refs):
-    updated, velocity = refs[-2:]
+    updated, velocity, mark = refs[-3:]
     for value, at in ((mine, core[0]), (other, 1 - core[0])):
-        updated[at], velocity[at] = nesterov(weights[at], value[0] * scale, moment[at])
+        updated[at], velocity[at] = nesterov(weights[at], value[...] * scale, moment[at])
+    mark[...] = jnp.zeros_like(mark)
 
 
 def layer_call(core, mine, other, weights, moment, after, scale):
     return pl.pallas_call(
         functools.partial(layer_kernel, scale),
         in_specs=[SMEM] + [VMEM] * 4 + [ANY] * len(after),
-        out_specs=[VMEM] * 2,
-        out_shape=[jax.ShapeDtypeStruct(weights.shape, jnp.float32)] * 2,
+        out_specs=[VMEM] * 3,
+        out_shape=[jax.ShapeDtypeStruct(weights.shape, jnp.float32)] * 2 + [jax.ShapeDtypeStruct((8, 128), jnp.float32)],
         compiler_params=pltpu.CompilerParams(vmem_limit_bytes=16 * MIB),
         name="layer",
     )(core, mine, other, weights, moment, *after)
@@ -334,59 +369,66 @@
     scale = 1 / replicas
     rank, width = warm_start.shape
     rows = embed_weights.shape[0]
-    chunks = 2 if rows % 512 == 0 else 1
-    size = rows // chunks
-    block = math.gcd(size, 256)
-    wide = math.gcd(size, 512)
+    sizes = (rows // 4, rows - rows // 4) if rows % 2048 == 0 else (rows,)
+    chunks = len(sizes)
     core = jnp.reshape(lax.axis_index("replica") % 2, (1,)).astype(jnp.int32)
 
     square_received = swap(square_copies, "replica", 1)
-    broad_received = swap(broad_copies, "replica", 1)
-    corrected, held, halves, after = [], [], [], ()
-    for chunk in range(chunks):
+    corrected, held, left, after, before = [], [], [], (), ()
+    start, exchanged = 0, []
+    for chunk, size in enumerate(sizes):
         value, weights, away, kept = left_call(
-            core, embed_weights, embed_copies, embed_error, warm_start, after, chunk * size, size, wide
+            core, embed_weights, embed_copies, embed_error, warm_start, after, start, size, math.gcd(size, 256 << chunk)
         )
+        start += size
         corrected.append(value)
         held.append(weights)
-        halves.append(sum_call(kept, swap(away, "replica", 1), ()))
+        half = sum_call(kept, swap(away, "replica", 1), exchanged)
         if chunk == 0:
-            square_half = term_call(core, square_weights, square_copies, square_received, (away,))
-            after = (square_half, halves[0])
-    left, before = [], ()
-    for chunk in range(chunks):
-        half = doubled(halves[chunk], "replica", 2)
+            square_half = difference_call(
+                both_kernel, core, (square_weights, square_copies, square_received), (away,)
+            )
+            after = (half, square_half)
+            square_half_first = square_half
+            square_half = sum_over_chips(square_half, ())
+            exchanged.append(square_half)
+            broad_away = difference_call(away_kernel, core, (broad_weights, broad_copies), (square_half_first,))
+            broad_received = swap(broad_away, "replica", 1)
+        half = sum_over_chips(half, ())
+        exchanged.append(half)
         other = swap(half, "replica", 1)
-        *before, piece = right_call(core, half, other, corrected[chunk], before, scale, block)
-        left.append(piece)
+        left.append((half, other))
+    broad_half = difference_call(term_kernel, core, (broad_weights, broad_copies, broad_received), (half,))
+    for chunk, size in enumerate(sizes):
+        *before, left[chunk] = right_call(
+            core, *left[chunk], corrected[chunk], before, scale, math.gcd(size, 256)
+        )
     away, kept = before
-    broad_half = term_call(core, broad_weights, broad_copies, broad_received, (half,))
 
     message = sum_call(kept, swap(away, "replica", 1), ())
     inner = lax.axis_size("inner")
     bit = 1
+    square_other = swap(square_half, "replica", 1)
     while bit < inner:
         received = swap(message, "inner", bit)
         after = ()
         if 2 * bit >= inner:
-            square_half = sum_over_chips(square_half, (message,))
-            square_other = swap(square_half, "replica", 1)
-            square_updated, square_velocity = layer_call(
-                core, square_half, square_other, square_weights, square_moment, (), scale
+            square_updated, square_velocity, mark = layer_call(
+                core, square_half, square_other, square_weights, square_moment, (message,), scale
             )
-            after = (square_velocity,)
+            after = (mark,)
         message = sum_call(message, received, after)
         bit *= 2
     inverse, *basis = factor_call(message, left, width)
     right_half = sum_over_chips(message, (inverse,))
-    broad_half = sum_over_chips(broad_half, (inverse,))
+    broad_half = sum_over_chips(broad_half, (message,))
     broad_other = swap(broad_half, "replica", 1)
-    broad_updated, broad_velocity = layer_call(
+    broad_updated, broad_velocity, mark = layer_call(
         core, broad_half, broad_other, broad_weights, broad_moment, (right_half,), scale
     )
     right_other = swap(right_half, "replica", 1)
     embed_updated, embed_velocity, embed_carried = final_call(
-        core, right_half, right_other, inverse, embed_moment, held, corrected, basis, scale, block
+        core, right_half, right_other, inverse, embed_moment, held, corrected, basis, (mark,), scale, math.gcd(rows, 256)
     )
     return (
         square_updated,

time: 84.2 us -> 77.7 us (0.923)
  starting transfers between devices: 19.5 us -> 17.2 us
  Pallas kernels: 37.5 us -> 35.7 us
  local copies, waits for them, and re-layouts: 2.22 us -> 0.75 us
    pallas_call x1, Pallas kernels: 6.45 us -> 3.78 us  [factor_call(): pl.pallas_call(functools.partial(factor_kernel, width), in_specs=[VMEM] *...]
    ppermute x18, starting transfers between devices: 19.5 us -> 17.2 us  [swap(): lax.ppermute(value, axis, [(i, i ^ bit) for i in range(lax.axis_size(axis...]
    unnamed x20 -> x16, local copies, waits for them, and re-layouts: 2.22 us -> 0.75 us
  transfers between devices with their start and end apart: 18 -> 18, of which waited for: 9 -> 9; matrix products, arithmetic and copies ran while one was open for 0% -> 0% of each run, Pallas kernels for 42% -> 32%
where the time goes in v3:
time: 77.7 us; the launch traced here: 77.6 us
  Pallas kernels  35.7 us (46%)
  waiting for transfers between devices  23.1 us (30%)
  starting transfers between devices  17.2 us (22%)
  between operations  0.84 us (1%)
    ppermute x18, waiting for transfers between devices, swap(): lax.ppermute(value, axis, [(i, i ^ bit) for i in range(lax.axis_size(axis...  23.1 us
    ppermute x18, starting transfers between devices, swap(): lax.ppermute(value, axis, [(i, i ^ bit) for i in range(lax.axis_size(axis...  17.2 us
    pallas_call x2, Pallas kernels, left_call(): pl.pallas_call(functools.partial(left_kernel, len(after)), grid=(rows //...  13.4 us
    pallas_call x1, Pallas kernels, final_call(): pl.pallas_call(functools.partial(final_kernel, scale, chunks), grid=(rows...  10.2 us
    pallas_call x2, Pallas kernels, layer_call(): pl.pallas_call(functools.partial(layer_kernel, scale), in_specs=[SMEM] +...  4.27 us
    pallas_call x1, Pallas kernels, factor_call(): pl.pallas_call(functools.partial(factor_kernel, width), in_specs=[VMEM] *...  3.78 us
    pallas_call x2, Pallas kernels, right_call(): pl.pallas_call(functools.partial(right_kernel, scale, block), in_specs=[S...  3.46 us
  transfers between devices with their start and end apart: 18, of which 9 were waited for; matrix products, arithmetic and copies ran while one was open for 0% of the time, Pallas kernels for 32%

profile of v3, /device:TPU:1, one launch (start us, length us, event | category | flops | bytes accessed | tf_op | source)
XLA Modules:
  0.0 77.6 jit_solution(17275233008072715371)
XLA Ops:
  0.6 0.1 collective-permute-start
  0.8 0.0 copy-start.2
  0.8 0.0 copy-start.5
  0.8 0.0 copy-start
  0.8 0.0 copy-start.1
  0.8 4.0 %left.2 = (f32[512,1024]{1,0:T(8,128)S(1)}, f32[512,1024]{1,0:T(8,128)S(1)}, f32[32,512]{1,0:T(8,128)S(1)}, f32[32,512]{1,0:T(8,128)S(1)}) custom-call(s32[1]{0:T(128)} %bitcast.core, f32[2048,1024]{1,0:T(8,128)} %weights.9, f32[1,2048,1024]{2,1,0:T(8,128)} %copies.7, f32[1,2048,1024]{2,1,0:T(8,128)} %error.3, f32[64,1024]{1,0:T(8,128)} %warm.3), custom_call_target="tpu_custom_call" | custom-call | tf_op jit(solution)/shard_map/left/pallas_call | solution.py:104
  4.7 0.0 collective-permute-done.received
  4.8 0.0 copy-done.2
  4.8 0.0 copy-done.5
  4.8 0.1 both.1.one.refs_1_.refs_0_
  4.9 0.1 copy-done
  4.9 0.6 copy-done.1
  5.6 0.1 away.1
  5.7 0.5 collective-permute-start.12
  6.2 2.3 %collective-permute-start.1 = (f32[128,1024]{1,0:T(8,128)S(1)}, f32[128,1024]{1,0:T(8,128)S(1)}, u32[]{:S(2)}, u32[]{:S(2)}) collective-permute-start(f32[128,1024]{1,0:T(8,128)S(1)} %both.1.one.refs_1_.refs_0_), channel_id=1, source_target_pairs={{0,16},{8,24},{16,0},{24,8},{1,17},{9,25},{17,1},{25,9},{2,18},{10... | collective-permute-start | bytes 1572872 | tf_op jit(solution)/shard_map/ppermute | solution.py:41
  8.5 0.7 collective-permute-start.3
  9.2 0.9 %collective-permute-done.3.two = f32[32,512]{1,0:T(8,128)S(1)} collective-permute-done((f32[32,512]{1,0:T(8,128)S(1)}, f32[32,512]{1,0:T(8,128)S(1)}, u32[]{:S(2)}, u32[]{:S(2)}) %collective-permute-start.3) | collective-permute-done | bytes 65568 | tf_op jit(solution)/shard_map/ppermute | solution.py:41
  10.1 9.4 %left.3 = (f32[1536,1024]{1,0:T(8,128)S(1)}, f32[1536,1024]{1,0:T(8,128)S(1)}, f32[32,1536]{1,0:T(8,128)S(1)}, f32[32,1536]{1,0:T(8,128)S(1)}) custom-call(s32[1]{0:T(128)} %bitcast.core, f32[2048,1024]{1,0:T(8,128)} %weights.9, f32[1,2048,1024]{2,1,0:T(8,128)} %copies.7, f32[1,2048,1024]{2,1,0:T(8,128)} %error.3, f32[64,1024]{1,0:T(8,128)} %warm.3, ...), custom_call_target="tpu_custom_call" | custom-call | tf_op jit(solution)/shard_map/left/pallas_call | solution.py:104
  19.5 0.4 collective-permute-start.4
  19.9 0.8 %collective-permute-start.5 = (f32[32,512]{1,0:T(8,128)S(1)}, f32[32,512]{1,0:T(8,128)S(1)}, u32[]{:S(2)}, u32[]{:S(2)}) collective-permute-start(f32[32,512]{1,0:T(8,128)S(1)} %sum.12.refs_0_.one), channel_id=1, source_target_pairs={{0,16},{8,24},{16,0},{24,8},{1,17},{9,25},{17,1},{25,9},{2,18},{10... | collective-permute-start | bytes 196616 | tf_op jit(solution)/shard_map/ppermute | solution.py:41
  20.8 2.7 %collective-permute-done.5.two = f32[32,512]{1,0:T(8,128)S(1)} collective-permute-done((f32[32,512]{1,0:T(8,128)S(1)}, f32[32,512]{1,0:T(8,128)S(1)}, u32[]{:S(2)}, u32[]{:S(2)}) %collective-permute-start.5) | collective-permute-done | bytes 65568 | tf_op jit(solution)/shard_map/ppermute | solution.py:41
  23.5 0.0 collective-permute-done.1.two
  23.5 0.1 sum.11.refs_0_.mine
  23.6 0.0 collective-permute-done.4.two
  23.6 0.5 collective-permute-start.6
  24.1 5.0 %collective-permute-done.6.two = f32[32,1536]{1,0:T(8,128)S(1)} collective-permute-done((f32[32,1536]{1,0:T(8,128)S(1)}, f32[32,1536]{1,0:T(8,128)S(1)}, u32[]{:S(2)}, u32[]{:S(2)}) %collective-permute-start.6) | collective-permute-done | bytes 196640 | tf_op jit(solution)/shard_map/ppermute | solution.py:41
  29.2 0.0 collective-permute-done.12.received
  29.2 0.2 term.1.one
  29.3 0.0 copy-start.4
  29.3 0.1 collective-permute-start.13
  29.4 2.6 %collective-permute-start.7 = (f32[32,1536]{1,0:T(8,128)S(1)}, f32[32,1536]{1,0:T(8,128)S(1)}, u32[]{:S(2)}, u32[]{:S(2)}) collective-permute-start(f32[32,1536]{1,0:T(8,128)S(1)} %sum.15.mine.refs_0_), channel_id=1, source_target_pairs={{0,8},{8,0},{16,24},{24,16},{1,9},{9,1},{17,25},{25,17},{2,10},{10... | collective-permute-start | bytes 589832 | tf_op jit(solution)/shard_map/ppermute | solution.py:41
  32.0 0.0 collective-permute-start.8
  32.0 1.3 %collective-permute-done.8.other = f32[32,512]{1,0:T(8,128)S(1)} collective-permute-done((f32[32,512]{1,0:T(8,128)S(1)}, f32[32,512]{1,0:T(8,128)S(1)}, u32[]{:S(2)}, u32[]{:S(2)}) %collective-permute-start.8) | collective-permute-done | bytes 65568 | tf_op jit(solution)/shard_map/ppermute | solution.py:41
  33.2 0.9 %right.2 = (f32[32,1152]{1,0:T(8,128)S(1)}, f32[32,1152]{1,0:T(8,128)S(1)}, f32[64,512]{1,0:T(8,128)S(1)}) custom-call(s32[1]{0:T(128)} %bitcast.core, f32[32,512]{1,0:T(8,128)S(1)} %sum.13.refs_1_.mine, f32[32,512]{1,0:T(8,128)S(1)} %collective-permute-done.8.other, f32[512,1024]{1,0:T(8,128)S(1)} %get-tuple-element.38.corrected.refs_2_), custom_call_target="tpu_custom_call" | custom-call | tf_op jit(solution)/shard_map/right/pallas_call | solution.py:165
  34.2 0.0 collective-permute-done.7.other
  34.2 2.5 %right.3 = (f32[32,1152]{1,0:T(8,128)S(1)}, f32[32,1152]{1,0:T(8,128)S(1)}, f32[64,1536]{1,0:T(8,128)S(1)}) custom-call(s32[1]{0:T(128)} %bitcast.core, f32[32,1536]{1,0:T(8,128)S(1)} %sum.15.mine.refs_0_, f32[32,1536]{1,0:T(8,128)S(1)} %collective-permute-done.7.other, f32[1536,1024]{1,0:T(8,128)S(1)} %get-tuple-element.37.corrected.refs_3_, ...), custom_call_target="tpu_custom_call" | custom-call | tf_op jit(solution)/shard_map/right/pallas_call | solution.py:165
  36.7 0.0 copy-start.3
  36.7 0.3 collective-permute-start.9
  37.0 0.2 collective-permute-start.2
  37.3 0.9 %collective-permute-done.9.two = f32[32,1152]{1,0:T(8,128)S(1)} collective-permute-done((f32[32,1152]{1,0:T(8,128)S(1)}, f32[32,1152]{1,0:T(8,128)S(1)}, u32[]{:S(2)}, u32[]{:S(2)}) %collective-permute-start.9) | collective-permute-done | bytes 147488 | tf_op jit(solution)/shard_map/ppermute | solution.py:41
  38.1 1.3 %collective-permute-start.10 = (f32[32,1152]{1,0:T(8,128)S(1)}, f32[32,1152]{1,0:T(8,128)S(1)}, u32[]{:S(2)}, u32[]{:S(2)}) collective-permute-start(f32[32,1152]{1,0:T(8,128)S(1)} %sum.16.one), channel_id=1, source_target_pairs={{0,1},{1,0},{2,3},{3,2},{4,5},{5,4},{6,7},{7,6},{8,9},{9,8},{10,11... | collective-permute-start | bytes 442376 | tf_op jit(solution)/shard_map/ppermute | solution.py:41
  39.4 3.9 %collective-permute-done.10.two = f32[32,1152]{1,0:T(8,128)S(1)} collective-permute-done((f32[32,1152]{1,0:T(8,128)S(1)}, f32[32,1152]{1,0:T(8,128)S(1)}, u32[]{:S(2)}, u32[]{:S(2)}) %collective-permute-start.10) | collective-permute-done | bytes 147488 | tf_op jit(solution)/shard_map/ppermute | solution.py:41
  43.4 1.4 %collective-permute-start.11 = (f32[32,1152]{1,0:T(8,128)S(1)}, f32[32,1152]{1,0:T(8,128)S(1)}, u32[]{:S(2)}, u32[]{:S(2)}) collective-permute-start(f32[32,1152]{1,0:T(8,128)S(1)} %sum.17.one), channel_id=1, source_target_pairs={{0,2},{1,3},{2,0},{3,1},{4,6},{5,7},{6,4},{7,5},{8,10},{9,11},{10,... | collective-permute-start | bytes 442376 | tf_op jit(solution)/shard_map/ppermute | solution.py:41
  44.8 3.0 %collective-permute-done.11.two = f32[32,1152]{1,0:T(8,128)S(1)} collective-permute-done((f32[32,1152]{1,0:T(8,128)S(1)}, f32[32,1152]{1,0:T(8,128)S(1)}, u32[]{:S(2)}, u32[]{:S(2)}) %collective-permute-start.11) | collective-permute-done | bytes 147488 | tf_op jit(solution)/shard_map/ppermute | solution.py:41
  47.8 2.4 %collective-permute-start.14 = (f32[32,1152]{1,0:T(8,128)S(1)}, f32[32,1152]{1,0:T(8,128)S(1)}, u32[]{:S(2)}, u32[]{:S(2)}) collective-permute-start(f32[32,1152]{1,0:T(8,128)S(1)} %sum.18.refs_0_.one), channel_id=1, source_target_pairs={{0,4},{1,5},{2,6},{3,7},{4,0},{5,1},{6,2},{7,3},{8,12},{9,13},{10,... | collective-permute-start | bytes 442376 | tf_op jit(solution)/shard_map/ppermute | solution.py:41
  50.1 0.0 collective-permute-done.2.other
  50.1 0.0 copy-done.4
  50.1 1.6 %layer.2 = (f32[2,128,1024]{2,1,0:T(8,128)}, f32[2,128,1024]{2,1,0:T(8,128)}, f32[8,128]{1,0:T(8,128)S(1)}) custom-call(s32[1]{0:T(128)} %bitcast.core, f32[128,1024]{1,0:T(8,128)S(1)} %sum.11.refs_0_.mine, f32[128,1024]{1,0:T(8,128)S(1)} %collective-permute-done.2.other, f32[2,128,1024]{2,1,0:T(8,128)S(1)} %copy-done.2, f32[2,128,1024]{2,1,0:T(8,128)S(1)} %copy-done.4, ...), custom_call_target="tpu_custom_call" | custom-call | tf_op jit(solution)/shard_map/layer/pallas_call | solution.py:345
  51.8 4.8 %collective-permute-done.14.two = f32[32,1152]{1,0:T(8,128)S(1)} collective-permute-done((f32[32,1152]{1,0:T(8,128)S(1)}, f32[32,1152]{1,0:T(8,128)S(1)}, u32[]{:S(2)}, u32[]{:S(2)}) %collective-permute-start.14) | collective-permute-done | bytes 147488 | tf_op jit(solution)/shard_map/ppermute | solution.py:41
  56.6 0.0 slice-start.1
  56.6 0.0 collective-permute-done.13.two
  56.6 0.1 sum.20.mine
  56.7 1.6 %collective-permute-start.15 = (f32[128,2048]{1,0:T(8,128)S(1)}, f32[128,2048]{1,0:T(8,128)S(1)}, u32[]{:S(2)}, u32[]{:S(2)}) collective-permute-start(f32[128,2048]{1,0:T(8,128)S(1)} %sum.20.mine), channel_id=1, source_target_pairs={{0,8},{8,0},{16,24},{24,16},{1,9},{9,1},{17,25},{25,17},{2,10},{10... | collective-permute-start | bytes 3145736 | tf_op jit(solution)/shard_map/ppermute | solution.py:41
  58.4 1.0 %collective-permute-start.16 = (f32[32,1152]{1,0:T(8,128)S(1)}, f32[32,1152]{1,0:T(8,128)S(1)}, u32[]{:S(2)}, u32[]{:S(2)}) collective-permute-start(f32[32,1152]{1,0:T(8,128)S(1)} %sum.19.refs_0_.message.one), channel_id=1, source_target_pairs={{0,16},{8,24},{16,0},{24,8},{1,17},{9,25},{17,1},{25,9},{2,18},{10... | collective-permute-start | bytes 442376 | tf_op jit(solution)/shard_map/ppermute | solution.py:41
  59.4 3.8 %factor.1 = (f32[64,64]{1,0:T(8,128)S(1)}, bf16[512,384]{1,0:T(8,128)(2,1)S(1)}, bf16[1536,384]{1,0:T(8,128)(2,1)S(1)}) custom-call(f32[32,1152]{1,0:T(8,128)S(1)} %sum.19.refs_0_.message.one, f32[64,512]{1,0:T(8,128)S(1)} %get-tuple-element.46.refs_0_, f32[64,1536]{1,0:T(8,128)S(1)} %get-tuple-element.47.refs_1_), custom_call_target="tpu_custom_call" | custom-call | tf_op jit(solution)/shard_map/factor/pallas_call | solution.py:231
  63.2 0.6 collective-permute-done.16.two
  63.8 0.9 %collective-permute-start.17 = (f32[32,1152]{1,0:T(8,128)S(1)}, f32[32,1152]{1,0:T(8,128)S(1)}, u32[]{:S(2)}, u32[]{:S(2)}) collective-permute-start(f32[32,1152]{1,0:T(8,128)S(1)} %sum.21.refs_0_.mine), channel_id=1, source_target_pairs={{0,8},{8,0},{16,24},{24,16},{1,9},{9,1},{17,25},{25,17},{2,10},{10... | collective-permute-start | bytes 442376 | tf_op jit(solution)/shard_map/ppermute | solution.py:41
  64.8 0.0 collective-permute-done.15.other
  64.8 0.0 copy-done.3
  64.8 2.6 %layer.3 = (f32[2,128,2048]{2,1,0:T(8,128)}, f32[2,128,2048]{2,1,0:T(8,128)}, f32[8,128]{1,0:T(8,128)S(1)}) custom-call(s32[1]{0:T(128)} %bitcast.core, f32[128,2048]{1,0:T(8,128)S(1)} %sum.20.mine, f32[128,2048]{1,0:T(8,128)S(1)} %collective-permute-done.15.other, f32[2,128,2048]{2,1,0:T(8,128)S(1)} %copy-done, f32[2,128,2048]{2,1,0:T(8,128)S(1)} %copy-done.3, ...), custom_call_target="tpu_custom_call" | custom-call | tf_op jit(solution)/shard_map/layer/pallas_call | solution.py:345
  67.4 0.0 collective-permute-done.17.other
  67.4 0.0 slice-done
  67.4 0.0 slice-done.1
  67.4 10.2 %final.1 = (f32[2048,1024]{1,0:T(8,128)}, f32[2048,1024]{1,0:T(8,128)}, f32[1,2048,1024]{2,1,0:T(8,128)}) custom-call(s32[1]{0:T(128)} %bitcast.core, f32[32,1152]{1,0:T(8,128)S(1)} %sum.21.refs_0_.mine, f32[32,1152]{1,0:T(8,128)S(1)} %collective-permute-done.17.other, f32[64,64]{1,0:T(8,128)S(1)} %get-tuple-element.48.refs_0_.inverse, ...), custom_call_target="tpu_custom_call" | custom-call | tf_op jit(solution)/shard_map/final/pallas_call | solution.py:280
  (11 shorter events, 0.1 us)
Async XLA Ops:
  0.6 4.1 %collective-permute-start = (f32[1,2,128,1024]{3,2,1,0:T(8,128)}, f32[1,2,128,1024]{3,2,1,0:T(8,128)S(1)}, u32[]{:S(2)}, u32[]{:S(2)}) collective-permute-start(f32[1,2,128,1024]{3,2,1,0:T(8,128)} %copies.6), channel_id=1, source_target_pairs={{0,8},{8,0},{16,24},{24,16},{1,9},{9,1},{17,25},{25,17},{2,10},{10... | collective-permute-start | bytes 3145736 | tf_op jit(solution)/shard_map/ppermute | solution.py:41
  0.8 4.0 %copy-start.2 = (f32[2,128,1024]{2,1,0:T(8,128)S(1)}, f32[2,128,1024]{2,1,0:T(8,128)}, u32[]{:S(2)}) copy-start(f32[2,128,1024]{2,1,0:T(8,128)} %weights.10) | copy-start | bytes 3145732
  0.8 4.0 %copy-start.5 = (f32[1,2,128,1024]{3,2,1,0:T(8,128)S(1)}, f32[1,2,128,1024]{3,2,1,0:T(8,128)}, u32[]{:S(2)}) copy-start(f32[1,2,128,1024]{3,2,1,0:T(8,128)} %copies.6) | copy-start | bytes 3145732
  0.8 4.2 %copy-start = (f32[2,128,2048]{2,1,0:T(8,128)S(1)}, f32[2,128,2048]{2,1,0:T(8,128)}, u32[]{:S(2)}) copy-start(f32[2,128,2048]{2,1,0:T(8,128)} %weights.13) | copy-start | bytes 6291460
  0.8 4.8 %copy-start.1 = (f32[1,2,128,2048]{3,2,1,0:T(8,128)S(1)}, f32[1,2,128,2048]{3,2,1,0:T(8,128)}, u32[]{:S(2)}) copy-start(f32[1,2,128,2048]{3,2,1,0:T(8,128)} %copies.9) | copy-start | bytes 6291460
  5.7 23.5 %collective-permute-start.12 = (f32[128,2048]{1,0:T(8,128)S(1)}, f32[128,2048]{1,0:T(8,128)S(1)}, u32[]{:S(2)}, u32[]{:S(2)}) collective-permute-start(f32[128,2048]{1,0:T(8,128)S(1)} %away.1), channel_id=1, source_target_pairs={{0,8},{8,0},{16,24},{24,16},{1,9},{9,1},{17,25},{25,17},{2,10},{10... | collective-permute-start | bytes 3145736 | tf_op jit(solution)/shard_map/ppermute | solution.py:41
  6.2 17.3 %collective-permute-start.1 = (f32[128,1024]{1,0:T(8,128)S(1)}, f32[128,1024]{1,0:T(8,128)S(1)}, u32[]{:S(2)}, u32[]{:S(2)}) collective-permute-start(f32[128,1024]{1,0:T(8,128)S(1)} %both.1.one.refs_1_.refs_0_), channel_id=1, source_target_pairs={{0,16},{8,24},{16,0},{24,8},{1,17},{9,25},{17,1},{25,9},{2,18},{10... | collective-permute-start | bytes 1572872 | tf_op jit(solution)/shard_map/ppermute | solution.py:41
  8.5 1.6 %collective-permute-start.3 = (f32[32,512]{1,0:T(8,128)S(1)}, f32[32,512]{1,0:T(8,128)S(1)}, u32[]{:S(2)}, u32[]{:S(2)}) collective-permute-start(f32[32,512]{1,0:T(8,128)S(1)} %get-tuple-element.33.refs_0_), channel_id=1, source_target_pairs={{0,8},{8,0},{16,24},{24,16},{1,9},{9,1},{17,25},{25,17},{2,10},{10... | collective-permute-start | bytes 196616 | tf_op jit(solution)/shard_map/ppermute | solution.py:41
  19.5 4.1 %collective-permute-start.4 = (f32[32,1536]{1,0:T(8,128)S(1)}, f32[32,1536]{1,0:T(8,128)S(1)}, u32[]{:S(2)}, u32[]{:S(2)}) collective-permute-start(f32[32,1536]{1,0:T(8,128)S(1)} %get-tuple-element.36), channel_id=1, source_target_pairs={{0,8},{8,0},{16,24},{24,16},{1,9},{9,1},{17,25},{25,17},{2,10},{10... | collective-permute-start | bytes 589832 | tf_op jit(solution)/shard_map/ppermute | solution.py:41
  19.9 3.5 %collective-permute-start.5 = (f32[32,512]{1,0:T(8,128)S(1)}, f32[32,512]{1,0:T(8,128)S(1)}, u32[]{:S(2)}, u32[]{:S(2)}) collective-permute-start(f32[32,512]{1,0:T(8,128)S(1)} %sum.12.refs_0_.one), channel_id=1, source_target_pairs={{0,16},{8,24},{16,0},{24,8},{1,17},{9,25},{17,1},{25,9},{2,18},{10... | collective-permute-start | bytes 196616 | tf_op jit(solution)/shard_map/ppermute | solution.py:41
  23.6 5.5 %collective-permute-start.6 = (f32[32,1536]{1,0:T(8,128)S(1)}, f32[32,1536]{1,0:T(8,128)S(1)}, u32[]{:S(2)}, u32[]{:S(2)}) collective-permute-start(f32[32,1536]{1,0:T(8,128)S(1)} %sum.14.one), channel_id=1, source_target_pairs={{0,16},{8,24},{16,0},{24,8},{1,17},{9,25},{17,1},{25,9},{2,18},{10... | collective-permute-start | bytes 589832 | tf_op jit(solution)/shard_map/ppermute | solution.py:41
  29.3 20.8 %copy-start.4 = (f32[2,128,1024]{2,1,0:T(8,128)S(1)}, f32[2,128,1024]{2,1,0:T(8,128)}, u32[]{:S(2)}) copy-start(f32[2,128,1024]{2,1,0:T(8,128)} %moment.3) | copy-start | bytes 3145732
  29.3 27.3 %collective-permute-start.13 = (f32[128,2048]{1,0:T(8,128)S(1)}, f32[128,2048]{1,0:T(8,128)S(1)}, u32[]{:S(2)}, u32[]{:S(2)}) collective-permute-start(f32[128,2048]{1,0:T(8,128)S(1)} %term.1.one), channel_id=1, source_target_pairs={{0,16},{8,24},{16,0},{24,8},{1,17},{9,25},{17,1},{25,9},{2,18},{10... | collective-permute-start | bytes 3145736 | tf_op jit(solution)/shard_map/ppermute | solution.py:41
  29.4 4.7 %collective-permute-start.7 = (f32[32,1536]{1,0:T(8,128)S(1)}, f32[32,1536]{1,0:T(8,128)S(1)}, u32[]{:S(2)}, u32[]{:S(2)}) collective-permute-start(f32[32,1536]{1,0:T(8,128)S(1)} %sum.15.mine.refs_0_), channel_id=1, source_target_pairs={{0,8},{8,0},{16,24},{24,16},{1,9},{9,1},{17,25},{25,17},{2,10},{10... | collective-permute-start | bytes 589832 | tf_op jit(solution)/shard_map/ppermute | solution.py:41
  32.0 1.3 %collective-permute-start.8 = (f32[32,512]{1,0:T(8,128)S(1)}, f32[32,512]{1,0:T(8,128)S(1)}, u32[]{:S(2)}, u32[]{:S(2)}) collective-permute-start(f32[32,512]{1,0:T(8,128)S(1)} %sum.13.refs_1_.mine), channel_id=1, source_target_pairs={{0,8},{8,0},{16,24},{24,16},{1,9},{9,1},{17,25},{25,17},{2,10},{10... | collective-permute-start | bytes 196616 | tf_op jit(solution)/shard_map/ppermute | solution.py:41
  36.7 28.1 %copy-start.3 = (f32[2,128,2048]{2,1,0:T(8,128)S(1)}, f32[2,128,2048]{2,1,0:T(8,128)}, u32[]{:S(2)}) copy-start(f32[2,128,2048]{2,1,0:T(8,128)} %moment.4) | copy-start | bytes 6291460
  36.7 1.4 %collective-permute-start.9 = (f32[32,1152]{1,0:T(8,128)S(1)}, f32[32,1152]{1,0:T(8,128)S(1)}, u32[]{:S(2)}, u32[]{:S(2)}) collective-permute-start(f32[32,1152]{1,0:T(8,128)S(1)} %get-tuple-element.42), channel_id=1, source_target_pairs={{0,8},{8,0},{16,24},{24,16},{1,9},{9,1},{17,25},{25,17},{2,10},{10... | collective-permute-start | bytes 442376 | tf_op jit(solution)/shard_map/ppermute | solution.py:41
  37.0 13.1 %collective-permute-start.2 = (f32[128,1024]{1,0:T(8,128)S(1)}, f32[128,1024]{1,0:T(8,128)S(1)}, u32[]{:S(2)}, u32[]{:S(2)}) collective-permute-start(f32[128,1024]{1,0:T(8,128)S(1)} %sum.11.refs_0_.mine), channel_id=1, source_target_pairs={{0,8},{8,0},{16,24},{24,16},{1,9},{9,1},{17,25},{25,17},{2,10},{10... | collective-permute-start | bytes 1572872 | tf_op jit(solution)/shard_map/ppermute | solution.py:41
  38.1 5.2 %collective-permute-start.10 = (f32[32,1152]{1,0:T(8,128)S(1)}, f32[32,1152]{1,0:T(8,128)S(1)}, u32[]{:S(2)}, u32[]{:S(2)}) collective-permute-start(f32[32,1152]{1,0:T(8,128)S(1)} %sum.16.one), channel_id=1, source_target_pairs={{0,1},{1,0},{2,3},{3,2},{4,5},{5,4},{6,7},{7,6},{8,9},{9,8},{10,11... | collective-permute-start | bytes 442376 | tf_op jit(solution)/shard_map/ppermute | solution.py:41
  43.4 24.0 %slice-start = ((s8[8388608]{0:T(1024)(128)(4,1)}), s8[4194304]{0:T(1024)(128)(4,1)S(1)}, s32[]{:S(2)}) async-start(s8[8388608]{0:T(1024)(128)(4,1)} %bitcast.1), calls=%async_computation | async-start | bytes 8388608
  43.4 4.4 %collective-permute-start.11 = (f32[32,1152]{1,0:T(8,128)S(1)}, f32[32,1152]{1,0:T(8,128)S(1)}, u32[]{:S(2)}, u32[]{:S(2)}) collective-permute-start(f32[32,1152]{1,0:T(8,128)S(1)} %sum.17.one), channel_id=1, source_target_pairs={{0,2},{1,3},{2,0},{3,1},{4,6},{5,7},{6,4},{7,5},{8,10},{9,11},{10,... | collective-permute-start | bytes 442376 | tf_op jit(solution)/shard_map/ppermute | solution.py:41
  47.8 8.8 %collective-permute-start.14 = (f32[32,1152]{1,0:T(8,128)S(1)}, f32[32,1152]{1,0:T(8,128)S(1)}, u32[]{:S(2)}, u32[]{:S(2)}) collective-permute-start(f32[32,1152]{1,0:T(8,128)S(1)} %sum.18.refs_0_.one), channel_id=1, source_target_pairs={{0,4},{1,5},{2,6},{3,7},{4,0},{5,1},{6,2},{7,3},{8,12},{9,13},{10,... | collective-permute-start | bytes 442376 | tf_op jit(solution)/shard_map/ppermute | solution.py:41
  56.6 10.8 %slice-start.1 = ((s8[8388608]{0:T(1024)(128)(4,1)}), s8[4194304]{0:T(1024)(128)(4,1)S(1)}, s32[]{:S(2)}) async-start(s8[8388608]{0:T(1024)(128)(4,1)} %bitcast.1), calls=%async_computation.1 | async-start | bytes 8388608
  56.7 8.0 %collective-permute-start.15 = (f32[128,2048]{1,0:T(8,128)S(1)}, f32[128,2048]{1,0:T(8,128)S(1)}, u32[]{:S(2)}, u32[]{:S(2)}) collective-permute-start(f32[128,2048]{1,0:T(8,128)S(1)} %sum.20.mine), channel_id=1, source_target_pairs={{0,8},{8,0},{16,24},{24,16},{1,9},{9,1},{17,25},{25,17},{2,10},{10... | collective-permute-start | bytes 3145736 | tf_op jit(solution)/shard_map/ppermute | solution.py:41
  58.4 5.4 %collective-permute-start.16 = (f32[32,1152]{1,0:T(8,128)S(1)}, f32[32,1152]{1,0:T(8,128)S(1)}, u32[]{:S(2)}, u32[]{:S(2)}) collective-permute-start(f32[32,1152]{1,0:T(8,128)S(1)} %sum.19.refs_0_.message.one), channel_id=1, source_target_pairs={{0,16},{8,24},{16,0},{24,8},{1,17},{9,25},{17,1},{25,9},{2,18},{10... | collective-permute-start | bytes 442376 | tf_op jit(solution)/shard_map/ppermute | solution.py:41
  63.8 3.6 %collective-permute-start.17 = (f32[32,1152]{1,0:T(8,128)S(1)}, f32[32,1152]{1,0:T(8,128)S(1)}, u32[]{:S(2)}, u32[]{:S(2)}) collective-permute-start(f32[32,1152]{1,0:T(8,128)S(1)} %sum.21.refs_0_.mine), channel_id=1, source_target_pairs={{0,8},{8,0},{16,24},{24,16},{1,9},{9,1},{17,25},{25,17},{2,10},{10... | collective-permute-start | bytes 442376 | tf_op jit(solution)/shard_map/ppermute | solution.py:41

commit v4 on v3

--- a/solution.py
+++ b/solution.py
@@ -130,7 +130,7 @@
     )(core, in_hbm(weights), in_hbm(copies), in_hbm(error), in_hbm(warm), *after)
 
 
-def right_kernel(scale, block, core, mine, other, corrected, *refs):
+def right_kernel(scale, block, chunk, core, mine, other, corrected, *refs):
     away, kept, left = refs[-3:]
     half, rows = mine.shape
     width = corrected.shape[1]
@@ -141,7 +141,8 @@
     total = None
     for i in range(rows // block):
         cut = slice(i * block, (i + 1) * block)
-        term = stacked_product(parts[:, cut], corrected[cut, :], ((1,), (0,)))
+        here = slice(chunk * rows + i * block, chunk * rows + (i + 1) * block)
+        term = stacked_product(parts[:, cut], corrected[here, :], ((1,), (0,)))
         total = term if total is None else total + term
     square = stacked_product(parts, whole, ((1,), (1,)))
     top, bottom = total[:half], total[half:]
@@ -158,12 +159,12 @@
     kept[:, width:] = gram
 
 
-def right_call(core, mine, other, corrected, before, scale, block):
+def right_call(core, mine, other, corrected, before, scale, block, chunk):
     half, rows = mine.shape
     width = corrected.shape[1]
     message = jax.ShapeDtypeStruct((half, width + 4 * half), jnp.float32)
     return pl.pallas_call(
-        functools.partial(right_kernel, scale, block),
+        functools.partial(right_kernel, scale, block, chunk),
         in_specs=[SMEM] + [VMEM] * (3 + len(before)),
         out_specs=[VMEM] * 3,
         out_shape=[message, message, jax.ShapeDtypeStruct((2 * half, rows), jnp.float32)],
@@ -239,8 +240,8 @@
     )(message, *left)
 
 
-def final_kernel(scale, chunks, core, mine, other, inverse, moment, *refs):
-    weights, corrected, basis = refs[:chunks], refs[chunks : 2 * chunks], refs[2 * chunks : 3 * chunks]
+def final_kernel(scale, chunks, core, mine, other, inverse, moment, weights, corrected, *refs):
+    basis = refs[:chunks]
     updated, velocity, carried, parts = refs[-4:]
     step = pl.program_id(0)
     rows, width = updated.shape
@@ -258,14 +259,14 @@
     def work(chunk, at):
         there = pl.ds(pl.multiple_of(at, rows), rows)
         change = jnp.dot(basis[chunk][there, :], parts[...], preferred_element_type=jnp.float32)
-        carried[0] = corrected[chunk][there, :] - change
-        new, speed = nesterov(weights[chunk][there, :], change, moment[here, :])
+        carried[0] = corrected[here, :] - change
+        new, speed = nesterov(weights[here, :], change, moment[here, :])
         updated[...] = new
         velocity[...] = speed
 
     first = 0
     for chunk in range(chunks):
-        count = corrected[chunk].shape[0] // rows
+        count = basis[chunk].shape[0] // rows
         here_now = jnp.logical_and(step >= first, step < first + count)
         pl.when(here_now)(functools.partial(work, chunk, (step - first) * rows))
         first += count
@@ -274,9 +275,9 @@
 def final_call(core, mine, other, inverse, moment, weights, corrected, basis, after, scale, block):
     rows, width = moment.shape
     rank = inverse.shape[0]
-    chunks = len(corrected)
+    chunks = len(basis)
     out = pl.BlockSpec((block, width), lambda i: (i, 0))
-    large = [in_vmem(value) for value in (moment, *weights, *corrected, *basis)]
+    large = [in_vmem(value) for value in (moment, weights, corrected, *basis)]
     return pl.pallas_call(
         functools.partial(final_kernel, scale, chunks),
         grid=(rows // block,),
@@ -288,29 +289,56 @@
             jax.ShapeDtypeStruct((1, rows, width), jnp.float32),
         ],
         scratch_shapes=[pltpu.VMEM((6 * rank, width), jnp.bfloat16)],
-        compiler_params=pltpu.CompilerParams(vmem_limit_bytes=16 * MIB),
+        compiler_params=pltpu.CompilerParams(vmem_limit_bytes=24 * MIB),
         name="final",
     )(core, mine, other, inverse, *large, *after)
 
 
-def sum_kernel(one, two, *refs):
-    refs[-1][...] = one[...] + two[...]
-
-
-def sum_call(one, two, after):
-    return pl.pallas_call(
-        sum_kernel,
+def sum_kernel(parts, one, two, *refs):
+    width = one.shape[1] // parts
+    for i, out in enumerate(refs[len(refs) - parts :]):
+        cut = slice(i * width, (i + 1) * width)
+        out[...] = one[:, cut] + two[:, cut]
+
+
+def sum_call(one, two, after, parts=1):
+    out = jax.ShapeDtypeStruct((one.shape[0], one.shape[1] // parts), one.dtype)
+    return pl.pallas_call(
+        functools.partial(sum_kernel, parts),
         in_specs=[VMEM] * 2 + [ANY] * len(after),
-        out_specs=VMEM,
-        out_shape=jax.ShapeDtypeStruct(one.shape, one.dtype),
+        out_specs=VMEM if parts == 1 else [VMEM] * parts,
+        out_shape=out if parts == 1 else [out] * parts,
         compiler_params=pltpu.CompilerParams(vmem_limit_bytes=8 * MIB),
         name="sum",
     )(one, two, *after)
 
 
 def away_kernel(core, weights, copies, *refs):
-    at = 1 - core[0]
-    refs[-1][...] = weights[at] - copies[0, at]
+    refs[-1][...] = weights[0] - copies[0, 0]
+
+
+def both_kernel(core, weights, copies, received, *refs):
+    refs[-1][...] = (weights[0] - copies[0, 0]) + (weights[0] - received[0, 0])
+
+
+def half_call(kernel, flip, core, weights, copies, after):
+    _, rows, width = weights.shape
+    block = rows // 2 if rows % 16 == 0 else rows
+    pick = (lambda core: 1 - core[0]) if flip else (lambda core: core[0])
+    part = pl.BlockSpec((1, block, width), lambda i, core: (pick(core), i, 0))
+    whole = pl.BlockSpec((1, 1, block, width), lambda i, core: (0, pick(core), i, 0))
+    return pl.pallas_call(
+        kernel,
+        grid_spec=pltpu.PrefetchScalarGridSpec(
+            num_scalar_prefetch=1,
+            grid=(rows // block,),
+            in_specs=[part] + [whole] * len(copies) + [ANY] * len(after),
+            out_specs=pl.BlockSpec((block, width), lambda i, core: (i, 0)),
+        ),
+        out_shape=jax.ShapeDtypeStruct((rows, width), jnp.float32),
+        compiler_params=pltpu.CompilerParams(vmem_limit_bytes=12 * MIB),
+        name=kernel.__name__[:-7],
+    )(core, in_hbm(weights), in_hbm(copies[0]), *copies[1:], *after)
 
 
 def term_kernel(core, weights, copies, received, *refs):
@@ -318,20 +346,15 @@
     refs[-1][...] = (weights[at] - copies[0, at]) + received[...]
 
 
-def both_kernel(core, weights, copies, received, *refs):
-    at = core[0]
-    refs[-1][...] = (weights[at] - copies[0, at]) + (weights[at] - received[0, at])
-
-
-def difference_call(kernel, core, operands, after):
-    return pl.pallas_call(
-        kernel,
-        in_specs=[SMEM] + [VMEM] * len(operands) + [ANY] * len(after),
+def term_call(core, weights, copies, received, after):
+    return pl.pallas_call(
+        term_kernel,
+        in_specs=[SMEM] + [VMEM] * 3 + [ANY] * len(after),
         out_specs=VMEM,
-        out_shape=jax.ShapeDtypeStruct(operands[0].shape[1:], jnp.float32),
+        out_shape=jax.ShapeDtypeStruct(weights.shape[1:], jnp.float32),
         compiler_params=pltpu.CompilerParams(vmem_limit_bytes=12 * MIB),
-        name=kernel.__name__[:-7],
-    )(core, *operands, *after)
+        name="term",
+    )(core, weights, copies, received, *after)
 
 
 def layer_kernel(scale, core, mine, other, weights, moment, *refs):
@@ -369,40 +392,30 @@
     scale = 1 / replicas
     rank, width = warm_start.shape
     rows = embed_weights.shape[0]
-    sizes = (rows // 4, rows - rows // 4) if rows % 2048 == 0 else (rows,)
-    chunks = len(sizes)
     core = jnp.reshape(lax.axis_index("replica") % 2, (1,)).astype(jnp.int32)
 
     square_received = swap(square_copies, "replica", 1)
-    corrected, held, left, after, before = [], [], [], (), ()
-    start, exchanged = 0, []
-    for chunk, size in enumerate(sizes):
-        value, weights, away, kept = left_call(
-            core, embed_weights, embed_copies, embed_error, warm_start, after, start, size, math.gcd(size, 256 << chunk)
+    broad_away = half_call(away_kernel, True, core, broad_weights, (broad_copies,), ())
+    square_half = half_call(both_kernel, False, core, square_weights, (square_copies, square_received), (broad_away,))
+    broad_received = swap(broad_away, "replica", 1)
+    chunks = 2 if rows % 512 == 0 else 1
+    corrected, held, away, kept = left_call(
+        core, embed_weights, embed_copies, embed_error, warm_start, (square_half,), 0, rows, math.gcd(rows, 512)
+    )
+    square_half = sum_over_chips(square_half, ())
+    pair = sum_call(kept, swap(away, "replica", 1), (square_half,), chunks)
+    halves, others, ready = [], [], ()
+    for piece in pair if chunks > 1 else [pair]:
+        halves.append(sum_over_chips(piece, ready))
+        others.append(swap(halves[-1], "replica", 1))
+        ready = (others[-1],)
+    broad_half = term_call(core, broad_weights, broad_copies, broad_received, tuple(halves))
+    before, left = [], []
+    for chunk, half in enumerate(halves):
+        *before, piece = right_call(
+            core, half, others[chunk], corrected, before, scale, math.gcd(rows // chunks, 256), chunk
         )
-        start += size
-        corrected.append(value)
-        held.append(weights)
-        half = sum_call(kept, swap(away, "replica", 1), exchanged)
-        if chunk == 0:
-            square_half = difference_call(
-                both_kernel, core, (square_weights, square_copies, square_received), (away,)
-            )
-            after = (half, square_half)
-            square_half_first = square_half
-            square_half = sum_over_chips(square_half, ())
-            exchanged.append(square_half)
-            broad_away = difference_call(away_kernel, core, (broad_weights, broad_copies), (square_half_first,))
-            broad_received = swap(broad_away, "replica", 1)
-        half = sum_over_chips(half, ())
-        exchanged.append(half)
-        other = swap(half, "replica", 1)
-        left.append((half, other))
-    broad_half = difference_call(term_kernel, core, (broad_weights, broad_copies, broad_received), (half,))
-    for chunk, size in enumerate(sizes):
-        *before, left[chunk] = right_call(
-            core, *left[chunk], corrected[chunk], before, scale, math.gcd(size, 256)
-        )
+        left.append(piece)
     away, kept = before
 
     message = sum_call(kept, swap(away, "replica", 1), ())
@@ -428,7 +441,7 @@
     )
     right_other = swap(right_half, "replica", 1)
     embed_updated, embed_velocity, embed_carried = final_call(
-        core, right_half, right_other, inverse, embed_moment, held, corrected, basis, (mark,), scale, math.gcd(rows, 256)
+        core, right_half, right_other, inverse, embed_moment, held, corrected, basis, (mark,), scale, math.gcd(rows, 512)
     )
     return (
         square_updated,

time: 77.7 us -> 75.3 us (0.969)
  waiting for transfers between devices: 23.1 us -> 21.2 us
    pallas_call x16 -> x15, Pallas kernels: 4.12 us -> 6.76 us  [the longest x2 3.4 us: right_call(): pl.pallas_call(functools.partial(right_kernel, scale, block, chunk), in_s...]
    pallas_call x2 -> x1, Pallas kernels: 13.4 us -> 11.3 us  [left_call(): pl.pallas_call(functools.partial(left_kernel, len(after)), grid=(rows //...]
    ppermute x18 -> x17, waiting for transfers between devices: 23.1 us -> 21.2 us  [swap(): lax.ppermute(value, axis, [(i, i ^ bit) for i in range(lax.axis_size(axis...]
    ppermute x18 -> x17, starting transfers between devices: 17.2 us -> 17.1 us  [swap(): lax.ppermute(value, axis, [(i, i ^ bit) for i in range(lax.axis_size(axis...]
  transfers between devices with their start and end apart: 18 -> 17, of which waited for: 9 -> 10; matrix products, arithmetic and copies ran while one was open for 0% -> 0% of each run, Pallas kernels for 32% -> 34%
where the time goes in v4:
time: 75.3 us; the launch traced here: 75.1 us
  Pallas kernels  36.1 us (48%)
  waiting for transfers between devices  21.2 us (28%)
  starting transfers between devices  17.1 us (23%)
  between operations  0.81 us (1%)
    ppermute x17, waiting for transfers between devices, swap(): lax.ppermute(value, axis, [(i, i ^ bit) for i in range(lax.axis_size(axis...  21.2 us
    ppermute x17, starting transfers between devices, swap(): lax.ppermute(value, axis, [(i, i ^ bit) for i in range(lax.axis_size(axis...  17.1 us
    pallas_call x1, Pallas kernels, left_call(): pl.pallas_call(functools.partial(left_kernel, len(after)), grid=(rows //...  11.3 us
    pallas_call x1, Pallas kernels, final_call(): pl.pallas_call(functools.partial(final_kernel, scale, chunks), grid=(rows...  9.96 us
    pallas_call x2, Pallas kernels, layer_call(): pl.pallas_call(functools.partial(layer_kernel, scale), in_specs=[SMEM] +...  4.28 us
    pallas_call x1, Pallas kernels, factor_call(): pl.pallas_call(functools.partial(factor_kernel, width), in_specs=[VMEM] *...  3.78 us
    pallas_call x2, Pallas kernels, right_call(): pl.pallas_call(functools.partial(right_kernel, scale, block, chunk), in_s...  3.4 us
    pallas_call x2, Pallas kernels, half_call(): pl.pallas_call(kernel, grid_spec=pltpu.PrefetchScalarGridSpec(num_scalar_...  2.85 us
  transfers between devices with their start and end apart: 17, of which 10 were waited for; matrix products, arithmetic and copies ran while one was open for 0% of the time, Pallas kernels for 34%

profile of v4, /device:TPU:1, one launch (start us, length us, event | category | flops | bytes accessed | tf_op | source)
XLA Modules:
  0.0 75.1 jit_solution(4188668124412679722)
XLA Ops:
  0.6 0.1 collective-permute-start
  0.8 1.6 %away.1.refs_0_ = f32[128,2048]{1,0:T(8,128)S(1)} custom-call(s32[1]{0:T(128)} %bitcast.core, f32[2,128,2048]{2,1,0:T(8,128)} %weights.11, f32[1,2,128,2048]{3,2,1,0:T(8,128)} %copies.7), custom_call_target="tpu_custom_call" | custom-call | tf_op jit(solution)/shard_map/away/pallas_call | solution.py:330
  2.4 0.5 collective-permute-start.11
  2.9 0.7 collective-permute-done.received
  3.6 1.3 %both.1.one.refs_0_ = f32[128,1024]{1,0:T(8,128)S(1)} custom-call(s32[1]{0:T(128)} %bitcast.core, f32[2,128,1024]{2,1,0:T(8,128)} %weights.9, f32[1,2,128,1024]{3,2,1,0:T(8,128)} %copies.5, f32[1,2,128,1024]{3,2,1,0:T(8,128)S(1)} %collective-permute-done.received, f32[128,2048]{1,0:T(8,128)S(1)} %away.1.refs_0_), custom_call_target="tpu_custom_call" | custom-call | tf_op jit(solution)/shard_map/both/pallas_call | solution.py:330
  4.8 0.0 copy-start
  4.8 0.0 copy-start.1
  4.9 2.4 %collective-permute-start.1 = (f32[128,1024]{1,0:T(8,128)S(1)}, f32[128,1024]{1,0:T(8,128)S(1)}, u32[]{:S(2)}, u32[]{:S(2)}) collective-permute-start(f32[128,1024]{1,0:T(8,128)S(1)} %both.1.one.refs_0_), channel_id=1, source_target_pairs={{0,16},{8,24},{16,0},{24,8},{1,17},{9,25},{17,1},{25,9},{2,18},{10... | collective-permute-start | bytes 1572872 | tf_op jit(solution)/shard_map/ppermute | solution.py:41
  7.3 11.3 %left.1 = (f32[2048,1024]{1,0:T(8,128)S(1)}, f32[2048,1024]{1,0:T(8,128)S(1)}, f32[32,2048]{1,0:T(8,128)S(1)}, f32[32,2048]{1,0:T(8,128)S(1)}) custom-call(s32[1]{0:T(128)} %bitcast.core, f32[2048,1024]{1,0:T(8,128)} %weights.8, f32[1,2048,1024]{2,1,0:T(8,128)} %copies.6, f32[1,2048,1024]{2,1,0:T(8,128)} %error.1, f32[64,1024]{1,0:T(8,128)} %warm.1, ...), custom_call_target="tpu_custom_call" | custom-call | tf_op jit(solution)/shard_map/left/pallas_call | solution.py:104
  18.5 0.7 collective-permute-start.3
  19.3 0.0 collective-permute-done.1.two
  19.3 0.1 sum.10.refs_0_.mine
  19.3 1.1 %collective-permute-done.3.two = f32[32,2048]{1,0:T(8,128)S(1)} collective-permute-done((f32[32,2048]{1,0:T(8,128)S(1)}, f32[32,2048]{1,0:T(8,128)S(1)}, u32[]{:S(2)}, u32[]{:S(2)}) %collective-permute-start.3) | collective-permute-done | bytes 262176 | tf_op jit(solution)/shard_map/ppermute | solution.py:41
  20.5 0.1 collective-permute-start.5
  20.6 1.4 %collective-permute-start.4 = (f32[32,1024]{1,0:T(8,128)S(1)}, f32[32,1024]{1,0:T(8,128)S(1)}, u32[]{:S(2)}, u32[]{:S(2)}) collective-permute-start(f32[32,1024]{1,0:T(8,128)S(1)} %get-tuple-element.33.one), channel_id=1, source_target_pairs={{0,16},{8,24},{16,0},{24,8},{1,17},{9,25},{17,1},{25,9},{2,18},{10... | collective-permute-start | bytes 393224 | tf_op jit(solution)/shard_map/ppermute | solution.py:41
  22.0 3.2 %collective-permute-done.5.two = f32[32,1024]{1,0:T(8,128)S(1)} collective-permute-done((f32[32,1024]{1,0:T(8,128)S(1)}, f32[32,1024]{1,0:T(8,128)S(1)}, u32[]{:S(2)}, u32[]{:S(2)}) %collective-permute-start.5) | collective-permute-done | bytes 131104 | tf_op jit(solution)/shard_map/ppermute | solution.py:41
  25.3 2.1 %collective-permute-start.6 = (f32[32,1024]{1,0:T(8,128)S(1)}, f32[32,1024]{1,0:T(8,128)S(1)}, u32[]{:S(2)}, u32[]{:S(2)}) collective-permute-start(f32[32,1024]{1,0:T(8,128)S(1)} %sum.12.mine.refs_0_), channel_id=1, source_target_pairs={{0,8},{8,0},{16,24},{24,16},{1,9},{9,1},{17,25},{25,17},{2,10},{10... | collective-permute-start | bytes 393224 | tf_op jit(solution)/shard_map/ppermute | solution.py:41
  27.3 0.7 collective-permute-done.4.two
  28.0 0.3 collective-permute-done.6.refs_0_.other
  28.3 0.0 collective-permute-done.11.received
  28.3 0.0 copy-done
  28.3 0.0 copy-done.1
  28.4 0.2 term.1.one
  28.6 0.7 collective-permute-start.12
  29.3 0.6 collective-permute-start.7
  29.9 0.0 copy-start.2
  29.9 0.0 copy-start.4
  29.9 1.7 %right.2 = (f32[32,1152]{1,0:T(8,128)S(1)}, f32[32,1152]{1,0:T(8,128)S(1)}, f32[64,1024]{1,0:T(8,128)S(1)}) custom-call(s32[1]{0:T(128)} %bitcast.core, f32[32,1024]{1,0:T(8,128)S(1)} %sum.12.mine.refs_0_, f32[32,1024]{1,0:T(8,128)S(1)} %collective-permute-done.6.refs_0_.other, f32[2048,1024]{1,0:T(8,128)S(1)} %get-tuple-element.35.corrected), custom_call_target="tpu_custom_call" | custom-call | tf_op jit(solution)/shard_map/right/pallas_call | solution.py:166
  31.6 0.0 collective-permute-done.7.other
  31.6 0.0 copy-start.3
  31.7 1.7 %right.3 = (f32[32,1152]{1,0:T(8,128)S(1)}, f32[32,1152]{1,0:T(8,128)S(1)}, f32[64,1024]{1,0:T(8,128)S(1)}) custom-call(s32[1]{0:T(128)} %bitcast.core, f32[32,1024]{1,0:T(8,128)S(1)} %sum.13.mine.refs_1_, f32[32,1024]{1,0:T(8,128)S(1)} %collective-permute-done.7.other, f32[2048,1024]{1,0:T(8,128)S(1)} %get-tuple-element.35.corrected, ...), custom_call_target="tpu_custom_call" | custom-call | tf_op jit(solution)/shard_map/right/pallas_call | solution.py:166
  33.4 0.0 slice-start
  33.4 0.1 collective-permute-start.8
  33.4 0.5 collective-permute-start.2
  33.9 0.9 %collective-permute-done.8.two = f32[32,1152]{1,0:T(8,128)S(1)} collective-permute-done((f32[32,1152]{1,0:T(8,128)S(1)}, f32[32,1152]{1,0:T(8,128)S(1)}, u32[]{:S(2)}, u32[]{:S(2)}) %collective-permute-start.8) | collective-permute-done | bytes 147488 | tf_op jit(solution)/shard_map/ppermute | solution.py:41
  34.8 1.8 %collective-permute-start.9 = (f32[32,1152]{1,0:T(8,128)S(1)}, f32[32,1152]{1,0:T(8,128)S(1)}, u32[]{:S(2)}, u32[]{:S(2)}) collective-permute-start(f32[32,1152]{1,0:T(8,128)S(1)} %sum.14.one), channel_id=1, source_target_pairs={{0,1},{1,0},{2,3},{3,2},{4,5},{5,4},{6,7},{7,6},{8,9},{9,8},{10,11... | collective-permute-start | bytes 442376 | tf_op jit(solution)/shard_map/ppermute | solution.py:41
  36.6 4.1 %collective-permute-done.9.two = f32[32,1152]{1,0:T(8,128)S(1)} collective-permute-done((f32[32,1152]{1,0:T(8,128)S(1)}, f32[32,1152]{1,0:T(8,128)S(1)}, u32[]{:S(2)}, u32[]{:S(2)}) %collective-permute-start.9) | collective-permute-done | bytes 147488 | tf_op jit(solution)/shard_map/ppermute | solution.py:41
  40.7 1.3 %collective-permute-start.10 = (f32[32,1152]{1,0:T(8,128)S(1)}, f32[32,1152]{1,0:T(8,128)S(1)}, u32[]{:S(2)}, u32[]{:S(2)}) collective-permute-start(f32[32,1152]{1,0:T(8,128)S(1)} %sum.15.one), channel_id=1, source_target_pairs={{0,2},{1,3},{2,0},{3,1},{4,6},{5,7},{6,4},{7,5},{8,10},{9,11},{10,... | collective-permute-start | bytes 442376 | tf_op jit(solution)/shard_map/ppermute | solution.py:41
  42.0 3.5 %collective-permute-done.10.two = f32[32,1152]{1,0:T(8,128)S(1)} collective-permute-done((f32[32,1152]{1,0:T(8,128)S(1)}, f32[32,1152]{1,0:T(8,128)S(1)}, u32[]{:S(2)}, u32[]{:S(2)}) %collective-permute-start.10) | collective-permute-done | bytes 147488 | tf_op jit(solution)/shard_map/ppermute | solution.py:41
  45.5 2.0 %collective-permute-start.13 = (f32[32,1152]{1,0:T(8,128)S(1)}, f32[32,1152]{1,0:T(8,128)S(1)}, u32[]{:S(2)}, u32[]{:S(2)}) collective-permute-start(f32[32,1152]{1,0:T(8,128)S(1)} %sum.16.refs_0_.one), channel_id=1, source_target_pairs={{0,4},{1,5},{2,6},{3,7},{4,0},{5,1},{6,2},{7,3},{8,12},{9,13},{10,... | collective-permute-start | bytes 442376 | tf_op jit(solution)/shard_map/ppermute | solution.py:41
  47.5 0.0 collective-permute-done.2.other
  47.5 0.0 copy-done.2
  47.5 0.0 copy-done.4
  47.5 1.6 %layer.2 = (f32[2,128,1024]{2,1,0:T(8,128)}, f32[2,128,1024]{2,1,0:T(8,128)}, f32[8,128]{1,0:T(8,128)S(1)}) custom-call(s32[1]{0:T(128)} %bitcast.core, f32[128,1024]{1,0:T(8,128)S(1)} %sum.10.refs_0_.mine, f32[128,1024]{1,0:T(8,128)S(1)} %collective-permute-done.2.other, f32[2,128,1024]{2,1,0:T(8,128)S(1)} %copy-done.2, f32[2,128,1024]{2,1,0:T(8,128)S(1)} %copy-done.4, ...), custom_call_target="tpu_custom_call" | custom-call | tf_op jit(solution)/shard_map/layer/pallas_call | solution.py:368
  49.2 5.6 %collective-permute-done.13.two = f32[32,1152]{1,0:T(8,128)S(1)} collective-permute-done((f32[32,1152]{1,0:T(8,128)S(1)}, f32[32,1152]{1,0:T(8,128)S(1)}, u32[]{:S(2)}, u32[]{:S(2)}) %collective-permute-start.13) | collective-permute-done | bytes 147488 | tf_op jit(solution)/shard_map/ppermute | solution.py:41
  54.7 0.0 slice-start.1
  54.8 0.0 collective-permute-done.12.two
  54.8 0.1 sum.18.mine
  54.9 1.3 %collective-permute-start.14 = (f32[128,2048]{1,0:T(8,128)S(1)}, f32[128,2048]{1,0:T(8,128)S(1)}, u32[]{:S(2)}, u32[]{:S(2)}) collective-permute-start(f32[128,2048]{1,0:T(8,128)S(1)} %sum.18.mine), channel_id=1, source_target_pairs={{0,8},{8,0},{16,24},{24,16},{1,9},{9,1},{17,25},{25,17},{2,10},{10... | collective-permute-start | bytes 3145736 | tf_op jit(solution)/shard_map/ppermute | solution.py:41
  56.1 0.5 collective-permute-start.15
  56.7 3.8 %factor.1 = (f32[64,64]{1,0:T(8,128)S(1)}, bf16[1024,384]{1,0:T(8,128)(2,1)S(1)}, bf16[1024,384]{1,0:T(8,128)(2,1)S(1)}) custom-call(f32[32,1152]{1,0:T(8,128)S(1)} %sum.17.refs_0_.message.one, f32[64,1024]{1,0:T(8,128)S(1)} %get-tuple-element.43.refs_0_, f32[64,1024]{1,0:T(8,128)S(1)} %get-tuple-element.44.refs_1_), custom_call_target="tpu_custom_call" | custom-call | tf_op jit(solution)/shard_map/factor/pallas_call | solution.py:232
  60.5 1.1 %collective-permute-done.15.two = f32[32,1152]{1,0:T(8,128)S(1)} collective-permute-done((f32[32,1152]{1,0:T(8,128)S(1)}, f32[32,1152]{1,0:T(8,128)S(1)}, u32[]{:S(2)}, u32[]{:S(2)}) %collective-permute-start.15) | collective-permute-done | bytes 147488 | tf_op jit(solution)/shard_map/ppermute | solution.py:41
  61.6 0.9 %collective-permute-start.16 = (f32[32,1152]{1,0:T(8,128)S(1)}, f32[32,1152]{1,0:T(8,128)S(1)}, u32[]{:S(2)}, u32[]{:S(2)}) collective-permute-start(f32[32,1152]{1,0:T(8,128)S(1)} %sum.19.refs_0_.mine), channel_id=1, source_target_pairs={{0,8},{8,0},{16,24},{24,16},{1,9},{9,1},{17,25},{25,17},{2,10},{10... | collective-permute-start | bytes 442376 | tf_op jit(solution)/shard_map/ppermute | solution.py:41
  62.5 0.0 collective-permute-done.14.other
  62.5 0.0 copy-done.3
  62.5 2.6 %layer.3 = (f32[2,128,2048]{2,1,0:T(8,128)}, f32[2,128,2048]{2,1,0:T(8,128)}, f32[8,128]{1,0:T(8,128)S(1)}) custom-call(s32[1]{0:T(128)} %bitcast.core, f32[128,2048]{1,0:T(8,128)S(1)} %sum.18.mine, f32[128,2048]{1,0:T(8,128)S(1)} %collective-permute-done.14.other, f32[2,128,2048]{2,1,0:T(8,128)S(1)} %copy-done, f32[2,128,2048]{2,1,0:T(8,128)S(1)} %copy-done.3, ...), custom_call_target="tpu_custom_call" | custom-call | tf_op jit(solution)/shard_map/layer/pallas_call | solution.py:368
  65.2 0.0 collective-permute-done.16.other
  65.2 0.0 slice-done
  65.2 0.0 slice-done.1
  65.2 10.0 %final.1 = (f32[2048,1024]{1,0:T(8,128)}, f32[2048,1024]{1,0:T(8,128)}, f32[1,2048,1024]{2,1,0:T(8,128)}) custom-call(s32[1]{0:T(128)} %bitcast.core, f32[32,1152]{1,0:T(8,128)S(1)} %sum.19.refs_0_.mine, f32[32,1152]{1,0:T(8,128)S(1)} %collective-permute-done.16.other, f32[64,64]{1,0:T(8,128)S(1)} %get-tuple-element.45.refs_0_.inverse, ...), custom_call_target="tpu_custom_call" | custom-call | tf_op jit(solution)/shard_map/final/pallas_call | solution.py:281
  (9 shorter events, 0.1 us)
Async XLA Ops:
  0.6 2.9 %collective-permute-start = (f32[1,2,128,1024]{3,2,1,0:T(8,128)}, f32[1,2,128,1024]{3,2,1,0:T(8,128)S(1)}, u32[]{:S(2)}, u32[]{:S(2)}) collective-permute-start(f32[1,2,128,1024]{3,2,1,0:T(8,128)} %copies.5), channel_id=1, source_target_pairs={{0,8},{8,0},{16,24},{24,16},{1,9},{9,1},{17,25},{25,17},{2,10},{10... | collective-permute-start | bytes 3145736 | tf_op jit(solution)/shard_map/ppermute | solution.py:41
  2.4 26.0 %collective-permute-start.11 = (f32[128,2048]{1,0:T(8,128)S(1)}, f32[128,2048]{1,0:T(8,128)S(1)}, u32[]{:S(2)}, u32[]{:S(2)}) collective-permute-start(f32[128,2048]{1,0:T(8,128)S(1)} %away.1.refs_0_), channel_id=1, source_target_pairs={{0,8},{8,0},{16,24},{24,16},{1,9},{9,1},{17,25},{25,17},{2,10},{10... | collective-permute-start | bytes 3145736 | tf_op jit(solution)/shard_map/ppermute | solution.py:41
  4.8 23.5 %copy-start = (f32[2,128,2048]{2,1,0:T(8,128)S(1)}, f32[2,128,2048]{2,1,0:T(8,128)}, u32[]{:S(2)}) copy-start(f32[2,128,2048]{2,1,0:T(8,128)} %weights.11) | copy-start | bytes 6291460
  4.8 23.5 %copy-start.1 = (f32[1,2,128,2048]{3,2,1,0:T(8,128)S(1)}, f32[1,2,128,2048]{3,2,1,0:T(8,128)}, u32[]{:S(2)}) copy-start(f32[1,2,128,2048]{3,2,1,0:T(8,128)} %copies.7) | copy-start | bytes 6291460
  4.9 14.4 %collective-permute-start.1 = (f32[128,1024]{1,0:T(8,128)S(1)}, f32[128,1024]{1,0:T(8,128)S(1)}, u32[]{:S(2)}, u32[]{:S(2)}) collective-permute-start(f32[128,1024]{1,0:T(8,128)S(1)} %both.1.one.refs_0_), channel_id=1, source_target_pairs={{0,16},{8,24},{16,0},{24,8},{1,17},{9,25},{17,1},{25,9},{2,18},{10... | collective-permute-start | bytes 1572872 | tf_op jit(solution)/shard_map/ppermute | solution.py:41
  18.5 1.9 %collective-permute-start.3 = (f32[32,2048]{1,0:T(8,128)S(1)}, f32[32,2048]{1,0:T(8,128)S(1)}, u32[]{:S(2)}, u32[]{:S(2)}) collective-permute-start(f32[32,2048]{1,0:T(8,128)S(1)} %get-tuple-element.32), channel_id=1, source_target_pairs={{0,8},{8,0},{16,24},{24,16},{1,9},{9,1},{17,25},{25,17},{2,10},{10... | collective-permute-start | bytes 786440 | tf_op jit(solution)/shard_map/ppermute | solution.py:41
  20.5 4.8 %collective-permute-start.5 = (f32[32,1024]{1,0:T(8,128)S(1)}, f32[32,1024]{1,0:T(8,128)S(1)}, u32[]{:S(2)}, u32[]{:S(2)}) collective-permute-start(f32[32,1024]{1,0:T(8,128)S(1)} %get-tuple-element.34.one), channel_id=1, source_target_pairs={{0,16},{8,24},{16,0},{24,8},{1,17},{9,25},{17,1},{25,9},{2,18},{10... | collective-permute-start | bytes 393224 | tf_op jit(solution)/shard_map/ppermute | solution.py:41
  20.6 7.5 %collective-permute-start.4 = (f32[32,1024]{1,0:T(8,128)S(1)}, f32[32,1024]{1,0:T(8,128)S(1)}, u32[]{:S(2)}, u32[]{:S(2)}) collective-permute-start(f32[32,1024]{1,0:T(8,128)S(1)} %get-tuple-element.33.one), channel_id=1, source_target_pairs={{0,16},{8,24},{16,0},{24,8},{1,17},{9,25},{17,1},{25,9},{2,18},{10... | collective-permute-start | bytes 393224 | tf_op jit(solution)/shard_map/ppermute | solution.py:41
  25.3 3.1 %collective-permute-start.6 = (f32[32,1024]{1,0:T(8,128)S(1)}, f32[32,1024]{1,0:T(8,128)S(1)}, u32[]{:S(2)}, u32[]{:S(2)}) collective-permute-start(f32[32,1024]{1,0:T(8,128)S(1)} %sum.12.mine.refs_0_), channel_id=1, source_target_pairs={{0,8},{8,0},{16,24},{24,16},{1,9},{9,1},{17,25},{25,17},{2,10},{10... | collective-permute-start | bytes 393224 | tf_op jit(solution)/shard_map/ppermute | solution.py:41
  28.6 26.2 %collective-permute-start.12 = (f32[128,2048]{1,0:T(8,128)S(1)}, f32[128,2048]{1,0:T(8,128)S(1)}, u32[]{:S(2)}, u32[]{:S(2)}) collective-permute-start(f32[128,2048]{1,0:T(8,128)S(1)} %term.1.one), channel_id=1, source_target_pairs={{0,16},{8,24},{16,0},{24,8},{1,17},{9,25},{17,1},{25,9},{2,18},{10... | collective-permute-start | bytes 3145736 | tf_op jit(solution)/shard_map/ppermute | solution.py:41
  29.3 2.3 %collective-permute-start.7 = (f32[32,1024]{1,0:T(8,128)S(1)}, f32[32,1024]{1,0:T(8,128)S(1)}, u32[]{:S(2)}, u32[]{:S(2)}) collective-permute-start(f32[32,1024]{1,0:T(8,128)S(1)} %sum.13.mine.refs_1_), channel_id=1, source_target_pairs={{0,8},{8,0},{16,24},{24,16},{1,9},{9,1},{17,25},{25,17},{2,10},{10... | collective-permute-start | bytes 393224 | tf_op jit(solution)/shard_map/ppermute | solution.py:41
  29.9 17.6 %copy-start.2 = (f32[2,128,1024]{2,1,0:T(8,128)S(1)}, f32[2,128,1024]{2,1,0:T(8,128)}, u32[]{:S(2)}) copy-start(f32[2,128,1024]{2,1,0:T(8,128)} %weights.9) | copy-start | bytes 3145732
  29.9 17.6 %copy-start.4 = (f32[2,128,1024]{2,1,0:T(8,128)S(1)}, f32[2,128,1024]{2,1,0:T(8,128)}, u32[]{:S(2)}) copy-start(f32[2,128,1024]{2,1,0:T(8,128)} %moment.3) | copy-start | bytes 3145732
  31.6 30.9 %copy-start.3 = (f32[2,128,2048]{2,1,0:T(8,128)S(1)}, f32[2,128,2048]{2,1,0:T(8,128)}, u32[]{:S(2)}) copy-start(f32[2,128,2048]{2,1,0:T(8,128)} %moment.4) | copy-start | bytes 6291460
  33.4 31.8 %slice-start = ((s8[8388608]{0:T(1024)(128)(4,1)}), s8[4194304]{0:T(1024)(128)(4,1)S(1)}, s32[]{:S(2)}) async-start(s8[8388608]{0:T(1024)(128)(4,1)} %bitcast.1), calls=%async_computation | async-start | bytes 8388608
  33.4 1.4 %collective-permute-start.8 = (f32[32,1152]{1,0:T(8,128)S(1)}, f32[32,1152]{1,0:T(8,128)S(1)}, u32[]{:S(2)}, u32[]{:S(2)}) collective-permute-start(f32[32,1152]{1,0:T(8,128)S(1)} %get-tuple-element.39), channel_id=1, source_target_pairs={{0,8},{8,0},{16,24},{24,16},{1,9},{9,1},{17,25},{25,17},{2,10},{10... | collective-permute-start | bytes 442376 | tf_op jit(solution)/shard_map/ppermute | solution.py:41
  33.4 14.1 %collective-permute-start.2 = (f32[128,1024]{1,0:T(8,128)S(1)}, f32[128,1024]{1,0:T(8,128)S(1)}, u32[]{:S(2)}, u32[]{:S(2)}) collective-permute-start(f32[128,1024]{1,0:T(8,128)S(1)} %sum.10.refs_0_.mine), channel_id=1, source_target_pairs={{0,8},{8,0},{16,24},{24,16},{1,9},{9,1},{17,25},{25,17},{2,10},{10... | collective-permute-start | bytes 1572872 | tf_op jit(solution)/shard_map/ppermute | solution.py:41
  34.8 5.9 %collective-permute-start.9 = (f32[32,1152]{1,0:T(8,128)S(1)}, f32[32,1152]{1,0:T(8,128)S(1)}, u32[]{:S(2)}, u32[]{:S(2)}) collective-permute-start(f32[32,1152]{1,0:T(8,128)S(1)} %sum.14.one), channel_id=1, source_target_pairs={{0,1},{1,0},{2,3},{3,2},{4,5},{5,4},{6,7},{7,6},{8,9},{9,8},{10,11... | collective-permute-start | bytes 442376 | tf_op jit(solution)/shard_map/ppermute | solution.py:41
  40.7 4.8 %collective-permute-start.10 = (f32[32,1152]{1,0:T(8,128)S(1)}, f32[32,1152]{1,0:T(8,128)S(1)}, u32[]{:S(2)}, u32[]{:S(2)}) collective-permute-start(f32[32,1152]{1,0:T(8,128)S(1)} %sum.15.one), channel_id=1, source_target_pairs={{0,2},{1,3},{2,0},{3,1},{4,6},{5,7},{6,4},{7,5},{8,10},{9,11},{10,... | collective-permute-start | bytes 442376 | tf_op jit(solution)/shard_map/ppermute | solution.py:41
  45.5 9.2 %collective-permute-start.13 = (f32[32,1152]{1,0:T(8,128)S(1)}, f32[32,1152]{1,0:T(8,128)S(1)}, u32[]{:S(2)}, u32[]{:S(2)}) collective-permute-start(f32[32,1152]{1,0:T(8,128)S(1)} %sum.16.refs_0_.one), channel_id=1, source_target_pairs={{0,4},{1,5},{2,6},{3,7},{4,0},{5,1},{6,2},{7,3},{8,12},{9,13},{10,... | collective-permute-start | bytes 442376 | tf_op jit(solution)/shard_map/ppermute | solution.py:41
  54.7 10.4 %slice-start.1 = ((s8[8388608]{0:T(1024)(128)(4,1)}), s8[4194304]{0:T(1024)(128)(4,1)S(1)}, s32[]{:S(2)}) async-start(s8[8388608]{0:T(1024)(128)(4,1)} %bitcast.1), calls=%async_computation.1 | async-start | bytes 8388608
  54.9 7.6 %collective-permute-start.14 = (f32[128,2048]{1,0:T(8,128)S(1)}, f32[128,2048]{1,0:T(8,128)S(1)}, u32[]{:S(2)}, u32[]{:S(2)}) collective-permute-start(f32[128,2048]{1,0:T(8,128)S(1)} %sum.18.mine), channel_id=1, source_target_pairs={{0,8},{8,0},{16,24},{24,16},{1,9},{9,1},{17,25},{25,17},{2,10},{10... | collective-permute-start | bytes 3145736 | tf_op jit(solution)/shard_map/ppermute | solution.py:41
  56.1 5.4 %collective-permute-start.15 = (f32[32,1152]{1,0:T(8,128)S(1)}, f32[32,1152]{1,0:T(8,128)S(1)}, u32[]{:S(2)}, u32[]{:S(2)}) collective-permute-start(f32[32,1152]{1,0:T(8,128)S(1)} %sum.17.refs_0_.message.one), channel_id=1, source_target_pairs={{0,16},{8,24},{16,0},{24,8},{1,17},{9,25},{17,1},{25,9},{2,18},{10... | collective-permute-start | bytes 442376 | tf_op jit(solution)/shard_map/ppermute | solution.py:41
  61.6 3.6 %collective-permute-start.16 = (f32[32,1152]{1,0:T(8,128)S(1)}, f32[32,1152]{1,0:T(8,128)S(1)}, u32[]{:S(2)}, u32[]{:S(2)}) collective-permute-start(f32[32,1152]{1,0:T(8,128)S(1)} %sum.19.refs_0_.mine), channel_id=1, source_target_pairs={{0,8},{8,0},{16,24},{24,16},{1,9},{9,1},{17,25},{25,17},{2,10},{10... | collective-permute-start | bytes 442376 | tf_op jit(solution)/shard_map/ppermute | solution.py:41

commit v5 on v4

--- a/solution.py
+++ b/solution.py
@@ -49,6 +49,28 @@
     return value
 
 
+def part_kernel(one, two, *refs):
+    left, right = refs[-2:]
+    width = left.shape[1]
+    left[...] = one[:, :width] + two[:, :width]
+    right[...] = one[:, width:] + two[:, width:]
+
+
+def part_call(one, two, after, width):
+    rows, total = one.shape
+    return pl.pallas_call(
+        part_kernel,
+        in_specs=[VMEM] * 2 + [ANY] * len(after),
+        out_specs=[VMEM] * 2,
+        out_shape=[
+            jax.ShapeDtypeStruct((rows, width), jnp.float32),
+            jax.ShapeDtypeStruct((rows, total - width), jnp.float32),
+        ],
+        compiler_params=pltpu.CompilerParams(vmem_limit_bytes=8 * MIB),
+        name="part",
+    )(one, two, *after)
+
+
 def sum_over_chips(value, after):
     bit = 2
     while bit < lax.axis_size("replica"):
@@ -75,7 +97,7 @@
 
 
 def left_kernel(chunk_after, core, weights, copies, error, warm, *refs):
-    corrected, held, away, kept, parts = refs[chunk_after:]
+    corrected, away, kept, parts = refs[chunk_after:]
     step = pl.program_id(0)
     rows = weights.shape[0]
     half = away.shape[0]
@@ -90,7 +112,6 @@
     value = weights[...] - copies[0] + error[0]
     here = pl.ds(pl.multiple_of(step * rows, rows), rows)
     corrected[here, :] = value
-    held[here, :] = weights[...]
     left = stacked_product(parts[...], value, ((1,), (1,)))
     away[...] = left[:half]
     kept[...] = left[half:]
@@ -114,12 +135,10 @@
         + [ANY] * len(after),
         out_specs=[
             VMEM,
-            VMEM,
             pl.BlockSpec((rank // 2, block), lambda i: (0, i)),
             pl.BlockSpec((rank // 2, block), lambda i: (0, i)),
         ],
         out_shape=[
-            pltpu.VMEM((rows, width), jnp.float32),
             pltpu.VMEM((rows, width), jnp.float32),
             jax.ShapeDtypeStruct((rank // 2, rows), jnp.float32),
             jax.ShapeDtypeStruct((rank // 2, rows), jnp.float32),
@@ -173,12 +192,12 @@
     )(core, mine, other, in_vmem(corrected), *before)
 
 
-def factor_kernel(width, message, *refs):
+def factor_kernel(message, *refs):
     chunks = (len(refs) - 1) // 2
     left, inverse, basis = refs[:chunks], refs[chunks], refs[chunks + 1 :]
     half = message.shape[0]
     rank = 2 * half
-    pair = message[:, width:]
+    pair = message[...]
     gram = jnp.concatenate([pair[:, :rank], pair[:, rank:]], axis=0)
     eye = jnp.where(
         lax.broadcasted_iota(jnp.int32, (rank, rank), 0) == lax.broadcasted_iota(jnp.int32, (rank, rank), 1), 1.0, 0.0
@@ -226,11 +245,11 @@
         basis[chunk][...] = jnp.concatenate([high, high, middle, high, low, middle], axis=1)
 
 
-def factor_call(message, left, width):
+def factor_call(message, left):
     half = message.shape[0]
     rank = 2 * half
     return pl.pallas_call(
-        functools.partial(factor_kernel, width),
+        factor_kernel,
         in_specs=[VMEM] * (1 + len(left)),
         out_specs=[VMEM] * (1 + len(left)),
         out_shape=[jax.ShapeDtypeStruct((rank, rank), jnp.float32)]
@@ -392,14 +411,14 @@
     scale = 1 / replicas
     rank, width = warm_start.shape
     rows = embed_weights.shape[0]
-    core = jnp.reshape(lax.axis_index("replica") % 2, (1,)).astype(jnp.int32)
+    core = jnp.reshape(lax.axis_index("replica") & 1, (1,)).astype(jnp.int32)
 
     square_received = swap(square_copies, "replica", 1)
     broad_away = half_call(away_kernel, True, core, broad_weights, (broad_copies,), ())
     square_half = half_call(both_kernel, False, core, square_weights, (square_copies, square_received), (broad_away,))
     broad_received = swap(broad_away, "replica", 1)
     chunks = 2 if rows % 512 == 0 else 1
-    corrected, held, away, kept = left_call(
+    corrected, away, kept = left_call(
         core, embed_weights, embed_copies, embed_error, warm_start, (square_half,), 0, rows, math.gcd(rows, 512)
     )
     square_half = sum_over_chips(square_half, ())
@@ -421,18 +440,16 @@
     message = sum_call(kept, swap(away, "replica", 1), ())
     inner = lax.axis_size("inner")
     bit = 1
+    while 2 * bit < inner:
+        message = sum_call(message, swap(message, "inner", bit), ())
+        bit *= 2
     square_other = swap(square_half, "replica", 1)
-    while bit < inner:
-        received = swap(message, "inner", bit)
-        after = ()
-        if 2 * bit >= inner:
-            square_updated, square_velocity, mark = layer_call(
-                core, square_half, square_other, square_weights, square_moment, (message,), scale
-            )
-            after = (mark,)
-        message = sum_call(message, received, after)
-        bit *= 2
-    inverse, *basis = factor_call(message, left, width)
+    received = swap(message, "inner", bit)
+    square_updated, square_velocity, mark = layer_call(
+        core, square_half, square_other, square_weights, square_moment, (message,), scale
+    )
+    message, gram = part_call(message, received, (mark,), width)
+    inverse, *basis = factor_call(gram, left)
     right_half = sum_over_chips(message, (inverse,))
     broad_half = sum_over_chips(broad_half, (message,))
     broad_other = swap(broad_half, "replica", 1)
@@ -441,7 +458,7 @@
     )
     right_other = swap(right_half, "replica", 1)
     embed_updated, embed_velocity, embed_carried = final_call(
-        core, right_half, right_other, inverse, embed_moment, held, corrected, basis, (mark,), scale, math.gcd(rows, 512)
+        core, right_half, right_other, inverse, embed_moment, embed_weights, corrected, basis, (mark,), scale, math.gcd(rows, 512)
     )
     return (
         square_updated,

time: 75.3 us -> 74.3 us (0.987)
  waiting for transfers between devices: 21.2 us -> 18.8 us
  starting transfers between devices: 17.1 us -> 18.7 us
    ppermute x17, waiting for transfers between devices: 21.2 us -> 18.8 us  [swap(): lax.ppermute(value, axis, [(i, i ^ bit) for i in range(lax.axis_size(axis...]
    ppermute x17, starting transfers between devices: 17.1 us -> 18.7 us  [swap(): lax.ppermute(value, axis, [(i, i ^ bit) for i in range(lax.axis_size(axis...]
    pallas_call x1 -> x2, Pallas kernels: 3.78 us -> 3.79 us  [the longest x1 3.78 us: factor_call(): pl.pallas_call(factor_kernel, in_specs=[VMEM] * (1 + len(left)), out_spec...]
  transfers between devices with their start and end apart: 17 -> 17, of which waited for: 10 -> 11; matrix products, arithmetic and copies ran while one was open for 0% -> 0% of each run, Pallas kernels for 34% -> 34%
where the time goes in v5:
time: 74.3 us; the launch traced here: 74.1 us
  Pallas kernels  35.7 us (48%)
  waiting for transfers between devices  18.8 us (25%)
  starting transfers between devices  18.7 us (25%)
  between operations  0.84 us (1%)
    ppermute x17, waiting for transfers between devices, swap(): lax.ppermute(value, axis, [(i, i ^ bit) for i in range(lax.axis_size(axis...  18.8 us
    ppermute x17, starting transfers between devices, swap(): lax.ppermute(value, axis, [(i, i ^ bit) for i in range(lax.axis_size(axis...  18.7 us
    pallas_call x1, Pallas kernels, left_call(): pl.pallas_call(functools.partial(left_kernel, len(after)), grid=(rows //...  11 us
    pallas_call x1, Pallas kernels, final_call(): pl.pallas_call(functools.partial(final_kernel, scale, chunks), grid=(rows...  9.96 us
    pallas_call x2, Pallas kernels, layer_call(): pl.pallas_call(functools.partial(layer_kernel, scale), in_specs=[SMEM] +...  4.28 us
    pallas_call x1, Pallas kernels, factor_call(): pl.pallas_call(factor_kernel, in_specs=[VMEM] * (1 + len(left)), out_spec...  3.78 us
    pallas_call x2, Pallas kernels, right_call(): pl.pallas_call(functools.partial(right_kernel, scale, block, chunk), in_s...  3.4 us
    pallas_call x2, Pallas kernels, half_call(): pl.pallas_call(kernel, grid_spec=pltpu.PrefetchScalarGridSpec(num_scalar_...  2.85 us
  transfers between devices with their start and end apart: 17, of which 11 were waited for; matrix products, arithmetic and copies ran while one was open for 0% of the time, Pallas kernels for 34%

profile of v5, /device:TPU:1, one launch (start us, length us, event | category | flops | bytes accessed | tf_op | source)
XLA Modules:
  0.0 74.1 jit_solution(13534315007706974335)
XLA Ops:
  0.6 0.1 collective-permute-start
  0.8 1.6 %away.1.refs_0_ = f32[128,2048]{1,0:T(8,128)S(1)} custom-call(s32[1]{0:T(128)} %bitcast.core, f32[2,128,2048]{2,1,0:T(8,128)} %weights.12, f32[1,2,128,2048]{3,2,1,0:T(8,128)} %copies.7), custom_call_target="tpu_custom_call" | custom-call | tf_op jit(solution)/shard_map/away/pallas_call | solution.py:349
  2.4 0.5 collective-permute-start.11
  2.9 0.7 collective-permute-done.received
  3.6 1.3 %both.1.one.refs_0_ = f32[128,1024]{1,0:T(8,128)S(1)} custom-call(s32[1]{0:T(128)} %bitcast.core, f32[2,128,1024]{2,1,0:T(8,128)} %weights.10, f32[1,2,128,1024]{3,2,1,0:T(8,128)} %copies.5, f32[1,2,128,1024]{3,2,1,0:T(8,128)S(1)} %collective-permute-done.received, f32[128,2048]{1,0:T(8,128)S(1)} %away.1.refs_0_), custom_call_target="tpu_custom_call" | custom-call | tf_op jit(solution)/shard_map/both/pallas_call | solution.py:349
  4.8 0.0 copy-start
  4.8 0.0 copy-start.1
  4.9 2.4 %collective-permute-start.1 = (f32[128,1024]{1,0:T(8,128)S(1)}, f32[128,1024]{1,0:T(8,128)S(1)}, u32[]{:S(2)}, u32[]{:S(2)}) collective-permute-start(f32[128,1024]{1,0:T(8,128)S(1)} %both.1.one.refs_0_), channel_id=1, source_target_pairs={{0,16},{8,24},{16,0},{24,8},{1,17},{9,25},{17,1},{25,9},{2,18},{10... | collective-permute-start | bytes 1572872 | tf_op jit(solution)/shard_map/ppermute | solution.py:41
  7.3 11.0 %left.1 = (f32[2048,1024]{1,0:T(8,128)S(1)}, f32[32,2048]{1,0:T(8,128)S(1)}, f32[32,2048]{1,0:T(8,128)S(1)}) custom-call(s32[1]{0:T(128)} %bitcast.core, f32[2048,1024]{1,0:T(8,128)} %weights.13, f32[1,2048,1024]{2,1,0:T(8,128)} %copies.6, f32[1,2048,1024]{2,1,0:T(8,128)} %error.1, f32[64,1024]{1,0:T(8,128)} %warm.1, f32[128,1024]{1,0:T(8,128)S(1)} %both.1.one.refs_0_), custom_call_target="tpu_custom_call" | custom-call | tf_op jit(solution)/shard_map/left/pallas_call | solution.py:125
  18.3 0.7 collective-permute-start.3
  19.0 0.3 collective-permute-done.1.two
  19.3 0.1 sum.9.refs_0_.mine
  19.3 0.8 %collective-permute-done.3.two = f32[32,2048]{1,0:T(8,128)S(1)} collective-permute-done((f32[32,2048]{1,0:T(8,128)S(1)}, f32[32,2048]{1,0:T(8,128)S(1)}, u32[]{:S(2)}, u32[]{:S(2)}) %collective-permute-start.3) | collective-permute-done | bytes 262176 | tf_op jit(solution)/shard_map/ppermute | solution.py:41
  20.2 0.4 collective-permute-start.5
  20.6 1.1 %collective-permute-start.4 = (f32[32,1024]{1,0:T(8,128)S(1)}, f32[32,1024]{1,0:T(8,128)S(1)}, u32[]{:S(2)}, u32[]{:S(2)}) collective-permute-start(f32[32,1024]{1,0:T(8,128)S(1)} %get-tuple-element.34.one), channel_id=1, source_target_pairs={{0,16},{8,24},{16,0},{24,8},{1,17},{9,25},{17,1},{25,9},{2,18},{10... | collective-permute-start | bytes 393224 | tf_op jit(solution)/shard_map/ppermute | solution.py:41
  21.7 3.2 %collective-permute-done.5.two = f32[32,1024]{1,0:T(8,128)S(1)} collective-permute-done((f32[32,1024]{1,0:T(8,128)S(1)}, f32[32,1024]{1,0:T(8,128)S(1)}, u32[]{:S(2)}, u32[]{:S(2)}) %collective-permute-start.5) | collective-permute-done | bytes 131104 | tf_op jit(solution)/shard_map/ppermute | solution.py:41
  25.0 2.1 %collective-permute-start.6 = (f32[32,1024]{1,0:T(8,128)S(1)}, f32[32,1024]{1,0:T(8,128)S(1)}, u32[]{:S(2)}, u32[]{:S(2)}) collective-permute-start(f32[32,1024]{1,0:T(8,128)S(1)} %sum.11.mine.refs_0_), channel_id=1, source_target_pairs={{0,8},{8,0},{16,24},{24,16},{1,9},{9,1},{17,25},{25,17},{2,10},{10... | collective-permute-start | bytes 393224 | tf_op jit(solution)/shard_map/ppermute | solution.py:41
  27.0 0.7 collective-permute-done.4.two
  27.8 0.3 collective-permute-done.6.refs_0_.other
  28.1 0.0 collective-permute-done.11.received
  28.1 0.0 copy-done
  28.1 0.0 copy-done.1
  28.1 0.2 term.1.one
  28.2 1.0 %collective-permute-start.12 = (f32[128,2048]{1,0:T(8,128)S(1)}, f32[128,2048]{1,0:T(8,128)S(1)}, u32[]{:S(2)}, u32[]{:S(2)}) collective-permute-start(f32[128,2048]{1,0:T(8,128)S(1)} %term.1.one), channel_id=1, source_target_pairs={{0,16},{8,24},{16,0},{24,8},{1,17},{9,25},{17,1},{25,9},{2,18},{10... | collective-permute-start | bytes 3145736 | tf_op jit(solution)/shard_map/ppermute | solution.py:41
  29.2 0.6 collective-permute-start.7
  29.9 0.0 copy-start.2
  29.9 0.0 copy-start.4
  29.9 0.0 slice-start.2
  29.9 1.7 %right.2 = (f32[32,1152]{1,0:T(8,128)S(1)}, f32[32,1152]{1,0:T(8,128)S(1)}, f32[64,1024]{1,0:T(8,128)S(1)}) custom-call(s32[1]{0:T(128)} %bitcast.core, f32[32,1024]{1,0:T(8,128)S(1)} %sum.11.mine.refs_0_, f32[32,1024]{1,0:T(8,128)S(1)} %collective-permute-done.6.refs_0_.other, f32[2048,1024]{1,0:T(8,128)S(1)} %get-tuple-element.36.corrected), custom_call_target="tpu_custom_call" | custom-call | tf_op jit(solution)/shard_map/right/pallas_call | solution.py:185
  31.6 0.0 collective-permute-done.7.other
  31.6 0.0 copy-start.3
  31.6 0.0 slice-start.3
  31.6 1.7 %right.3 = (f32[32,1152]{1,0:T(8,128)S(1)}, f32[32,1152]{1,0:T(8,128)S(1)}, f32[64,1024]{1,0:T(8,128)S(1)}) custom-call(s32[1]{0:T(128)} %bitcast.core, f32[32,1024]{1,0:T(8,128)S(1)} %sum.12.mine.refs_1_, f32[32,1024]{1,0:T(8,128)S(1)} %collective-permute-done.7.other, f32[2048,1024]{1,0:T(8,128)S(1)} %get-tuple-element.36.corrected, ...), custom_call_target="tpu_custom_call" | custom-call | tf_op jit(solution)/shard_map/right/pallas_call | solution.py:185
  33.3 0.0 slice-start
  33.3 0.1 collective-permute-start.8
  33.4 0.5 collective-permute-start.2
  33.9 0.9 %collective-permute-done.8.two = f32[32,1152]{1,0:T(8,128)S(1)} collective-permute-done((f32[32,1152]{1,0:T(8,128)S(1)}, f32[32,1152]{1,0:T(8,128)S(1)}, u32[]{:S(2)}, u32[]{:S(2)}) %collective-permute-start.8) | collective-permute-done | bytes 147488 | tf_op jit(solution)/shard_map/ppermute | solution.py:41
  34.8 1.5 %collective-permute-start.9 = (f32[32,1152]{1,0:T(8,128)S(1)}, f32[32,1152]{1,0:T(8,128)S(1)}, u32[]{:S(2)}, u32[]{:S(2)}) collective-permute-start(f32[32,1152]{1,0:T(8,128)S(1)} %sum.13.one), channel_id=1, source_target_pairs={{0,1},{1,0},{2,3},{3,2},{4,5},{5,4},{6,7},{7,6},{8,9},{9,8},{10,11... | collective-permute-start | bytes 442376 | tf_op jit(solution)/shard_map/ppermute | solution.py:41
  36.3 3.9 %collective-permute-done.9.two = f32[32,1152]{1,0:T(8,128)S(1)} collective-permute-done((f32[32,1152]{1,0:T(8,128)S(1)}, f32[32,1152]{1,0:T(8,128)S(1)}, u32[]{:S(2)}, u32[]{:S(2)}) %collective-permute-start.9) | collective-permute-done | bytes 147488 | tf_op jit(solution)/shard_map/ppermute | solution.py:41
  40.2 1.6 %collective-permute-start.10 = (f32[32,1152]{1,0:T(8,128)S(1)}, f32[32,1152]{1,0:T(8,128)S(1)}, u32[]{:S(2)}, u32[]{:S(2)}) collective-permute-start(f32[32,1152]{1,0:T(8,128)S(1)} %sum.14.one), channel_id=1, source_target_pairs={{0,2},{1,3},{2,0},{3,1},{4,6},{5,7},{6,4},{7,5},{8,10},{9,11},{10,... | collective-permute-start | bytes 442376 | tf_op jit(solution)/shard_map/ppermute | solution.py:41
  41.8 3.0 %collective-permute-done.10.two = f32[32,1152]{1,0:T(8,128)S(1)} collective-permute-done((f32[32,1152]{1,0:T(8,128)S(1)}, f32[32,1152]{1,0:T(8,128)S(1)}, u32[]{:S(2)}, u32[]{:S(2)}) %collective-permute-start.10) | collective-permute-done | bytes 147488 | tf_op jit(solution)/shard_map/ppermute | solution.py:41
  44.8 2.5 %collective-permute-start.13 = (f32[32,1152]{1,0:T(8,128)S(1)}, f32[32,1152]{1,0:T(8,128)S(1)}, u32[]{:S(2)}, u32[]{:S(2)}) collective-permute-start(f32[32,1152]{1,0:T(8,128)S(1)} %sum.15.refs_0_.one), channel_id=1, source_target_pairs={{0,4},{1,5},{2,6},{3,7},{4,0},{5,1},{6,2},{7,3},{8,12},{9,13},{10,... | collective-permute-start | bytes 442376 | tf_op jit(solution)/shard_map/ppermute | solution.py:41
  47.2 0.0 collective-permute-done.2.other
  47.2 0.0 copy-done.2
  47.2 0.0 copy-done.4
  47.2 1.6 %layer.2 = (f32[2,128,1024]{2,1,0:T(8,128)}, f32[2,128,1024]{2,1,0:T(8,128)}, f32[8,128]{1,0:T(8,128)S(1)}) custom-call(s32[1]{0:T(128)} %bitcast.core, f32[128,1024]{1,0:T(8,128)S(1)} %sum.9.refs_0_.mine, f32[128,1024]{1,0:T(8,128)S(1)} %collective-permute-done.2.other, f32[2,128,1024]{2,1,0:T(8,128)S(1)} %copy-done.2, f32[2,128,1024]{2,1,0:T(8,128)S(1)} %copy-done.4, ...), custom_call_target="tpu_custom_call" | custom-call | tf_op jit(solution)/shard_map/layer/pallas_call | solution.py:387
  48.9 4.7 %collective-permute-done.13.two = f32[32,1152]{1,0:T(8,128)S(1)} collective-permute-done((f32[32,1152]{1,0:T(8,128)S(1)}, f32[32,1152]{1,0:T(8,128)S(1)}, u32[]{:S(2)}, u32[]{:S(2)}) %collective-permute-start.13) | collective-permute-done | bytes 147488 | tf_op jit(solution)/shard_map/ppermute | solution.py:41
  53.6 0.0 collective-permute-done.12.two
  53.6 0.0 slice-start.1
  53.6 0.1 sum.16.mine
  53.7 1.7 %collective-permute-start.14 = (f32[128,2048]{1,0:T(8,128)S(1)}, f32[128,2048]{1,0:T(8,128)S(1)}, u32[]{:S(2)}, u32[]{:S(2)}) collective-permute-start(f32[128,2048]{1,0:T(8,128)S(1)} %sum.16.mine), channel_id=1, source_target_pairs={{0,8},{8,0},{16,24},{24,16},{1,9},{9,1},{17,25},{25,17},{2,10},{10... | collective-permute-start | bytes 3145736 | tf_op jit(solution)/shard_map/ppermute | solution.py:41
  55.4 0.9 %collective-permute-start.15 = (f32[32,1024]{1,0:T(8,128)S(1)}, f32[32,1024]{1,0:T(8,128)S(1)}, u32[]{:S(2)}, u32[]{:S(2)}) collective-permute-start(f32[32,1024]{1,0:T(8,128)S(1)} %get-tuple-element.44.refs_0_.one), channel_id=1, source_target_pairs={{0,16},{8,24},{16,0},{24,8},{1,17},{9,25},{17,1},{25,9},{2,18},{10... | collective-permute-start | bytes 393224 | tf_op jit(solution)/shard_map/ppermute | solution.py:41
  56.4 3.8 %factor.1 = (f32[64,64]{1,0:T(8,128)S(1)}, bf16[1024,384]{1,0:T(8,128)(2,1)S(1)}, bf16[1024,384]{1,0:T(8,128)(2,1)S(1)}) custom-call(f32[32,128]{1,0:T(8,128)S(1)} %get-tuple-element.45.message, f32[64,1024]{1,0:T(8,128)S(1)} %get-tuple-element.46.refs_0_, f32[64,1024]{1,0:T(8,128)S(1)} %get-tuple-element.47.refs_1_), custom_call_target="tpu_custom_call" | custom-call | tf_op jit(solution)/shard_map/factor/pallas_call | solution.py:251
  60.2 0.4 collective-permute-done.15.two
  60.5 0.9 %collective-permute-start.16 = (f32[32,1024]{1,0:T(8,128)S(1)}, f32[32,1024]{1,0:T(8,128)S(1)}, u32[]{:S(2)}, u32[]{:S(2)}) collective-permute-start(f32[32,1024]{1,0:T(8,128)S(1)} %sum.17.refs_0_.mine), channel_id=1, source_target_pairs={{0,8},{8,0},{16,24},{24,16},{1,9},{9,1},{17,25},{25,17},{2,10},{10... | collective-permute-start | bytes 393224 | tf_op jit(solution)/shard_map/ppermute | solution.py:41
  61.4 0.0 collective-permute-done.14.other
  61.4 0.0 copy-done.3
  61.4 2.6 %layer.3 = (f32[2,128,2048]{2,1,0:T(8,128)}, f32[2,128,2048]{2,1,0:T(8,128)}, f32[8,128]{1,0:T(8,128)S(1)}) custom-call(s32[1]{0:T(128)} %bitcast.core, f32[128,2048]{1,0:T(8,128)S(1)} %sum.16.mine, f32[128,2048]{1,0:T(8,128)S(1)} %collective-permute-done.14.other, f32[2,128,2048]{2,1,0:T(8,128)S(1)} %copy-done, f32[2,128,2048]{2,1,0:T(8,128)S(1)} %copy-done.3, ...), custom_call_target="tpu_custom_call" | custom-call | tf_op jit(solution)/shard_map/layer/pallas_call | solution.py:387
  64.1 0.0 collective-permute-done.16.other
  64.1 0.0 slice-done.2
  64.1 0.0 slice-done.3
  64.1 0.0 slice-done
  64.1 0.0 slice-done.1
  64.1 10.0 %final.1 = (f32[2048,1024]{1,0:T(8,128)}, f32[2048,1024]{1,0:T(8,128)}, f32[1,2048,1024]{2,1,0:T(8,128)}) custom-call(s32[1]{0:T(128)} %bitcast.core, f32[32,1024]{1,0:T(8,128)S(1)} %sum.17.refs_0_.mine, f32[32,1024]{1,0:T(8,128)S(1)} %collective-permute-done.16.other, f32[64,64]{1,0:T(8,128)S(1)} %get-tuple-element.48.refs_0_.inverse, ...), custom_call_target="tpu_custom_call" | custom-call | tf_op jit(solution)/shard_map/final/pallas_call | solution.py:300
  (10 shorter events, 0.1 us)
Async XLA Ops:
  0.6 2.9 %collective-permute-start = (f32[1,2,128,1024]{3,2,1,0:T(8,128)}, f32[1,2,128,1024]{3,2,1,0:T(8,128)S(1)}, u32[]{:S(2)}, u32[]{:S(2)}) collective-permute-start(f32[1,2,128,1024]{3,2,1,0:T(8,128)} %copies.5), channel_id=1, source_target_pairs={{0,8},{8,0},{16,24},{24,16},{1,9},{9,1},{17,25},{25,17},{2,10},{10... | collective-permute-start | bytes 3145736 | tf_op jit(solution)/shard_map/ppermute | solution.py:41
  2.4 25.7 %collective-permute-start.11 = (f32[128,2048]{1,0:T(8,128)S(1)}, f32[128,2048]{1,0:T(8,128)S(1)}, u32[]{:S(2)}, u32[]{:S(2)}) collective-permute-start(f32[128,2048]{1,0:T(8,128)S(1)} %away.1.refs_0_), channel_id=1, source_target_pairs={{0,8},{8,0},{16,24},{24,16},{1,9},{9,1},{17,25},{25,17},{2,10},{10... | collective-permute-start | bytes 3145736 | tf_op jit(solution)/shard_map/ppermute | solution.py:41
  4.8 23.2 %copy-start = (f32[2,128,2048]{2,1,0:T(8,128)S(1)}, f32[2,128,2048]{2,1,0:T(8,128)}, u32[]{:S(2)}) copy-start(f32[2,128,2048]{2,1,0:T(8,128)} %weights.12) | copy-start | bytes 6291460
  4.8 23.2 %copy-start.1 = (f32[1,2,128,2048]{3,2,1,0:T(8,128)S(1)}, f32[1,2,128,2048]{3,2,1,0:T(8,128)}, u32[]{:S(2)}) copy-start(f32[1,2,128,2048]{3,2,1,0:T(8,128)} %copies.7) | copy-start | bytes 6291460
  4.9 14.4 %collective-permute-start.1 = (f32[128,1024]{1,0:T(8,128)S(1)}, f32[128,1024]{1,0:T(8,128)S(1)}, u32[]{:S(2)}, u32[]{:S(2)}) collective-permute-start(f32[128,1024]{1,0:T(8,128)S(1)} %both.1.one.refs_0_), channel_id=1, source_target_pairs={{0,16},{8,24},{16,0},{24,8},{1,17},{9,25},{17,1},{25,9},{2,18},{10... | collective-permute-start | bytes 1572872 | tf_op jit(solution)/shard_map/ppermute | solution.py:41
  18.3 1.9 %collective-permute-start.3 = (f32[32,2048]{1,0:T(8,128)S(1)}, f32[32,2048]{1,0:T(8,128)S(1)}, u32[]{:S(2)}, u32[]{:S(2)}) collective-permute-start(f32[32,2048]{1,0:T(8,128)S(1)} %get-tuple-element.33), channel_id=1, source_target_pairs={{0,8},{8,0},{16,24},{24,16},{1,9},{9,1},{17,25},{25,17},{2,10},{10... | collective-permute-start | bytes 786440 | tf_op jit(solution)/shard_map/ppermute | solution.py:41
  20.2 4.8 %collective-permute-start.5 = (f32[32,1024]{1,0:T(8,128)S(1)}, f32[32,1024]{1,0:T(8,128)S(1)}, u32[]{:S(2)}, u32[]{:S(2)}) collective-permute-start(f32[32,1024]{1,0:T(8,128)S(1)} %get-tuple-element.35.one), channel_id=1, source_target_pairs={{0,16},{8,24},{16,0},{24,8},{1,17},{9,25},{17,1},{25,9},{2,18},{10... | collective-permute-start | bytes 393224 | tf_op jit(solution)/shard_map/ppermute | solution.py:41
  20.6 7.2 %collective-permute-start.4 = (f32[32,1024]{1,0:T(8,128)S(1)}, f32[32,1024]{1,0:T(8,128)S(1)}, u32[]{:S(2)}, u32[]{:S(2)}) collective-permute-start(f32[32,1024]{1,0:T(8,128)S(1)} %get-tuple-element.34.one), channel_id=1, source_target_pairs={{0,16},{8,24},{16,0},{24,8},{1,17},{9,25},{17,1},{25,9},{2,18},{10... | collective-permute-start | bytes 393224 | tf_op jit(solution)/shard_map/ppermute | solution.py:41
  25.0 3.1 %collective-permute-start.6 = (f32[32,1024]{1,0:T(8,128)S(1)}, f32[32,1024]{1,0:T(8,128)S(1)}, u32[]{:S(2)}, u32[]{:S(2)}) collective-permute-start(f32[32,1024]{1,0:T(8,128)S(1)} %sum.11.mine.refs_0_), channel_id=1, source_target_pairs={{0,8},{8,0},{16,24},{24,16},{1,9},{9,1},{17,25},{25,17},{2,10},{10... | collective-permute-start | bytes 393224 | tf_op jit(solution)/shard_map/ppermute | solution.py:41
  28.2 25.4 %collective-permute-start.12 = (f32[128,2048]{1,0:T(8,128)S(1)}, f32[128,2048]{1,0:T(8,128)S(1)}, u32[]{:S(2)}, u32[]{:S(2)}) collective-permute-start(f32[128,2048]{1,0:T(8,128)S(1)} %term.1.one), channel_id=1, source_target_pairs={{0,16},{8,24},{16,0},{24,8},{1,17},{9,25},{17,1},{25,9},{2,18},{10... | collective-permute-start | bytes 3145736 | tf_op jit(solution)/shard_map/ppermute | solution.py:41
  29.2 2.3 %collective-permute-start.7 = (f32[32,1024]{1,0:T(8,128)S(1)}, f32[32,1024]{1,0:T(8,128)S(1)}, u32[]{:S(2)}, u32[]{:S(2)}) collective-permute-start(f32[32,1024]{1,0:T(8,128)S(1)} %sum.12.mine.refs_1_), channel_id=1, source_target_pairs={{0,8},{8,0},{16,24},{24,16},{1,9},{9,1},{17,25},{25,17},{2,10},{10... | collective-permute-start | bytes 393224 | tf_op jit(solution)/shard_map/ppermute | solution.py:41
  29.9 17.4 %copy-start.2 = (f32[2,128,1024]{2,1,0:T(8,128)S(1)}, f32[2,128,1024]{2,1,0:T(8,128)}, u32[]{:S(2)}) copy-start(f32[2,128,1024]{2,1,0:T(8,128)} %weights.10) | copy-start | bytes 3145732
  29.9 17.4 %copy-start.4 = (f32[2,128,1024]{2,1,0:T(8,128)S(1)}, f32[2,128,1024]{2,1,0:T(8,128)}, u32[]{:S(2)}) copy-start(f32[2,128,1024]{2,1,0:T(8,128)} %moment.3) | copy-start | bytes 3145732
  29.9 34.2 %slice-start.2 = ((s8[8388608]{0:T(1024)(128)(4,1)}), s8[4194304]{0:T(1024)(128)(4,1)S(1)}, s32[]{:S(2)}) async-start(s8[8388608]{0:T(1024)(128)(4,1)} %bitcast.3), calls=%async_computation.2 | async-start | bytes 8388608
  31.6 29.9 %copy-start.3 = (f32[2,128,2048]{2,1,0:T(8,128)S(1)}, f32[2,128,2048]{2,1,0:T(8,128)}, u32[]{:S(2)}) copy-start(f32[2,128,2048]{2,1,0:T(8,128)} %moment.4) | copy-start | bytes 6291460
  31.6 32.5 %slice-start.3 = ((s8[8388608]{0:T(1024)(128)(4,1)}), s8[4194304]{0:T(1024)(128)(4,1)S(1)}, s32[]{:S(2)}) async-start(s8[8388608]{0:T(1024)(128)(4,1)} %bitcast.3), calls=%async_computation.3 | async-start | bytes 8388608
  33.3 30.8 %slice-start = ((s8[8388608]{0:T(1024)(128)(4,1)}), s8[4194304]{0:T(1024)(128)(4,1)S(1)}, s32[]{:S(2)}) async-start(s8[8388608]{0:T(1024)(128)(4,1)} %bitcast.1), calls=%async_computation | async-start | bytes 8388608
  33.3 1.4 %collective-permute-start.8 = (f32[32,1152]{1,0:T(8,128)S(1)}, f32[32,1152]{1,0:T(8,128)S(1)}, u32[]{:S(2)}, u32[]{:S(2)}) collective-permute-start(f32[32,1152]{1,0:T(8,128)S(1)} %get-tuple-element.40), channel_id=1, source_target_pairs={{0,8},{8,0},{16,24},{24,16},{1,9},{9,1},{17,25},{25,17},{2,10},{10... | collective-permute-start | bytes 442376 | tf_op jit(solution)/shard_map/ppermute | solution.py:41
  33.4 13.9 %collective-permute-start.2 = (f32[128,1024]{1,0:T(8,128)S(1)}, f32[128,1024]{1,0:T(8,128)S(1)}, u32[]{:S(2)}, u32[]{:S(2)}) collective-permute-start(f32[128,1024]{1,0:T(8,128)S(1)} %sum.9.refs_0_.mine), channel_id=1, source_target_pairs={{0,8},{8,0},{16,24},{24,16},{1,9},{9,1},{17,25},{25,17},{2,10},{10... | collective-permute-start | bytes 1572872 | tf_op jit(solution)/shard_map/ppermute | solution.py:41
  34.8 5.4 %collective-permute-start.9 = (f32[32,1152]{1,0:T(8,128)S(1)}, f32[32,1152]{1,0:T(8,128)S(1)}, u32[]{:S(2)}, u32[]{:S(2)}) collective-permute-start(f32[32,1152]{1,0:T(8,128)S(1)} %sum.13.one), channel_id=1, source_target_pairs={{0,1},{1,0},{2,3},{3,2},{4,5},{5,4},{6,7},{7,6},{8,9},{9,8},{10,11... | collective-permute-start | bytes 442376 | tf_op jit(solution)/shard_map/ppermute | solution.py:41
  40.2 4.5 %collective-permute-start.10 = (f32[32,1152]{1,0:T(8,128)S(1)}, f32[32,1152]{1,0:T(8,128)S(1)}, u32[]{:S(2)}, u32[]{:S(2)}) collective-permute-start(f32[32,1152]{1,0:T(8,128)S(1)} %sum.14.one), channel_id=1, source_target_pairs={{0,2},{1,3},{2,0},{3,1},{4,6},{5,7},{6,4},{7,5},{8,10},{9,11},{10,... | collective-permute-start | bytes 442376 | tf_op jit(solution)/shard_map/ppermute | solution.py:41
  44.8 8.8 %collective-permute-start.13 = (f32[32,1152]{1,0:T(8,128)S(1)}, f32[32,1152]{1,0:T(8,128)S(1)}, u32[]{:S(2)}, u32[]{:S(2)}) collective-permute-start(f32[32,1152]{1,0:T(8,128)S(1)} %sum.15.refs_0_.one), channel_id=1, source_target_pairs={{0,4},{1,5},{2,6},{3,7},{4,0},{5,1},{6,2},{7,3},{8,12},{9,13},{10,... | collective-permute-start | bytes 442376 | tf_op jit(solution)/shard_map/ppermute | solution.py:41
  53.6 10.5 %slice-start.1 = ((s8[8388608]{0:T(1024)(128)(4,1)}), s8[4194304]{0:T(1024)(128)(4,1)S(1)}, s32[]{:S(2)}) async-start(s8[8388608]{0:T(1024)(128)(4,1)} %bitcast.1), calls=%async_computation.1 | async-start | bytes 8388608
  53.7 7.7 %collective-permute-start.14 = (f32[128,2048]{1,0:T(8,128)S(1)}, f32[128,2048]{1,0:T(8,128)S(1)}, u32[]{:S(2)}, u32[]{:S(2)}) collective-permute-start(f32[128,2048]{1,0:T(8,128)S(1)} %sum.16.mine), channel_id=1, source_target_pairs={{0,8},{8,0},{16,24},{24,16},{1,9},{9,1},{17,25},{25,17},{2,10},{10... | collective-permute-start | bytes 3145736 | tf_op jit(solution)/shard_map/ppermute | solution.py:41
  55.4 5.1 %collective-permute-start.15 = (f32[32,1024]{1,0:T(8,128)S(1)}, f32[32,1024]{1,0:T(8,128)S(1)}, u32[]{:S(2)}, u32[]{:S(2)}) collective-permute-start(f32[32,1024]{1,0:T(8,128)S(1)} %get-tuple-element.44.refs_0_.one), channel_id=1, source_target_pairs={{0,16},{8,24},{16,0},{24,8},{1,17},{9,25},{17,1},{25,9},{2,18},{10... | collective-permute-start | bytes 393224 | tf_op jit(solution)/shard_map/ppermute | solution.py:41
  60.5 3.6 %collective-permute-start.16 = (f32[32,1024]{1,0:T(8,128)S(1)}, f32[32,1024]{1,0:T(8,128)S(1)}, u32[]{:S(2)}, u32[]{:S(2)}) collective-permute-start(f32[32,1024]{1,0:T(8,128)S(1)} %sum.17.refs_0_.mine), channel_id=1, source_target_pairs={{0,8},{8,0},{16,24},{24,16},{1,9},{9,1},{17,25},{25,17},{2,10},{10... | collective-permute-start | bytes 393224 | tf_op jit(solution)/shard_map/ppermute | solution.py:41

commit v6 on v5

--- a/solution.py
+++ b/solution.py
@@ -432,7 +432,7 @@
     before, left = [], []
     for chunk, half in enumerate(halves):
         *before, piece = right_call(
-            core, half, others[chunk], corrected, before, scale, math.gcd(rows // chunks, 256), chunk
+            core, half, others[chunk], corrected, before, scale, math.gcd(rows // chunks, 1024), chunk
         )
         left.append(piece)
     away, kept = before

time: 74.3 us -> 74.3 us (level)
  no operation moved by 1% of the time
where the time goes in v6:
time: 74.3 us; the launch traced here: 74.2 us
  Pallas kernels  35.8 us (48%)
  waiting for transfers between devices  18.8 us (25%)
  starting transfers between devices  18.7 us (25%)
  between operations  0.84 us (1%)
    ppermute x17, waiting for transfers between devices, swap(): lax.ppermute(value, axis, [(i, i ^ bit) for i in range(lax.axis_size(axis...  18.8 us
    ppermute x17, starting transfers between devices, swap(): lax.ppermute(value, axis, [(i, i ^ bit) for i in range(lax.axis_size(axis...  18.7 us
    pallas_call x1, Pallas kernels, left_call(): pl.pallas_call(functools.partial(left_kernel, len(after)), grid=(rows //...  11 us
    pallas_call x1, Pallas kernels, final_call(): pl.pallas_call(functools.partial(final_kernel, scale, chunks), grid=(rows...  9.97 us
    pallas_call x2, Pallas kernels, layer_call(): pl.pallas_call(functools.partial(layer_kernel, scale), in_specs=[SMEM] +...  4.28 us
    pallas_call x1, Pallas kernels, factor_call(): pl.pallas_call(factor_kernel, in_specs=[VMEM] * (1 + len(left)), out_spec...  3.78 us
    pallas_call x2, Pallas kernels, right_call(): pl.pallas_call(functools.partial(right_kernel, scale, block, chunk), in_s...  3.46 us
    pallas_call x2, Pallas kernels, half_call(): pl.pallas_call(kernel, grid_spec=pltpu.PrefetchScalarGridSpec(num_scalar_...  2.85 us
  transfers between devices with their start and end apart: 17, of which 11 were waited for; matrix products, arithmetic and copies ran while one was open for 0% of the time, Pallas kernels for 34%

profile of v6, /device:TPU:1, one launch (start us, length us, event | category | flops | bytes accessed | tf_op | source)
XLA Modules:
  0.0 74.2 jit_solution(14037126841571169814)
XLA Ops:
  0.6 0.1 collective-permute-start
  0.8 1.6 %away.1.refs_0_ = f32[128,2048]{1,0:T(8,128)S(1)} custom-call(s32[1]{0:T(128)} %bitcast.core, f32[2,128,2048]{2,1,0:T(8,128)} %weights.12, f32[1,2,128,2048]{3,2,1,0:T(8,128)} %copies.7), custom_call_target="tpu_custom_call" | custom-call | tf_op jit(solution)/shard_map/away/pallas_call | solution.py:349
  2.4 0.5 collective-permute-start.11
  2.9 0.7 collective-permute-done.received
  3.6 1.3 %both.1.one.refs_0_ = f32[128,1024]{1,0:T(8,128)S(1)} custom-call(s32[1]{0:T(128)} %bitcast.core, f32[2,128,1024]{2,1,0:T(8,128)} %weights.10, f32[1,2,128,1024]{3,2,1,0:T(8,128)} %copies.5, f32[1,2,128,1024]{3,2,1,0:T(8,128)S(1)} %collective-permute-done.received, f32[128,2048]{1,0:T(8,128)S(1)} %away.1.refs_0_), custom_call_target="tpu_custom_call" | custom-call | tf_op jit(solution)/shard_map/both/pallas_call | solution.py:349
  4.8 0.0 copy-start
  4.8 0.0 copy-start.1
  4.9 2.4 %collective-permute-start.1 = (f32[128,1024]{1,0:T(8,128)S(1)}, f32[128,1024]{1,0:T(8,128)S(1)}, u32[]{:S(2)}, u32[]{:S(2)}) collective-permute-start(f32[128,1024]{1,0:T(8,128)S(1)} %both.1.one.refs_0_), channel_id=1, source_target_pairs={{0,16},{8,24},{16,0},{24,8},{1,17},{9,25},{17,1},{25,9},{2,18},{10... | collective-permute-start | bytes 1572872 | tf_op jit(solution)/shard_map/ppermute | solution.py:41
  7.3 11.0 %left.1 = (f32[2048,1024]{1,0:T(8,128)S(1)}, f32[32,2048]{1,0:T(8,128)S(1)}, f32[32,2048]{1,0:T(8,128)S(1)}) custom-call(s32[1]{0:T(128)} %bitcast.core, f32[2048,1024]{1,0:T(8,128)} %weights.13, f32[1,2048,1024]{2,1,0:T(8,128)} %copies.6, f32[1,2048,1024]{2,1,0:T(8,128)} %error.1, f32[64,1024]{1,0:T(8,128)} %warm.1, f32[128,1024]{1,0:T(8,128)S(1)} %both.1.one.refs_0_), custom_call_target="tpu_custom_call" | custom-call | tf_op jit(solution)/shard_map/left/pallas_call | solution.py:125
  18.3 0.7 collective-permute-start.3
  19.0 0.3 collective-permute-done.1.two
  19.3 0.1 sum.9.refs_0_.mine
  19.3 0.8 %collective-permute-done.3.two = f32[32,2048]{1,0:T(8,128)S(1)} collective-permute-done((f32[32,2048]{1,0:T(8,128)S(1)}, f32[32,2048]{1,0:T(8,128)S(1)}, u32[]{:S(2)}, u32[]{:S(2)}) %collective-permute-start.3) | collective-permute-done | bytes 262176 | tf_op jit(solution)/shard_map/ppermute | solution.py:41
  20.2 0.4 collective-permute-start.5
  20.6 1.1 %collective-permute-start.4 = (f32[32,1024]{1,0:T(8,128)S(1)}, f32[32,1024]{1,0:T(8,128)S(1)}, u32[]{:S(2)}, u32[]{:S(2)}) collective-permute-start(f32[32,1024]{1,0:T(8,128)S(1)} %get-tuple-element.34.one), channel_id=1, source_target_pairs={{0,16},{8,24},{16,0},{24,8},{1,17},{9,25},{17,1},{25,9},{2,18},{10... | collective-permute-start | bytes 393224 | tf_op jit(solution)/shard_map/ppermute | solution.py:41
  21.7 3.2 %collective-permute-done.5.two = f32[32,1024]{1,0:T(8,128)S(1)} collective-permute-done((f32[32,1024]{1,0:T(8,128)S(1)}, f32[32,1024]{1,0:T(8,128)S(1)}, u32[]{:S(2)}, u32[]{:S(2)}) %collective-permute-start.5) | collective-permute-done | bytes 131104 | tf_op jit(solution)/shard_map/ppermute | solution.py:41
  25.0 2.1 %collective-permute-start.6 = (f32[32,1024]{1,0:T(8,128)S(1)}, f32[32,1024]{1,0:T(8,128)S(1)}, u32[]{:S(2)}, u32[]{:S(2)}) collective-permute-start(f32[32,1024]{1,0:T(8,128)S(1)} %sum.11.mine.refs_0_), channel_id=1, source_target_pairs={{0,8},{8,0},{16,24},{24,16},{1,9},{9,1},{17,25},{25,17},{2,10},{10... | collective-permute-start | bytes 393224 | tf_op jit(solution)/shard_map/ppermute | solution.py:41
  27.0 0.7 collective-permute-done.4.two
  27.8 0.3 collective-permute-done.6.refs_0_.other
  28.1 0.0 collective-permute-done.11.received
  28.1 0.0 copy-done
  28.1 0.0 copy-done.1
  28.1 0.2 term.1.one
  28.2 1.0 %collective-permute-start.12 = (f32[128,2048]{1,0:T(8,128)S(1)}, f32[128,2048]{1,0:T(8,128)S(1)}, u32[]{:S(2)}, u32[]{:S(2)}) collective-permute-start(f32[128,2048]{1,0:T(8,128)S(1)} %term.1.one), channel_id=1, source_target_pairs={{0,16},{8,24},{16,0},{24,8},{1,17},{9,25},{17,1},{25,9},{2,18},{10... | collective-permute-start | bytes 3145736 | tf_op jit(solution)/shard_map/ppermute | solution.py:41
  29.2 0.6 collective-permute-start.7
  29.9 0.0 copy-start.2
  29.9 0.0 copy-start.4
  29.9 0.0 slice-start.2
  29.9 1.7 %right.2 = (f32[32,1152]{1,0:T(8,128)S(1)}, f32[32,1152]{1,0:T(8,128)S(1)}, f32[64,1024]{1,0:T(8,128)S(1)}) custom-call(s32[1]{0:T(128)} %bitcast.core, f32[32,1024]{1,0:T(8,128)S(1)} %sum.11.mine.refs_0_, f32[32,1024]{1,0:T(8,128)S(1)} %collective-permute-done.6.refs_0_.other, f32[2048,1024]{1,0:T(8,128)S(1)} %get-tuple-element.36.corrected), custom_call_target="tpu_custom_call" | custom-call | tf_op jit(solution)/shard_map/right/pallas_call | solution.py:185
  31.6 0.0 collective-permute-done.7.other
  31.6 0.0 copy-start.3
  31.6 0.0 slice-start.3
  31.6 1.8 %right.3 = (f32[32,1152]{1,0:T(8,128)S(1)}, f32[32,1152]{1,0:T(8,128)S(1)}, f32[64,1024]{1,0:T(8,128)S(1)}) custom-call(s32[1]{0:T(128)} %bitcast.core, f32[32,1024]{1,0:T(8,128)S(1)} %sum.12.mine.refs_1_, f32[32,1024]{1,0:T(8,128)S(1)} %collective-permute-done.7.other, f32[2048,1024]{1,0:T(8,128)S(1)} %get-tuple-element.36.corrected, ...), custom_call_target="tpu_custom_call" | custom-call | tf_op jit(solution)/shard_map/right/pallas_call | solution.py:185
  33.4 0.0 slice-start
  33.4 0.1 collective-permute-start.8
  33.4 0.5 collective-permute-start.2
  33.9 0.9 %collective-permute-done.8.two = f32[32,1152]{1,0:T(8,128)S(1)} collective-permute-done((f32[32,1152]{1,0:T(8,128)S(1)}, f32[32,1152]{1,0:T(8,128)S(1)}, u32[]{:S(2)}, u32[]{:S(2)}) %collective-permute-start.8) | collective-permute-done | bytes 147488 | tf_op jit(solution)/shard_map/ppermute | solution.py:41
  34.8 1.5 %collective-permute-start.9 = (f32[32,1152]{1,0:T(8,128)S(1)}, f32[32,1152]{1,0:T(8,128)S(1)}, u32[]{:S(2)}, u32[]{:S(2)}) collective-permute-start(f32[32,1152]{1,0:T(8,128)S(1)} %sum.13.one), channel_id=1, source_target_pairs={{0,1},{1,0},{2,3},{3,2},{4,5},{5,4},{6,7},{7,6},{8,9},{9,8},{10,11... | collective-permute-start | bytes 442376 | tf_op jit(solution)/shard_map/ppermute | solution.py:41
  36.4 3.8 %collective-permute-done.9.two = f32[32,1152]{1,0:T(8,128)S(1)} collective-permute-done((f32[32,1152]{1,0:T(8,128)S(1)}, f32[32,1152]{1,0:T(8,128)S(1)}, u32[]{:S(2)}, u32[]{:S(2)}) %collective-permute-start.9) | collective-permute-done | bytes 147488 | tf_op jit(solution)/shard_map/ppermute | solution.py:41
  40.2 1.6 %collective-permute-start.10 = (f32[32,1152]{1,0:T(8,128)S(1)}, f32[32,1152]{1,0:T(8,128)S(1)}, u32[]{:S(2)}, u32[]{:S(2)}) collective-permute-start(f32[32,1152]{1,0:T(8,128)S(1)} %sum.14.one), channel_id=1, source_target_pairs={{0,2},{1,3},{2,0},{3,1},{4,6},{5,7},{6,4},{7,5},{8,10},{9,11},{10,... | collective-permute-start | bytes 442376 | tf_op jit(solution)/shard_map/ppermute | solution.py:41
  41.8 3.0 %collective-permute-done.10.two = f32[32,1152]{1,0:T(8,128)S(1)} collective-permute-done((f32[32,1152]{1,0:T(8,128)S(1)}, f32[32,1152]{1,0:T(8,128)S(1)}, u32[]{:S(2)}, u32[]{:S(2)}) %collective-permute-start.10) | collective-permute-done | bytes 147488 | tf_op jit(solution)/shard_map/ppermute | solution.py:41
  44.8 2.5 %collective-permute-start.13 = (f32[32,1152]{1,0:T(8,128)S(1)}, f32[32,1152]{1,0:T(8,128)S(1)}, u32[]{:S(2)}, u32[]{:S(2)}) collective-permute-start(f32[32,1152]{1,0:T(8,128)S(1)} %sum.15.refs_0_.one), channel_id=1, source_target_pairs={{0,4},{1,5},{2,6},{3,7},{4,0},{5,1},{6,2},{7,3},{8,12},{9,13},{10,... | collective-permute-start | bytes 442376 | tf_op jit(solution)/shard_map/ppermute | solution.py:41
  47.3 0.0 collective-permute-done.2.other
  47.3 0.0 copy-done.2
  47.3 0.0 copy-done.4
  47.3 1.6 %layer.2 = (f32[2,128,1024]{2,1,0:T(8,128)}, f32[2,128,1024]{2,1,0:T(8,128)}, f32[8,128]{1,0:T(8,128)S(1)}) custom-call(s32[1]{0:T(128)} %bitcast.core, f32[128,1024]{1,0:T(8,128)S(1)} %sum.9.refs_0_.mine, f32[128,1024]{1,0:T(8,128)S(1)} %collective-permute-done.2.other, f32[2,128,1024]{2,1,0:T(8,128)S(1)} %copy-done.2, f32[2,128,1024]{2,1,0:T(8,128)S(1)} %copy-done.4, ...), custom_call_target="tpu_custom_call" | custom-call | tf_op jit(solution)/shard_map/layer/pallas_call | solution.py:387
  48.9 4.7 %collective-permute-done.13.two = f32[32,1152]{1,0:T(8,128)S(1)} collective-permute-done((f32[32,1152]{1,0:T(8,128)S(1)}, f32[32,1152]{1,0:T(8,128)S(1)}, u32[]{:S(2)}, u32[]{:S(2)}) %collective-permute-start.13) | collective-permute-done | bytes 147488 | tf_op jit(solution)/shard_map/ppermute | solution.py:41
  53.7 0.0 collective-permute-done.12.two
  53.7 0.0 slice-start.1
  53.7 0.1 sum.16.mine
  53.8 1.7 %collective-permute-start.14 = (f32[128,2048]{1,0:T(8,128)S(1)}, f32[128,2048]{1,0:T(8,128)S(1)}, u32[]{:S(2)}, u32[]{:S(2)}) collective-permute-start(f32[128,2048]{1,0:T(8,128)S(1)} %sum.16.mine), channel_id=1, source_target_pairs={{0,8},{8,0},{16,24},{24,16},{1,9},{9,1},{17,25},{25,17},{2,10},{10... | collective-permute-start | bytes 3145736 | tf_op jit(solution)/shard_map/ppermute | solution.py:41
  55.5 1.0 %collective-permute-start.15 = (f32[32,1024]{1,0:T(8,128)S(1)}, f32[32,1024]{1,0:T(8,128)S(1)}, u32[]{:S(2)}, u32[]{:S(2)}) collective-permute-start(f32[32,1024]{1,0:T(8,128)S(1)} %get-tuple-element.44.refs_0_.one), channel_id=1, source_target_pairs={{0,16},{8,24},{16,0},{24,8},{1,17},{9,25},{17,1},{25,9},{2,18},{10... | collective-permute-start | bytes 393224 | tf_op jit(solution)/shard_map/ppermute | solution.py:41
  56.4 3.8 %factor.1 = (f32[64,64]{1,0:T(8,128)S(1)}, bf16[1024,384]{1,0:T(8,128)(2,1)S(1)}, bf16[1024,384]{1,0:T(8,128)(2,1)S(1)}) custom-call(f32[32,128]{1,0:T(8,128)S(1)} %get-tuple-element.45.message, f32[64,1024]{1,0:T(8,128)S(1)} %get-tuple-element.46.refs_0_, f32[64,1024]{1,0:T(8,128)S(1)} %get-tuple-element.47.refs_1_), custom_call_target="tpu_custom_call" | custom-call | tf_op jit(solution)/shard_map/factor/pallas_call | solution.py:251
  60.2 0.3 collective-permute-done.15.two
  60.6 0.9 %collective-permute-start.16 = (f32[32,1024]{1,0:T(8,128)S(1)}, f32[32,1024]{1,0:T(8,128)S(1)}, u32[]{:S(2)}, u32[]{:S(2)}) collective-permute-start(f32[32,1024]{1,0:T(8,128)S(1)} %sum.17.refs_0_.mine), channel_id=1, source_target_pairs={{0,8},{8,0},{16,24},{24,16},{1,9},{9,1},{17,25},{25,17},{2,10},{10... | collective-permute-start | bytes 393224 | tf_op jit(solution)/shard_map/ppermute | solution.py:41
  61.5 0.0 collective-permute-done.14.other
  61.5 0.0 copy-done.3
  61.5 2.6 %layer.3 = (f32[2,128,2048]{2,1,0:T(8,128)}, f32[2,128,2048]{2,1,0:T(8,128)}, f32[8,128]{1,0:T(8,128)S(1)}) custom-call(s32[1]{0:T(128)} %bitcast.core, f32[128,2048]{1,0:T(8,128)S(1)} %sum.16.mine, f32[128,2048]{1,0:T(8,128)S(1)} %collective-permute-done.14.other, f32[2,128,2048]{2,1,0:T(8,128)S(1)} %copy-done, f32[2,128,2048]{2,1,0:T(8,128)S(1)} %copy-done.3, ...), custom_call_target="tpu_custom_call" | custom-call | tf_op jit(solution)/shard_map/layer/pallas_call | solution.py:387
  64.1 0.0 collective-permute-done.16.other
  64.1 0.0 slice-done.2
  64.2 0.0 slice-done.3
  64.2 0.0 slice-done
  64.2 0.0 slice-done.1
  64.2 10.0 %final.1 = (f32[2048,1024]{1,0:T(8,128)}, f32[2048,1024]{1,0:T(8,128)}, f32[1,2048,1024]{2,1,0:T(8,128)}) custom-call(s32[1]{0:T(128)} %bitcast.core, f32[32,1024]{1,0:T(8,128)S(1)} %sum.17.refs_0_.mine, f32[32,1024]{1,0:T(8,128)S(1)} %collective-permute-done.16.other, f32[64,64]{1,0:T(8,128)S(1)} %get-tuple-element.48.refs_0_.inverse, ...), custom_call_target="tpu_custom_call" | custom-call | tf_op jit(solution)/shard_map/final/pallas_call | solution.py:300
  (10 shorter events, 0.1 us)
Async XLA Ops:
  0.6 2.9 %collective-permute-start = (f32[1,2,128,1024]{3,2,1,0:T(8,128)}, f32[1,2,128,1024]{3,2,1,0:T(8,128)S(1)}, u32[]{:S(2)}, u32[]{:S(2)}) collective-permute-start(f32[1,2,128,1024]{3,2,1,0:T(8,128)} %copies.5), channel_id=1, source_target_pairs={{0,8},{8,0},{16,24},{24,16},{1,9},{9,1},{17,25},{25,17},{2,10},{10... | collective-permute-start | bytes 3145736 | tf_op jit(solution)/shard_map/ppermute | solution.py:41
  2.4 25.7 %collective-permute-start.11 = (f32[128,2048]{1,0:T(8,128)S(1)}, f32[128,2048]{1,0:T(8,128)S(1)}, u32[]{:S(2)}, u32[]{:S(2)}) collective-permute-start(f32[128,2048]{1,0:T(8,128)S(1)} %away.1.refs_0_), channel_id=1, source_target_pairs={{0,8},{8,0},{16,24},{24,16},{1,9},{9,1},{17,25},{25,17},{2,10},{10... | collective-permute-start | bytes 3145736 | tf_op jit(solution)/shard_map/ppermute | solution.py:41
  4.8 23.2 %copy-start = (f32[2,128,2048]{2,1,0:T(8,128)S(1)}, f32[2,128,2048]{2,1,0:T(8,128)}, u32[]{:S(2)}) copy-start(f32[2,128,2048]{2,1,0:T(8,128)} %weights.12) | copy-start | bytes 6291460
  4.8 23.2 %copy-start.1 = (f32[1,2,128,2048]{3,2,1,0:T(8,128)S(1)}, f32[1,2,128,2048]{3,2,1,0:T(8,128)}, u32[]{:S(2)}) copy-start(f32[1,2,128,2048]{3,2,1,0:T(8,128)} %copies.7) | copy-start | bytes 6291460
  4.9 14.4 %collective-permute-start.1 = (f32[128,1024]{1,0:T(8,128)S(1)}, f32[128,1024]{1,0:T(8,128)S(1)}, u32[]{:S(2)}, u32[]{:S(2)}) collective-permute-start(f32[128,1024]{1,0:T(8,128)S(1)} %both.1.one.refs_0_), channel_id=1, source_target_pairs={{0,16},{8,24},{16,0},{24,8},{1,17},{9,25},{17,1},{25,9},{2,18},{10... | collective-permute-start | bytes 1572872 | tf_op jit(solution)/shard_map/ppermute | solution.py:41
  18.3 1.9 %collective-permute-start.3 = (f32[32,2048]{1,0:T(8,128)S(1)}, f32[32,2048]{1,0:T(8,128)S(1)}, u32[]{:S(2)}, u32[]{:S(2)}) collective-permute-start(f32[32,2048]{1,0:T(8,128)S(1)} %get-tuple-element.33), channel_id=1, source_target_pairs={{0,8},{8,0},{16,24},{24,16},{1,9},{9,1},{17,25},{25,17},{2,10},{10... | collective-permute-start | bytes 786440 | tf_op jit(solution)/shard_map/ppermute | solution.py:41
  20.2 4.8 %collective-permute-start.5 = (f32[32,1024]{1,0:T(8,128)S(1)}, f32[32,1024]{1,0:T(8,128)S(1)}, u32[]{:S(2)}, u32[]{:S(2)}) collective-permute-start(f32[32,1024]{1,0:T(8,128)S(1)} %get-tuple-element.35.one), channel_id=1, source_target_pairs={{0,16},{8,24},{16,0},{24,8},{1,17},{9,25},{17,1},{25,9},{2,18},{10... | collective-permute-start | bytes 393224 | tf_op jit(solution)/shard_map/ppermute | solution.py:41
  20.6 7.2 %collective-permute-start.4 = (f32[32,1024]{1,0:T(8,128)S(1)}, f32[32,1024]{1,0:T(8,128)S(1)}, u32[]{:S(2)}, u32[]{:S(2)}) collective-permute-start(f32[32,1024]{1,0:T(8,128)S(1)} %get-tuple-element.34.one), channel_id=1, source_target_pairs={{0,16},{8,24},{16,0},{24,8},{1,17},{9,25},{17,1},{25,9},{2,18},{10... | collective-permute-start | bytes 393224 | tf_op jit(solution)/shard_map/ppermute | solution.py:41
  25.0 3.1 %collective-permute-start.6 = (f32[32,1024]{1,0:T(8,128)S(1)}, f32[32,1024]{1,0:T(8,128)S(1)}, u32[]{:S(2)}, u32[]{:S(2)}) collective-permute-start(f32[32,1024]{1,0:T(8,128)S(1)} %sum.11.mine.refs_0_), channel_id=1, source_target_pairs={{0,8},{8,0},{16,24},{24,16},{1,9},{9,1},{17,25},{25,17},{2,10},{10... | collective-permute-start | bytes 393224 | tf_op jit(solution)/shard_map/ppermute | solution.py:41
  28.2 25.4 %collective-permute-start.12 = (f32[128,2048]{1,0:T(8,128)S(1)}, f32[128,2048]{1,0:T(8,128)S(1)}, u32[]{:S(2)}, u32[]{:S(2)}) collective-permute-start(f32[128,2048]{1,0:T(8,128)S(1)} %term.1.one), channel_id=1, source_target_pairs={{0,16},{8,24},{16,0},{24,8},{1,17},{9,25},{17,1},{25,9},{2,18},{10... | collective-permute-start | bytes 3145736 | tf_op jit(solution)/shard_map/ppermute | solution.py:41
  29.2 2.4 %collective-permute-start.7 = (f32[32,1024]{1,0:T(8,128)S(1)}, f32[32,1024]{1,0:T(8,128)S(1)}, u32[]{:S(2)}, u32[]{:S(2)}) collective-permute-start(f32[32,1024]{1,0:T(8,128)S(1)} %sum.12.mine.refs_1_), channel_id=1, source_target_pairs={{0,8},{8,0},{16,24},{24,16},{1,9},{9,1},{17,25},{25,17},{2,10},{10... | collective-permute-start | bytes 393224 | tf_op jit(solution)/shard_map/ppermute | solution.py:41
  29.9 17.4 %copy-start.2 = (f32[2,128,1024]{2,1,0:T(8,128)S(1)}, f32[2,128,1024]{2,1,0:T(8,128)}, u32[]{:S(2)}) copy-start(f32[2,128,1024]{2,1,0:T(8,128)} %weights.10) | copy-start | bytes 3145732
  29.9 17.4 %copy-start.4 = (f32[2,128,1024]{2,1,0:T(8,128)S(1)}, f32[2,128,1024]{2,1,0:T(8,128)}, u32[]{:S(2)}) copy-start(f32[2,128,1024]{2,1,0:T(8,128)} %moment.3) | copy-start | bytes 3145732
  29.9 34.3 %slice-start.2 = ((s8[8388608]{0:T(1024)(128)(4,1)}), s8[4194304]{0:T(1024)(128)(4,1)S(1)}, s32[]{:S(2)}) async-start(s8[8388608]{0:T(1024)(128)(4,1)} %bitcast.3), calls=%async_computation.2 | async-start | bytes 8388608
  31.6 29.9 %copy-start.3 = (f32[2,128,2048]{2,1,0:T(8,128)S(1)}, f32[2,128,2048]{2,1,0:T(8,128)}, u32[]{:S(2)}) copy-start(f32[2,128,2048]{2,1,0:T(8,128)} %moment.4) | copy-start | bytes 6291460
  31.6 32.5 %slice-start.3 = ((s8[8388608]{0:T(1024)(128)(4,1)}), s8[4194304]{0:T(1024)(128)(4,1)S(1)}, s32[]{:S(2)}) async-start(s8[8388608]{0:T(1024)(128)(4,1)} %bitcast.3), calls=%async_computation.3 | async-start | bytes 8388608
  33.4 30.8 %slice-start = ((s8[8388608]{0:T(1024)(128)(4,1)}), s8[4194304]{0:T(1024)(128)(4,1)S(1)}, s32[]{:S(2)}) async-start(s8[8388608]{0:T(1024)(128)(4,1)} %bitcast.1), calls=%async_computation | async-start | bytes 8388608
  33.4 1.4 %collective-permute-start.8 = (f32[32,1152]{1,0:T(8,128)S(1)}, f32[32,1152]{1,0:T(8,128)S(1)}, u32[]{:S(2)}, u32[]{:S(2)}) collective-permute-start(f32[32,1152]{1,0:T(8,128)S(1)} %get-tuple-element.40), channel_id=1, source_target_pairs={{0,8},{8,0},{16,24},{24,16},{1,9},{9,1},{17,25},{25,17},{2,10},{10... | collective-permute-start | bytes 442376 | tf_op jit(solution)/shard_map/ppermute | solution.py:41
  33.4 13.8 %collective-permute-start.2 = (f32[128,1024]{1,0:T(8,128)S(1)}, f32[128,1024]{1,0:T(8,128)S(1)}, u32[]{:S(2)}, u32[]{:S(2)}) collective-permute-start(f32[128,1024]{1,0:T(8,128)S(1)} %sum.9.refs_0_.mine), channel_id=1, source_target_pairs={{0,8},{8,0},{16,24},{24,16},{1,9},{9,1},{17,25},{25,17},{2,10},{10... | collective-permute-start | bytes 1572872 | tf_op jit(solution)/shard_map/ppermute | solution.py:41
  34.8 5.4 %collective-permute-start.9 = (f32[32,1152]{1,0:T(8,128)S(1)}, f32[32,1152]{1,0:T(8,128)S(1)}, u32[]{:S(2)}, u32[]{:S(2)}) collective-permute-start(f32[32,1152]{1,0:T(8,128)S(1)} %sum.13.one), channel_id=1, source_target_pairs={{0,1},{1,0},{2,3},{3,2},{4,5},{5,4},{6,7},{7,6},{8,9},{9,8},{10,11... | collective-permute-start | bytes 442376 | tf_op jit(solution)/shard_map/ppermute | solution.py:41
  40.2 4.6 %collective-permute-start.10 = (f32[32,1152]{1,0:T(8,128)S(1)}, f32[32,1152]{1,0:T(8,128)S(1)}, u32[]{:S(2)}, u32[]{:S(2)}) collective-permute-start(f32[32,1152]{1,0:T(8,128)S(1)} %sum.14.one), channel_id=1, source_target_pairs={{0,2},{1,3},{2,0},{3,1},{4,6},{5,7},{6,4},{7,5},{8,10},{9,11},{10,... | collective-permute-start | bytes 442376 | tf_op jit(solution)/shard_map/ppermute | solution.py:41
  44.8 8.8 %collective-permute-start.13 = (f32[32,1152]{1,0:T(8,128)S(1)}, f32[32,1152]{1,0:T(8,128)S(1)}, u32[]{:S(2)}, u32[]{:S(2)}) collective-permute-start(f32[32,1152]{1,0:T(8,128)S(1)} %sum.15.refs_0_.one), channel_id=1, source_target_pairs={{0,4},{1,5},{2,6},{3,7},{4,0},{5,1},{6,2},{7,3},{8,12},{9,13},{10,... | collective-permute-start | bytes 442376 | tf_op jit(solution)/shard_map/ppermute | solution.py:41
  53.7 10.5 %slice-start.1 = ((s8[8388608]{0:T(1024)(128)(4,1)}), s8[4194304]{0:T(1024)(128)(4,1)S(1)}, s32[]{:S(2)}) async-start(s8[8388608]{0:T(1024)(128)(4,1)} %bitcast.1), calls=%async_computation.1 | async-start | bytes 8388608
  53.8 7.7 %collective-permute-start.14 = (f32[128,2048]{1,0:T(8,128)S(1)}, f32[128,2048]{1,0:T(8,128)S(1)}, u32[]{:S(2)}, u32[]{:S(2)}) collective-permute-start(f32[128,2048]{1,0:T(8,128)S(1)} %sum.16.mine), channel_id=1, source_target_pairs={{0,8},{8,0},{16,24},{24,16},{1,9},{9,1},{17,25},{25,17},{2,10},{10... | collective-permute-start | bytes 3145736 | tf_op jit(solution)/shard_map/ppermute | solution.py:41
  55.5 5.1 %collective-permute-start.15 = (f32[32,1024]{1,0:T(8,128)S(1)}, f32[32,1024]{1,0:T(8,128)S(1)}, u32[]{:S(2)}, u32[]{:S(2)}) collective-permute-start(f32[32,1024]{1,0:T(8,128)S(1)} %get-tuple-element.44.refs_0_.one), channel_id=1, source_target_pairs={{0,16},{8,24},{16,0},{24,8},{1,17},{9,25},{17,1},{25,9},{2,18},{10... | collective-permute-start | bytes 393224 | tf_op jit(solution)/shard_map/ppermute | solution.py:41
  60.6 3.6 %collective-permute-start.16 = (f32[32,1024]{1,0:T(8,128)S(1)}, f32[32,1024]{1,0:T(8,128)S(1)}, u32[]{:S(2)}, u32[]{:S(2)}) collective-permute-start(f32[32,1024]{1,0:T(8,128)S(1)} %sum.17.refs_0_.mine), channel_id=1, source_target_pairs={{0,8},{8,0},{16,24},{24,16},{1,9},{9,1},{17,25},{25,17},{2,10},{10... | collective-permute-start | bytes 393224 | tf_op jit(solution)/shard_map/ppermute | solution.py:41

commit v7 on v5

--- a/solution.py
+++ b/solution.py
@@ -332,8 +332,29 @@
     )(one, two, *after)
 
 
-def away_kernel(core, weights, copies, *refs):
-    refs[-1][...] = weights[0] - copies[0, 0]
+def split_kernel(core, weights, copies, away, kept):
+    at = core[0]
+    away[...] = weights[1 - at] - copies[0, 1 - at]
+    kept[...] = weights[at] - copies[0, at]
+
+
+def split_call(core, weights, copies):
+    _, rows, width = weights.shape
+    block = rows // 4 if rows % 32 == 0 else rows
+    out = pl.BlockSpec((block, width), lambda i: (i, 0))
+    return pl.pallas_call(
+        split_kernel,
+        grid=(rows // block,),
+        in_specs=[
+            SMEM,
+            pl.BlockSpec((2, block, width), lambda i: (0, i, 0)),
+            pl.BlockSpec((1, 2, block, width), lambda i: (0, 0, i, 0)),
+        ],
+        out_specs=[out, out],
+        out_shape=[jax.ShapeDtypeStruct((rows, width), jnp.float32)] * 2,
+        compiler_params=pltpu.CompilerParams(vmem_limit_bytes=12 * MIB),
+        name="split",
+    )(core, in_hbm(weights), in_hbm(copies))
 
 
 def both_kernel(core, weights, copies, received, *refs):
@@ -358,22 +379,6 @@
         compiler_params=pltpu.CompilerParams(vmem_limit_bytes=12 * MIB),
         name=kernel.__name__[:-7],
     )(core, in_hbm(weights), in_hbm(copies[0]), *copies[1:], *after)
-
-
-def term_kernel(core, weights, copies, received, *refs):
-    at = core[0]
-    refs[-1][...] = (weights[at] - copies[0, at]) + received[...]
-
-
-def term_call(core, weights, copies, received, after):
-    return pl.pallas_call(
-        term_kernel,
-        in_specs=[SMEM] + [VMEM] * 3 + [ANY] * len(after),
-        out_specs=VMEM,
-        out_shape=jax.ShapeDtypeStruct(weights.shape[1:], jnp.float32),
-        compiler_params=pltpu.CompilerParams(vmem_limit_bytes=12 * MIB),
-        name="term",
-    )(core, weights, copies, received, *after)
 
 
 def layer_kernel(scale, core, mine, other, weights, moment, *refs):
@@ -414,7 +419,7 @@
     core = jnp.reshape(lax.axis_index("replica") & 1, (1,)).astype(jnp.int32)
 
     square_received = swap(square_copies, "replica", 1)
-    broad_away = half_call(away_kernel, True, core, broad_weights, (broad_copies,), ())
+    broad_away, broad_kept = split_call(core, broad_weights, broad_copies)
     square_half = half_call(both_kernel, False, core, square_weights, (square_copies, square_received), (broad_away,))
     broad_received = swap(broad_away, "replica", 1)
     chunks = 2 if rows % 512 == 0 else 1
@@ -428,7 +433,7 @@
         halves.append(sum_over_chips(piece, ready))
         others.append(swap(halves[-1], "replica", 1))
         ready = (others[-1],)
-    broad_half = term_call(core, broad_weights, broad_copies, broad_received, tuple(halves))
+    broad_half = sum_call(broad_kept, broad_received, tuple(halves))
     before, left = [], []
     for chunk, half in enumerate(halves):
         *before, piece = right_call(

time: 74.3 us -> 74.5 us (level)
  Pallas kernels: 35.7 us -> 37 us
  waiting for transfers between devices: 18.8 us -> 17.9 us
    pallas_call x1, Pallas kernels: 0.16 us -> 2.93 us  [split_call(): pl.pallas_call(split_kernel, grid=(rows // block,), in_specs=[SMEM, pl.Bl...]
    pallas_call x2 -> x1, Pallas kernels: 2.85 us -> 1.25 us  [half_call(): pl.pallas_call(kernel, grid_spec=pltpu.PrefetchScalarGridSpec(num_scalar_...]
    ppermute x17, waiting for transfers between devices: 18.8 us -> 17.9 us  [swap(): lax.ppermute(value, axis, [(i, i ^ bit) for i in range(lax.axis_size(axis...]
  transfers between devices with their start and end apart: 17 -> 17, of which waited for: 11 -> 9; matrix products, arithmetic and copies ran while one was open for 0% -> 0% of each run, Pallas kernels for 34% -> 36%
where the time goes in v7:
time: 74.5 us; the launch traced here: 74.3 us
  Pallas kernels  37 us (50%)
  starting transfers between devices  18.6 us (25%)
  waiting for transfers between devices  17.9 us (24%)
  between operations  0.82 us (1%)
    ppermute x17, starting transfers between devices, swap(): lax.ppermute(value, axis, [(i, i ^ bit) for i in range(lax.axis_size(axis...  18.6 us
    ppermute x17, waiting for transfers between devices, swap(): lax.ppermute(value, axis, [(i, i ^ bit) for i in range(lax.axis_size(axis...  17.9 us
    pallas_call x1, Pallas kernels, left_call(): pl.pallas_call(functools.partial(left_kernel, len(after)), grid=(rows //...  11 us
    pallas_call x1, Pallas kernels, final_call(): pl.pallas_call(functools.partial(final_kernel, scale, chunks), grid=(rows...  9.95 us
    pallas_call x2, Pallas kernels, layer_call(): pl.pallas_call(functools.partial(layer_kernel, scale), in_specs=[SMEM] +...  4.29 us
    pallas_call x1, Pallas kernels, factor_call(): pl.pallas_call(factor_kernel, in_specs=[VMEM] * (1 + len(left)), out_spec...  3.78 us
    pallas_call x2, Pallas kernels, right_call(): pl.pallas_call(functools.partial(right_kernel, scale, block, chunk), in_s...  3.4 us
    pallas_call x1, Pallas kernels, split_call(): pl.pallas_call(split_kernel, grid=(rows // block,), in_specs=[SMEM, pl.Bl...  2.93 us
  transfers between devices with their start and end apart: 17, of which 9 were waited for; matrix products, arithmetic and copies ran while one was open for 0% of the time, Pallas kernels for 36%

profile of v7, /device:TPU:1, one launch (start us, length us, event | category | flops | bytes accessed | tf_op | source)
XLA Modules:
  0.0 74.3 jit_solution(16362584930440196359)
XLA Ops:
  0.6 0.1 collective-permute-start
  0.8 2.9 %split.1 = (f32[128,2048]{1,0:T(8,128)S(1)}, f32[128,2048]{1,0:T(8,128)S(1)}) custom-call(s32[1]{0:T(128)} %bitcast.core, f32[2,128,2048]{2,1,0:T(8,128)} %weights.10, f32[1,2,128,2048]{3,2,1,0:T(8,128)} %copies.3), custom_call_target="tpu_custom_call" | custom-call | tf_op jit(solution)/shard_map/split/pallas_call | solution.py:345
  3.7 0.5 collective-permute-start.11
  4.2 0.0 collective-permute-done.received
  4.2 1.3 %both.1.one.refs_0_ = f32[128,1024]{1,0:T(8,128)S(1)} custom-call(s32[1]{0:T(128)} %bitcast.core, f32[2,128,1024]{2,1,0:T(8,128)} %weights.9, f32[1,2,128,1024]{3,2,1,0:T(8,128)} %copies.4, f32[1,2,128,1024]{3,2,1,0:T(8,128)S(1)} %collective-permute-done.received, f32[128,2048]{1,0:T(8,128)S(1)} %get-tuple-element.34.refs_0_), custom_call_target="tpu_custom_call" | custom-call | tf_op jit(solution)/shard_map/both/pallas_call | solution.py:370
  5.5 2.3 %collective-permute-start.1 = (f32[128,1024]{1,0:T(8,128)S(1)}, f32[128,1024]{1,0:T(8,128)S(1)}, u32[]{:S(2)}, u32[]{:S(2)}) collective-permute-start(f32[128,1024]{1,0:T(8,128)S(1)} %both.1.one.refs_0_), channel_id=1, source_target_pairs={{0,16},{8,24},{16,0},{24,8},{1,17},{9,25},{17,1},{25,9},{2,18},{10... | collective-permute-start | bytes 1572872 | tf_op jit(solution)/shard_map/ppermute | solution.py:41
  7.8 11.0 %left.1 = (f32[2048,1024]{1,0:T(8,128)S(1)}, f32[32,2048]{1,0:T(8,128)S(1)}, f32[32,2048]{1,0:T(8,128)S(1)}) custom-call(s32[1]{0:T(128)} %bitcast.core, f32[2048,1024]{1,0:T(8,128)} %weights.11, f32[1,2048,1024]{2,1,0:T(8,128)} %copies.5, f32[1,2048,1024]{2,1,0:T(8,128)} %error.1, f32[64,1024]{1,0:T(8,128)} %warm.1, f32[128,1024]{1,0:T(8,128)S(1)} %both.1.one.refs_0_), custom_call_target="tpu_custom_call" | custom-call | tf_op jit(solution)/shard_map/left/pallas_call | solution.py:125
  18.8 0.8 %collective-permute-start.3 = (f32[32,2048]{1,0:T(8,128)S(1)}, f32[32,2048]{1,0:T(8,128)S(1)}, u32[]{:S(2)}, u32[]{:S(2)}) collective-permute-start(f32[32,2048]{1,0:T(8,128)S(1)} %get-tuple-element.36), channel_id=1, source_target_pairs={{0,8},{8,0},{16,24},{24,16},{1,9},{9,1},{17,25},{25,17},{2,10},{10... | collective-permute-start | bytes 786440 | tf_op jit(solution)/shard_map/ppermute | solution.py:41
  19.6 0.1 collective-permute-done.1.two
  19.7 0.1 sum.10.refs_0_.mine
  19.7 1.0 %collective-permute-done.3.two = f32[32,2048]{1,0:T(8,128)S(1)} collective-permute-done((f32[32,2048]{1,0:T(8,128)S(1)}, f32[32,2048]{1,0:T(8,128)S(1)}, u32[]{:S(2)}, u32[]{:S(2)}) %collective-permute-start.3) | collective-permute-done | bytes 262176 | tf_op jit(solution)/shard_map/ppermute | solution.py:41
  20.8 0.2 collective-permute-start.5
  21.0 1.3 %collective-permute-start.4 = (f32[32,1024]{1,0:T(8,128)S(1)}, f32[32,1024]{1,0:T(8,128)S(1)}, u32[]{:S(2)}, u32[]{:S(2)}) collective-permute-start(f32[32,1024]{1,0:T(8,128)S(1)} %get-tuple-element.37.one), channel_id=1, source_target_pairs={{0,16},{8,24},{16,0},{24,8},{1,17},{9,25},{17,1},{25,9},{2,18},{10... | collective-permute-start | bytes 393224 | tf_op jit(solution)/shard_map/ppermute | solution.py:41
  22.3 3.2 %collective-permute-done.5.two = f32[32,1024]{1,0:T(8,128)S(1)} collective-permute-done((f32[32,1024]{1,0:T(8,128)S(1)}, f32[32,1024]{1,0:T(8,128)S(1)}, u32[]{:S(2)}, u32[]{:S(2)}) %collective-permute-start.5) | collective-permute-done | bytes 131104 | tf_op jit(solution)/shard_map/ppermute | solution.py:41
  25.6 2.1 %collective-permute-start.6 = (f32[32,1024]{1,0:T(8,128)S(1)}, f32[32,1024]{1,0:T(8,128)S(1)}, u32[]{:S(2)}, u32[]{:S(2)}) collective-permute-start(f32[32,1024]{1,0:T(8,128)S(1)} %sum.12.mine.refs_0_), channel_id=1, source_target_pairs={{0,8},{8,0},{16,24},{24,16},{1,9},{9,1},{17,25},{25,17},{2,10},{10... | collective-permute-start | bytes 393224 | tf_op jit(solution)/shard_map/ppermute | solution.py:41
  27.7 0.7 collective-permute-done.4.two
  28.4 0.3 collective-permute-done.6.refs_0_.other
  28.7 0.0 collective-permute-done.11.two
  28.7 0.1 sum.17.one
  28.8 0.8 %collective-permute-start.12 = (f32[128,2048]{1,0:T(8,128)S(1)}, f32[128,2048]{1,0:T(8,128)S(1)}, u32[]{:S(2)}, u32[]{:S(2)}) collective-permute-start(f32[128,2048]{1,0:T(8,128)S(1)} %sum.17.one), channel_id=1, source_target_pairs={{0,16},{8,24},{16,0},{24,8},{1,17},{9,25},{17,1},{25,9},{2,18},{10... | collective-permute-start | bytes 3145736 | tf_op jit(solution)/shard_map/ppermute | solution.py:41
  29.6 0.6 collective-permute-start.7
  30.2 0.0 copy-start.1
  30.2 0.0 copy-start.3
  30.2 0.0 slice-start.2
  30.2 1.7 %right.2 = (f32[32,1152]{1,0:T(8,128)S(1)}, f32[32,1152]{1,0:T(8,128)S(1)}, f32[64,1024]{1,0:T(8,128)S(1)}) custom-call(s32[1]{0:T(128)} %bitcast.core, f32[32,1024]{1,0:T(8,128)S(1)} %sum.12.mine.refs_0_, f32[32,1024]{1,0:T(8,128)S(1)} %collective-permute-done.6.refs_0_.other, f32[2048,1024]{1,0:T(8,128)S(1)} %get-tuple-element.39.corrected), custom_call_target="tpu_custom_call" | custom-call | tf_op jit(solution)/shard_map/right/pallas_call | solution.py:185
  31.9 0.0 collective-permute-done.7.other
  31.9 0.0 copy-start
  32.0 0.0 copy-start.2
  32.0 0.0 slice-start.3
  32.0 1.7 %right.3 = (f32[32,1152]{1,0:T(8,128)S(1)}, f32[32,1152]{1,0:T(8,128)S(1)}, f32[64,1024]{1,0:T(8,128)S(1)}) custom-call(s32[1]{0:T(128)} %bitcast.core, f32[32,1024]{1,0:T(8,128)S(1)} %sum.13.mine.refs_1_, f32[32,1024]{1,0:T(8,128)S(1)} %collective-permute-done.7.other, f32[2048,1024]{1,0:T(8,128)S(1)} %get-tuple-element.39.corrected, ...), custom_call_target="tpu_custom_call" | custom-call | tf_op jit(solution)/shard_map/right/pallas_call | solution.py:185
  33.7 0.0 slice-start
  33.7 0.1 collective-permute-start.8
  33.7 0.5 collective-permute-start.2
  34.2 0.9 %collective-permute-done.8.two = f32[32,1152]{1,0:T(8,128)S(1)} collective-permute-done((f32[32,1152]{1,0:T(8,128)S(1)}, f32[32,1152]{1,0:T(8,128)S(1)}, u32[]{:S(2)}, u32[]{:S(2)}) %collective-permute-start.8) | collective-permute-done | bytes 147488 | tf_op jit(solution)/shard_map/ppermute | solution.py:41
  35.1 1.4 %collective-permute-start.9 = (f32[32,1152]{1,0:T(8,128)S(1)}, f32[32,1152]{1,0:T(8,128)S(1)}, u32[]{:S(2)}, u32[]{:S(2)}) collective-permute-start(f32[32,1152]{1,0:T(8,128)S(1)} %sum.14.one), channel_id=1, source_target_pairs={{0,1},{1,0},{2,3},{3,2},{4,5},{5,4},{6,7},{7,6},{8,9},{9,8},{10,11... | collective-permute-start | bytes 442376 | tf_op jit(solution)/shard_map/ppermute | solution.py:41
  36.6 3.9 %collective-permute-done.9.two = f32[32,1152]{1,0:T(8,128)S(1)} collective-permute-done((f32[32,1152]{1,0:T(8,128)S(1)}, f32[32,1152]{1,0:T(8,128)S(1)}, u32[]{:S(2)}, u32[]{:S(2)}) %collective-permute-start.9) | collective-permute-done | bytes 147488 | tf_op jit(solution)/shard_map/ppermute | solution.py:41
  40.5 1.5 %collective-permute-start.10 = (f32[32,1152]{1,0:T(8,128)S(1)}, f32[32,1152]{1,0:T(8,128)S(1)}, u32[]{:S(2)}, u32[]{:S(2)}) collective-permute-start(f32[32,1152]{1,0:T(8,128)S(1)} %sum.15.one), channel_id=1, source_target_pairs={{0,2},{1,3},{2,0},{3,1},{4,6},{5,7},{6,4},{7,5},{8,10},{9,11},{10,... | collective-permute-start | bytes 442376 | tf_op jit(solution)/shard_map/ppermute | solution.py:41
  42.0 3.0 %collective-permute-done.10.two = f32[32,1152]{1,0:T(8,128)S(1)} collective-permute-done((f32[32,1152]{1,0:T(8,128)S(1)}, f32[32,1152]{1,0:T(8,128)S(1)}, u32[]{:S(2)}, u32[]{:S(2)}) %collective-permute-start.10) | collective-permute-done | bytes 147488 | tf_op jit(solution)/shard_map/ppermute | solution.py:41
  45.0 2.5 %collective-permute-start.13 = (f32[32,1152]{1,0:T(8,128)S(1)}, f32[32,1152]{1,0:T(8,128)S(1)}, u32[]{:S(2)}, u32[]{:S(2)}) collective-permute-start(f32[32,1152]{1,0:T(8,128)S(1)} %sum.16.refs_0_.one), channel_id=1, source_target_pairs={{0,4},{1,5},{2,6},{3,7},{4,0},{5,1},{6,2},{7,3},{8,12},{9,13},{10,... | collective-permute-start | bytes 442376 | tf_op jit(solution)/shard_map/ppermute | solution.py:41
  47.5 0.0 collective-permute-done.2.other
  47.5 0.0 copy-done.1
  47.5 0.0 copy-done.3
  47.5 1.6 %layer.2 = (f32[2,128,1024]{2,1,0:T(8,128)}, f32[2,128,1024]{2,1,0:T(8,128)}, f32[8,128]{1,0:T(8,128)S(1)}) custom-call(s32[1]{0:T(128)} %bitcast.core, f32[128,1024]{1,0:T(8,128)S(1)} %sum.10.refs_0_.mine, f32[128,1024]{1,0:T(8,128)S(1)} %collective-permute-done.2.other, f32[2,128,1024]{2,1,0:T(8,128)S(1)} %copy-done.1, f32[2,128,1024]{2,1,0:T(8,128)S(1)} %copy-done.3, ...), custom_call_target="tpu_custom_call" | custom-call | tf_op jit(solution)/shard_map/layer/pallas_call | solution.py:392
  49.1 4.7 %collective-permute-done.13.two = f32[32,1152]{1,0:T(8,128)S(1)} collective-permute-done((f32[32,1152]{1,0:T(8,128)S(1)}, f32[32,1152]{1,0:T(8,128)S(1)}, u32[]{:S(2)}, u32[]{:S(2)}) %collective-permute-start.13) | collective-permute-done | bytes 147488 | tf_op jit(solution)/shard_map/ppermute | solution.py:41
  53.8 0.0 collective-permute-done.12.two
  53.9 0.0 slice-start.1
  53.9 0.1 sum.18.mine
  54.0 1.7 %collective-permute-start.14 = (f32[128,2048]{1,0:T(8,128)S(1)}, f32[128,2048]{1,0:T(8,128)S(1)}, u32[]{:S(2)}, u32[]{:S(2)}) collective-permute-start(f32[128,2048]{1,0:T(8,128)S(1)} %sum.18.mine), channel_id=1, source_target_pairs={{0,8},{8,0},{16,24},{24,16},{1,9},{9,1},{17,25},{25,17},{2,10},{10... | collective-permute-start | bytes 3145736 | tf_op jit(solution)/shard_map/ppermute | solution.py:41
  55.7 1.2 %collective-permute-start.15 = (f32[32,1024]{1,0:T(8,128)S(1)}, f32[32,1024]{1,0:T(8,128)S(1)}, u32[]{:S(2)}, u32[]{:S(2)}) collective-permute-start(f32[32,1024]{1,0:T(8,128)S(1)} %get-tuple-element.48.refs_0_.one), channel_id=1, source_target_pairs={{0,16},{8,24},{16,0},{24,8},{1,17},{9,25},{17,1},{25,9},{2,18},{10... | collective-permute-start | bytes 393224 | tf_op jit(solution)/shard_map/ppermute | solution.py:41
  56.9 3.8 %factor.1 = (f32[64,64]{1,0:T(8,128)S(1)}, bf16[1024,384]{1,0:T(8,128)(2,1)S(1)}, bf16[1024,384]{1,0:T(8,128)(2,1)S(1)}) custom-call(f32[32,128]{1,0:T(8,128)S(1)} %get-tuple-element.49.message, f32[64,1024]{1,0:T(8,128)S(1)} %get-tuple-element.50.refs_0_, f32[64,1024]{1,0:T(8,128)S(1)} %get-tuple-element.51.refs_1_), custom_call_target="tpu_custom_call" | custom-call | tf_op jit(solution)/shard_map/factor/pallas_call | solution.py:251
  60.7 0.0 collective-permute-done.15.two
  60.8 0.9 %collective-permute-start.16 = (f32[32,1024]{1,0:T(8,128)S(1)}, f32[32,1024]{1,0:T(8,128)S(1)}, u32[]{:S(2)}, u32[]{:S(2)}) collective-permute-start(f32[32,1024]{1,0:T(8,128)S(1)} %sum.19.refs_0_.mine), channel_id=1, source_target_pairs={{0,8},{8,0},{16,24},{24,16},{1,9},{9,1},{17,25},{25,17},{2,10},{10... | collective-permute-start | bytes 393224 | tf_op jit(solution)/shard_map/ppermute | solution.py:41
  61.7 0.0 collective-permute-done.14.other
  61.7 0.0 copy-done
  61.7 0.0 copy-done.2
  61.7 2.6 %layer.3 = (f32[2,128,2048]{2,1,0:T(8,128)}, f32[2,128,2048]{2,1,0:T(8,128)}, f32[8,128]{1,0:T(8,128)S(1)}) custom-call(s32[1]{0:T(128)} %bitcast.core, f32[128,2048]{1,0:T(8,128)S(1)} %sum.18.mine, f32[128,2048]{1,0:T(8,128)S(1)} %collective-permute-done.14.other, f32[2,128,2048]{2,1,0:T(8,128)S(1)} %copy-done, f32[2,128,2048]{2,1,0:T(8,128)S(1)} %copy-done.2, ...), custom_call_target="tpu_custom_call" | custom-call | tf_op jit(solution)/shard_map/layer/pallas_call | solution.py:392
  64.3 0.0 collective-permute-done.16.other
  64.4 0.0 slice-done.2
  64.4 0.0 slice-done.3
  64.4 0.0 slice-done
  64.4 0.0 slice-done.1
  64.4 9.9 %final.1 = (f32[2048,1024]{1,0:T(8,128)}, f32[2048,1024]{1,0:T(8,128)}, f32[1,2048,1024]{2,1,0:T(8,128)}) custom-call(s32[1]{0:T(128)} %bitcast.core, f32[32,1024]{1,0:T(8,128)S(1)} %sum.19.refs_0_.mine, f32[32,1024]{1,0:T(8,128)S(1)} %collective-permute-done.16.other, f32[64,64]{1,0:T(8,128)S(1)} %get-tuple-element.52.refs_0_.inverse, ...), custom_call_target="tpu_custom_call" | custom-call | tf_op jit(solution)/shard_map/final/pallas_call | solution.py:300
  (10 shorter events, 0.2 us)
Async XLA Ops:
  0.6 3.6 %collective-permute-start = (f32[1,2,128,1024]{3,2,1,0:T(8,128)}, f32[1,2,128,1024]{3,2,1,0:T(8,128)S(1)}, u32[]{:S(2)}, u32[]{:S(2)}) collective-permute-start(f32[1,2,128,1024]{3,2,1,0:T(8,128)} %copies.4), channel_id=1, source_target_pairs={{0,8},{8,0},{16,24},{24,16},{1,9},{9,1},{17,25},{25,17},{2,10},{10... | collective-permute-start | bytes 3145736 | tf_op jit(solution)/shard_map/ppermute | solution.py:41
  3.7 25.0 %collective-permute-start.11 = (f32[128,2048]{1,0:T(8,128)S(1)}, f32[128,2048]{1,0:T(8,128)S(1)}, u32[]{:S(2)}, u32[]{:S(2)}) collective-permute-start(f32[128,2048]{1,0:T(8,128)S(1)} %get-tuple-element.34.refs_0_), channel_id=1, source_target_pairs={{0,8},{8,0},{16,24},{24,16},{1,9},{9,1},{17,25},{25,17},{2,10},{10... | collective-permute-start | bytes 3145736 | tf_op jit(solution)/shard_map/ppermute | solution.py:41
  5.5 14.2 %collective-permute-start.1 = (f32[128,1024]{1,0:T(8,128)S(1)}, f32[128,1024]{1,0:T(8,128)S(1)}, u32[]{:S(2)}, u32[]{:S(2)}) collective-permute-start(f32[128,1024]{1,0:T(8,128)S(1)} %both.1.one.refs_0_), channel_id=1, source_target_pairs={{0,16},{8,24},{16,0},{24,8},{1,17},{9,25},{17,1},{25,9},{2,18},{10... | collective-permute-start | bytes 1572872 | tf_op jit(solution)/shard_map/ppermute | solution.py:41
  18.8 2.0 %collective-permute-start.3 = (f32[32,2048]{1,0:T(8,128)S(1)}, f32[32,2048]{1,0:T(8,128)S(1)}, u32[]{:S(2)}, u32[]{:S(2)}) collective-permute-start(f32[32,2048]{1,0:T(8,128)S(1)} %get-tuple-element.36), channel_id=1, source_target_pairs={{0,8},{8,0},{16,24},{24,16},{1,9},{9,1},{17,25},{25,17},{2,10},{10... | collective-permute-start | bytes 786440 | tf_op jit(solution)/shard_map/ppermute | solution.py:41
  20.8 4.8 %collective-permute-start.5 = (f32[32,1024]{1,0:T(8,128)S(1)}, f32[32,1024]{1,0:T(8,128)S(1)}, u32[]{:S(2)}, u32[]{:S(2)}) collective-permute-start(f32[32,1024]{1,0:T(8,128)S(1)} %get-tuple-element.38.one), channel_id=1, source_target_pairs={{0,16},{8,24},{16,0},{24,8},{1,17},{9,25},{17,1},{25,9},{2,18},{10... | collective-permute-start | bytes 393224 | tf_op jit(solution)/shard_map/ppermute | solution.py:41
  21.0 7.4 %collective-permute-start.4 = (f32[32,1024]{1,0:T(8,128)S(1)}, f32[32,1024]{1,0:T(8,128)S(1)}, u32[]{:S(2)}, u32[]{:S(2)}) collective-permute-start(f32[32,1024]{1,0:T(8,128)S(1)} %get-tuple-element.37.one), channel_id=1, source_target_pairs={{0,16},{8,24},{16,0},{24,8},{1,17},{9,25},{17,1},{25,9},{2,18},{10... | collective-permute-start | bytes 393224 | tf_op jit(solution)/shard_map/ppermute | solution.py:41
  25.6 3.1 %collective-permute-start.6 = (f32[32,1024]{1,0:T(8,128)S(1)}, f32[32,1024]{1,0:T(8,128)S(1)}, u32[]{:S(2)}, u32[]{:S(2)}) collective-permute-start(f32[32,1024]{1,0:T(8,128)S(1)} %sum.12.mine.refs_0_), channel_id=1, source_target_pairs={{0,8},{8,0},{16,24},{24,16},{1,9},{9,1},{17,25},{25,17},{2,10},{10... | collective-permute-start | bytes 393224 | tf_op jit(solution)/shard_map/ppermute | solution.py:41
  28.8 25.1 %collective-permute-start.12 = (f32[128,2048]{1,0:T(8,128)S(1)}, f32[128,2048]{1,0:T(8,128)S(1)}, u32[]{:S(2)}, u32[]{:S(2)}) collective-permute-start(f32[128,2048]{1,0:T(8,128)S(1)} %sum.17.one), channel_id=1, source_target_pairs={{0,16},{8,24},{16,0},{24,8},{1,17},{9,25},{17,1},{25,9},{2,18},{10... | collective-permute-start | bytes 3145736 | tf_op jit(solution)/shard_map/ppermute | solution.py:41
  29.6 2.4 %collective-permute-start.7 = (f32[32,1024]{1,0:T(8,128)S(1)}, f32[32,1024]{1,0:T(8,128)S(1)}, u32[]{:S(2)}, u32[]{:S(2)}) collective-permute-start(f32[32,1024]{1,0:T(8,128)S(1)} %sum.13.mine.refs_1_), channel_id=1, source_target_pairs={{0,8},{8,0},{16,24},{24,16},{1,9},{9,1},{17,25},{25,17},{2,10},{10... | collective-permute-start | bytes 393224 | tf_op jit(solution)/shard_map/ppermute | solution.py:41
  30.2 17.3 %copy-start.1 = (f32[2,128,1024]{2,1,0:T(8,128)S(1)}, f32[2,128,1024]{2,1,0:T(8,128)}, u32[]{:S(2)}) copy-start(f32[2,128,1024]{2,1,0:T(8,128)} %weights.9) | copy-start | bytes 3145732
  30.2 17.3 %copy-start.3 = (f32[2,128,1024]{2,1,0:T(8,128)S(1)}, f32[2,128,1024]{2,1,0:T(8,128)}, u32[]{:S(2)}) copy-start(f32[2,128,1024]{2,1,0:T(8,128)} %moment.3) | copy-start | bytes 3145732
  30.2 34.1 %slice-start.2 = ((s8[8388608]{0:T(1024)(128)(4,1)}), s8[4194304]{0:T(1024)(128)(4,1)S(1)}, s32[]{:S(2)}) async-start(s8[8388608]{0:T(1024)(128)(4,1)} %bitcast.3), calls=%async_computation.2 | async-start | bytes 8388608
  31.9 29.7 %copy-start = (f32[2,128,2048]{2,1,0:T(8,128)S(1)}, f32[2,128,2048]{2,1,0:T(8,128)}, u32[]{:S(2)}) copy-start(f32[2,128,2048]{2,1,0:T(8,128)} %weights.10) | copy-start | bytes 6291460
  32.0 29.7 %copy-start.2 = (f32[2,128,2048]{2,1,0:T(8,128)S(1)}, f32[2,128,2048]{2,1,0:T(8,128)}, u32[]{:S(2)}) copy-start(f32[2,128,2048]{2,1,0:T(8,128)} %moment.4) | copy-start | bytes 6291460
  32.0 32.4 %slice-start.3 = ((s8[8388608]{0:T(1024)(128)(4,1)}), s8[4194304]{0:T(1024)(128)(4,1)S(1)}, s32[]{:S(2)}) async-start(s8[8388608]{0:T(1024)(128)(4,1)} %bitcast.3), calls=%async_computation.3 | async-start | bytes 8388608
  33.7 30.7 %slice-start = ((s8[8388608]{0:T(1024)(128)(4,1)}), s8[4194304]{0:T(1024)(128)(4,1)S(1)}, s32[]{:S(2)}) async-start(s8[8388608]{0:T(1024)(128)(4,1)} %bitcast.1), calls=%async_computation | async-start | bytes 8388608
  33.7 1.4 %collective-permute-start.8 = (f32[32,1152]{1,0:T(8,128)S(1)}, f32[32,1152]{1,0:T(8,128)S(1)}, u32[]{:S(2)}, u32[]{:S(2)}) collective-permute-start(f32[32,1152]{1,0:T(8,128)S(1)} %get-tuple-element.43), channel_id=1, source_target_pairs={{0,8},{8,0},{16,24},{24,16},{1,9},{9,1},{17,25},{25,17},{2,10},{10... | collective-permute-start | bytes 442376 | tf_op jit(solution)/shard_map/ppermute | solution.py:41
  33.7 13.7 %collective-permute-start.2 = (f32[128,1024]{1,0:T(8,128)S(1)}, f32[128,1024]{1,0:T(8,128)S(1)}, u32[]{:S(2)}, u32[]{:S(2)}) collective-permute-start(f32[128,1024]{1,0:T(8,128)S(1)} %sum.10.refs_0_.mine), channel_id=1, source_target_pairs={{0,8},{8,0},{16,24},{24,16},{1,9},{9,1},{17,25},{25,17},{2,10},{10... | collective-permute-start | bytes 1572872 | tf_op jit(solution)/shard_map/ppermute | solution.py:41
  35.1 5.4 %collective-permute-start.9 = (f32[32,1152]{1,0:T(8,128)S(1)}, f32[32,1152]{1,0:T(8,128)S(1)}, u32[]{:S(2)}, u32[]{:S(2)}) collective-permute-start(f32[32,1152]{1,0:T(8,128)S(1)} %sum.14.one), channel_id=1, source_target_pairs={{0,1},{1,0},{2,3},{3,2},{4,5},{5,4},{6,7},{7,6},{8,9},{9,8},{10,11... | collective-permute-start | bytes 442376 | tf_op jit(solution)/shard_map/ppermute | solution.py:41
  40.5 4.5 %collective-permute-start.10 = (f32[32,1152]{1,0:T(8,128)S(1)}, f32[32,1152]{1,0:T(8,128)S(1)}, u32[]{:S(2)}, u32[]{:S(2)}) collective-permute-start(f32[32,1152]{1,0:T(8,128)S(1)} %sum.15.one), channel_id=1, source_target_pairs={{0,2},{1,3},{2,0},{3,1},{4,6},{5,7},{6,4},{7,5},{8,10},{9,11},{10,... | collective-permute-start | bytes 442376 | tf_op jit(solution)/shard_map/ppermute | solution.py:41
  45.0 8.8 %collective-permute-start.13 = (f32[32,1152]{1,0:T(8,128)S(1)}, f32[32,1152]{1,0:T(8,128)S(1)}, u32[]{:S(2)}, u32[]{:S(2)}) collective-permute-start(f32[32,1152]{1,0:T(8,128)S(1)} %sum.16.refs_0_.one), channel_id=1, source_target_pairs={{0,4},{1,5},{2,6},{3,7},{4,0},{5,1},{6,2},{7,3},{8,12},{9,13},{10,... | collective-permute-start | bytes 442376 | tf_op jit(solution)/shard_map/ppermute | solution.py:41
  53.9 10.5 %slice-start.1 = ((s8[8388608]{0:T(1024)(128)(4,1)}), s8[4194304]{0:T(1024)(128)(4,1)S(1)}, s32[]{:S(2)}) async-start(s8[8388608]{0:T(1024)(128)(4,1)} %bitcast.1), calls=%async_computation.1 | async-start | bytes 8388608
  54.0 7.7 %collective-permute-start.14 = (f32[128,2048]{1,0:T(8,128)S(1)}, f32[128,2048]{1,0:T(8,128)S(1)}, u32[]{:S(2)}, u32[]{:S(2)}) collective-permute-start(f32[128,2048]{1,0:T(8,128)S(1)} %sum.18.mine), channel_id=1, source_target_pairs={{0,8},{8,0},{16,24},{24,16},{1,9},{9,1},{17,25},{25,17},{2,10},{10... | collective-permute-start | bytes 3145736 | tf_op jit(solution)/shard_map/ppermute | solution.py:41
  55.7 5.1 %collective-permute-start.15 = (f32[32,1024]{1,0:T(8,128)S(1)}, f32[32,1024]{1,0:T(8,128)S(1)}, u32[]{:S(2)}, u32[]{:S(2)}) collective-permute-start(f32[32,1024]{1,0:T(8,128)S(1)} %get-tuple-element.48.refs_0_.one), channel_id=1, source_target_pairs={{0,16},{8,24},{16,0},{24,8},{1,17},{9,25},{17,1},{25,9},{2,18},{10... | collective-permute-start | bytes 393224 | tf_op jit(solution)/shard_map/ppermute | solution.py:41
  60.8 3.6 %collective-permute-start.16 = (f32[32,1024]{1,0:T(8,128)S(1)}, f32[32,1024]{1,0:T(8,128)S(1)}, u32[]{:S(2)}, u32[]{:S(2)}) collective-permute-start(f32[32,1024]{1,0:T(8,128)S(1)} %sum.19.refs_0_.mine), channel_id=1, source_target_pairs={{0,8},{8,0},{16,24},{24,16},{1,9},{9,1},{17,25},{25,17},{2,10},{10... | collective-permute-start | bytes 393224 | tf_op jit(solution)/shard_map/ppermute | solution.py:41
